TPU v7x, 32 devices: a whole 2x2x4 slice. The times are simulated.
32 devices in a mesh: dp: 4 (over y, x), latent: 8 (over z, core).
Axes of the slice: x: 2, y: 2, z: 4, core: 2. Of those that a mesh axis runs over, the one named last changes fastest.
Arguments:
- queries: bfloat16 [1024, 2048], P(('dp', 'latent')), may hold values from -32 to 32, as said below
- cache_keys: bfloat16 [32, 512, 1024], P(('dp', 'latent')), may hold values from -6 to 6
- cache_values: bfloat16 [32, 512, 1024], P(('dp', 'latent')), may hold values from -96 to 96
- positions: int32 [1024], P(('dp', 'latent')), may hold values from 224 to 511, as said below
- shuffle: int32 [1024], P(('dp', 'latent')), may hold values from 0 to 1023, as said below
- enc_weight: bfloat16 [2048, 16384], P(None, 'latent'), may hold values from -0.125 to 0.125
- enc_bias: float32 [16384], P('latent'), may hold values from -3 to 3
- dec_weight: bfloat16 [16384, 2048], P('latent'), may hold values from -0.046875 to 0.046875
- dec_bias: float32 [2048], replicated, may hold values from -3 to 3
Outputs:
- rebuilt: bfloat16 [1024, 2048], P(('dp', 'latent'))
- grad_enc: float32 [2048, 16384], P('dp', 'latent')
- grad_dec: float32 [16384, 2048], P('latent', 'dp')
Inputs may be any that keep to these rules, and one draw needn't show every extreme that they name: `queries`: entries are finite; a few rows may be aligned with keys of their sequence. The rows of one sequence have consecutive positions ending at its length minus one; lengths lie between 256 and 512, and sequence 0 has length 512. A permutation of 0 to 1023. Row r and its place shuffle[r] lie in sequences r // 32 and shuffle[r] // 32 that are equal modulo 256 // 32; from each such sequence exactly 8 rows go to each such sequence.
All inputs are finite; a program needn't handle non-finite values.
Results may differ from a plain program's by a relative error of at most 0.012.
Values may be sent and summed in bfloat16 or wider, within the bound.
No kernel may reach another device: no remote copies, remote signals or barrier semaphores. Data moves between devices by JAX's collectives and lax.ppermute only.
A program may use at most 128 MiB of HBM per device.

v0:
```python
import jax
import jax.numpy as jnp
from jax import lax
from jax.sharding import PartitionSpec as P

HEAD_DIM = 256


sharpness = 4.0
sparsity_weight = 1.0
epsilon = 1e-06


def attend(queries, cache_keys, cache_values, positions):
    rows_here = queries.shape[0]
    kv_heads = cache_keys.shape[-1] // HEAD_DIM
    grouped = queries.reshape(rows_here, kv_heads, -1, HEAD_DIM)
    keys_local = cache_keys[0].reshape(-1, kv_heads, HEAD_DIM)
    values_local = cache_values[0].reshape(-1, kv_heads, HEAD_DIM)
    scores = jnp.einsum(
        "qgid,kgd->gqik", grouped, keys_local, preferred_element_type=jnp.float32
    ) * HEAD_DIM ** (-0.5)
    slot_index = jnp.arange(keys_local.shape[0])
    visible = slot_index[None, None, None, :] <= positions[None, :, None, None]
    scores = jnp.where(visible, scores, -jnp.inf)
    highest = jnp.max(scores, axis=-1, keepdims=True)
    weights = jnp.exp(scores - highest)
    attn_probs = (weights / jnp.sum(weights, axis=-1, keepdims=True)).astype(jnp.bfloat16)
    head_mix = jnp.einsum(
        "gqik,kgd->qgid", attn_probs, values_local, preferred_element_type=jnp.float32
    )
    return head_mix.reshape(rows_here, -1).astype(jnp.bfloat16)


def shuffle_rows(moving, shuffle):
    data_size = lax.axis_size("dp")
    latent_size = lax.axis_size("latent")
    rows_here = moving.shape[0]
    per_peer = rows_here // data_size
    target = shuffle // (rows_here * latent_size)
    send_order = jnp.argsort(target, stable=True)
    outgoing = moving[send_order].reshape(data_size, per_peer, moving.shape[1])
    places = (shuffle[send_order] % rows_here).reshape(data_size, per_peer)
    arrived, arrival_slots = (
        lax.all_to_all(outgoing, "dp", split_axis=0, concat_axis=0, tiled=True),
        lax.all_to_all(places, "dp", split_axis=0, concat_axis=0, tiled=True),
    )
    arrived = arrived.reshape(rows_here, moving.shape[1])
    arrival_slots = arrival_slots.reshape(rows_here)
    return arrived[jnp.argsort(arrival_slots)]


def shards(
    queries,
    cache_keys,
    cache_values,
    positions,
    shuffle,
    enc_weight,
    enc_bias,
    dec_weight,
    dec_bias,
):
    rows_here = queries.shape[0]
    att_width = queries.shape[1]
    data_size = lax.axis_size("dp")
    latent_size = lax.axis_size("latent")
    all_rows = rows_here * data_size * latent_size
    heads_out = attend(queries, cache_keys, cache_values, positions)
    arrived = shuffle_rows(heads_out, shuffle)
    gathered = lax.all_gather(arrived, "latent", axis=0, tiled=True)
    start_row = lax.axis_index("latent") * rows_here
    group_energy = jnp.sum(jnp.square(gathered.astype(jnp.float32)))
    energy = lax.psum(group_energy, "dp")
    norm_scale = lax.rsqrt(energy / (all_rows * att_width) + epsilon)
    inputs = (gathered.astype(jnp.float32) * norm_scale).astype(jnp.bfloat16)
    preact = jnp.dot(inputs, enc_weight, preferred_element_type=jnp.float32) + enc_bias[None, :]
    active = jax.nn.softplus(sharpness * preact) / sharpness
    coded_half = active.astype(jnp.bfloat16)
    dec_float = dec_weight.astype(jnp.float32)
    dec_norms = jnp.sqrt(jnp.sum(jnp.square(dec_float), axis=1) + epsilon)
    partial_value = jnp.dot(coded_half, dec_weight, preferred_element_type=jnp.float32)
    summed = lax.psum(partial_value, "latent")
    rebuilt_all = summed + dec_bias[None, :]
    residual = rebuilt_all - inputs.astype(jnp.float32)
    residual_half = residual.astype(jnp.bfloat16)
    own_rebuilt = lax.dynamic_slice_in_dim(rebuilt_all, start_row, rows_here, 0)
    grad_active = (
        2.0
        / all_rows
        * lax.dot_general(
            residual_half, dec_weight, (((1,), (1,)), ((), ())), preferred_element_type=jnp.float32
        )
    )
    grad_active = grad_active + sparsity_weight / all_rows * dec_norms[None, :]
    grad_pre = (grad_active * jax.nn.sigmoid(sharpness * preact)).astype(jnp.bfloat16)
    grad_enc = lax.psum_scatter(
        lax.dot_general(
            inputs, grad_pre, (((0,), (0,)), ((), ())), preferred_element_type=jnp.float32
        ).astype(jnp.bfloat16),
        "dp",
        scatter_dimension=0,
        tiled=True,
    ).astype(jnp.float32)
    column_sums = jnp.sum(coded_half.astype(jnp.float32), axis=0)
    dec_term = (
        2.0
        / all_rows
        * lax.dot_general(
            coded_half, residual_half, (((0,), (0,)), ((), ())), preferred_element_type=jnp.float32
        )
    )
    dec_term = (
        dec_term
        + sparsity_weight / all_rows * column_sums[:, None] * dec_float / dec_norms[:, None]
    )
    grad_dec = lax.psum_scatter(
        dec_term.astype(jnp.bfloat16), "dp", scatter_dimension=1, tiled=True
    ).astype(jnp.float32)
    return (own_rebuilt.astype(jnp.bfloat16), grad_enc, grad_dec)


def solution(mesh):
    in_specs = (
        P(("dp", "latent"), None),
        P(("dp", "latent"), None, None),
        P(("dp", "latent"), None, None),
        P(("dp", "latent")),
        P(("dp", "latent")),
        P(None, "latent"),
        P("latent"),
        P("latent", None),
        P(),
    )
    out_specs = (P(("dp", "latent"), None), P("dp", "latent"), P("latent", "dp"))
    return jax.shard_map(shards, mesh=mesh, in_specs=in_specs, out_specs=out_specs, check_vma=False)
```

profile of v0, /device:TPU:0, one launch (start us, length us, event | category | flops | bytes accessed | tf_op | source)
XLA Modules:
  0.0 350.2 jit_solution(11054778938022510244)
XLA Ops:
  7.2 0.7 and_select_fusion
  7.8 1.6 sort.34
  9.5 1.4 gather_fusion.1
  11.5 5.2 %all-to-all-start.1 = ((s32[4,1,8]{2,1,0:T(1,128)}), s32[4,1,8]{2,1,0:T(1,128)S(1)}, u32[]{:S(2)}, u32[]{:S(2)}) async-start(s32[4,1,8]{2,1,0:T(1,128)} %bitcast.5), calls=%async_computation.1 | async-start | bytes 4096 | tf_op jit(solution)/shard_map/all_to_all | solution.py:46
  16.7 0.7 iota_compare_fusion
  17.4 1.0 reshape.117
  18.4 1.9 reshape_squeeze.6
  21.0 0.8 reshape_squeeze.7
  22.6 1.3 gather_fusion
  23.9 4.2 %all-to-all-start = ((bf16[4,8,2048]{2,1,0:T(8,128)(2,1)}), bf16[4,8,2048]{2,1,0:T(8,128)(2,1)S(1)}, u32[]{:S(2)}, u32[]{:S(2)}) async-start(bf16[4,8,2048]{2,1,0:T(8,128)(2,1)} %bitcast.3), calls=%async_computation | async-start | bytes 262144 | tf_op jit(solution)/shard_map/all_to_all | solution.py:45
  28.6 0.7 reduce.3
  29.4 1.6 sort.35
  31.0 2.1 all-to-all-done
  33.1 1.3 gather_fusion.2
  34.5 21.9 %all-gather.3.cloned.1.call-done = bf16[256,2048]{1,0:T(8,128)(2,1)} async-done(((bf16[32,2048]{1,0:T(8,128)(2,1)}), bf16[256,2048]{1,0:T(8,128)(2,1)}) %all-gather.3.cloned.1.call-update) | async-done | bytes 1048592 | tf_op jit(solution)/shard_map/all_gather | solution.py:71
  56.4 2.4 fusion.9
  58.8 10.4 %psum.14 = f32[]{:T(128)} all-reduce(f32[]{:T(128)} %fusion.9), channel_id=1, replica_groups=mesh['dp'=4,'latent'=8] {'dp'}, use_global_device_ids=true, to_apply=%region_5.6 | all-reduce | flops 1 | bytes 8 | tf_op jit(solution)/shard_map/psum | solution.py:74
  69.9 8.7 %convert_reduce_fusion = (f32[2048]{0:T(1024)S(1)}, bf16[256,2048]{1,0:T(8,128)(2,1)S(1)}, f32[256,2048]{1,0:T(8,128)}) fusion(f32[2048]{0:T(1024)S(1)} %copy-done.3, bf16[2048,2048]{1,0:T(8,128)(2,1)} %param.14, bf16[256,2048]{1,0:T(8,128)(2,1)} %all-gather.3.cloned.1.call-done, f32[]{:T(128)S(6)} %rsqrt.3), kind=kOutput, calls=%fused_computation.24 | convolution fusion | flops 2155345920 | bytes 12599300 | tf_op jit(solution)/shard_map/dot_general | solution.py:77
  78.7 1.1 copy-done.4
  79.7 7.0 %fusion.27 = f32[256,2048]{1,0:T(8,128)} fusion(bf16[256,2048]{1,0:T(8,128)(2,1)S(1)} %get-tuple-element.8, bf16[2048,2048]{1,0:T(8,128)(2,1)} %param.16), kind=kOutput, calls=%fused_computation.57 | convolution fusion | flops 2147483648 | bytes 11534336 | tf_op jit(solution)/shard_map/dot_general | solution.py:82
  87.1 5.3 %fusion.1 = f32[2048]{0:T(1024)S(1)} fusion(bf16[2048,2048]{1,0:T(8,128)(2,1)} %param.16), kind=kLoop, calls=%fused_computation.6 | loop fusion | flops 12580864 | bytes 8396800 | tf_op jit(solution)/shard_map/reduce_sum | solution.py:81
  92.4 57.3 %all-reduce.2.cloned.1.call-done = f32[256,2048]{1,0:T(8,128)} async-done(((f32[256,2048]{1,0:T(8,128)}), f32[256,2048]{1,0:T(8,128)}) %all-reduce.2.cloned.1.call-update) | async-done | bytes 2097168 | tf_op jit(solution)/shard_map/psum | solution.py:83
  149.7 2.2 subtract_convert_fusion
  151.9 6.0 %fusion.8 = bf16[256,2048]{1,0:T(8,128)(2,1)S(1)} fusion(bf16[256,2048]{1,0:T(8,128)(2,1)S(1)} %get-tuple-element.9, bf16[2048,2048]{1,0:T(8,128)(2,1)} %param.16, f32[256,2048]{1,0:T(8,128)S(1)} %copy-done.6, f32[2048]{0:T(1024)S(1)} %get-tuple-element.12), kind=kOutput, calls=%fused_computation.19 | convolution fusion | flops 2151153664 | bytes 12591104 | tf_op jit(solution)/shard_map/dot_general | solution.py:91
  158.0 5.6 %convolution_convert_fusion = bf16[2048,2048]{1,0:T(8,128)(2,1)} fusion(bf16[256,2048]{1,0:T(8,128)(2,1)S(1)} %fusion.8, bf16[256,2048]{1,0:T(8,128)(2,1)S(1)} %copy-done, f32[]{:T(128)S(6)} %rsqrt.3), kind=kOutput, calls=%fused_computation.10 | convolution fusion | flops 2153250816 | bytes 10485764 | tf_op jit(solution)/shard_map/dot_general | solution.py:98
  163.7 1.1 copy-done.5
  164.8 8.0 %fusion.4 = bf16[2048,2048]{1,0:T(8,128)(2,1)} fusion(bf16[2048,2048]{1,0:T(8,128)(2,1)} %param.16, bf16[256,2048]{1,0:T(8,128)(2,1)S(1)} %copy-done.5, bf16[256,2048]{1,0:T(8,128)(2,1)S(1)} %get-tuple-element.9, f32[2048]{0:T(1024)S(1)} %get-tuple-element.11, f32[2048]{0:T(1024)S(1)} %broadcast_multiply_fusion), kind=kOutput, calls=%fused_computation.9 | convolution fusion | flops 2172649472 | bytes 18890752 | tf_op jit(solution)/shard_map/dot_general | solution.py:109
  172.8 0.7 dynamic-slice_convert_fusion
  173.5 76.3 %reduce-scatter.3.cloned.1.call-done = bf16[512,2048]{1,0:T(8,128)(2,1)} async-done(((bf16[2048,2048]{1,0:T(8,128)(2,1)}), bf16[512,2048]{1,0:T(8,128)(2,1)}) %reduce-scatter.3.cloned.1.call-update) | async-done | bytes 2097168 | tf_op jit(solution)/shard_map/reduce_scatter | solution.py:97
  249.8 4.1 %convert_element_type.65 = f32[512,2048]{1,0:T(8,128)} convert(bf16[512,2048]{1,0:T(8,128)(2,1)} %reduce-scatter.3.cloned.1.call-done) | non-fusion elementwise | flops 1048576 | bytes 6291456 | tf_op jit(solution)/shard_map/convert_element_type | solution.py:104
  253.9 85.5 %reduce-scatter.5.cloned.1.call-done = bf16[2048,512]{1,0:T(8,128)(2,1)} async-done(((bf16[2048,2048]{1,0:T(8,128)(2,1)}), bf16[2048,512]{1,0:T(8,128)(2,1)}) %reduce-scatter.5.cloned.1.call-update) | async-done | bytes 2097168 | tf_op jit(solution)/shard_map/reduce_scatter | solution.py:117
  339.4 4.2 %convert_element_type.68 = f32[2048,512]{1,0:T(8,128)} convert(bf16[2048,512]{1,0:T(8,128)(2,1)} %reduce-scatter.5.cloned.1.call-done) | non-fusion elementwise | flops 1048576 | bytes 6291456 | tf_op jit(solution)/shard_map/convert_element_type | solution.py:119
  (38 shorter events, 3.1 us)
Async XLA Ops:
  11.5 12.4 %all-to-all-start.1 = ((s32[4,1,8]{2,1,0:T(1,128)}), s32[4,1,8]{2,1,0:T(1,128)S(1)}, u32[]{:S(2)}, u32[]{:S(2)}) async-start(s32[4,1,8]{2,1,0:T(1,128)} %bitcast.5), calls=%async_computation.1 | async-start | bytes 4096 | tf_op jit(solution)/shard_map/all_to_all | solution.py:46
  18.4 2.7 copy-start.1
  22.5 47.4 %copy-start.3 = (f32[2048]{0:T(1024)S(1)}, f32[2048]{0:T(1024)}, u32[]{:S(2)}) copy-start(f32[2048]{0:T(1024)} %param.15) | copy-start | bytes 24580
  23.9 9.2 %all-to-all-start = ((bf16[4,8,2048]{2,1,0:T(8,128)(2,1)}), bf16[4,8,2048]{2,1,0:T(8,128)(2,1)S(1)}, u32[]{:S(2)}, u32[]{:S(2)}) async-start(bf16[4,8,2048]{2,1,0:T(8,128)(2,1)} %bitcast.3), calls=%async_computation | async-start | bytes 262144 | tf_op jit(solution)/shard_map/all_to_all | solution.py:45
  28.1 28.3 %all-gather.3.cloned.1.call-start = ((), (), s32[]{:S(2)}) async-start(), calls=%async_computation.7 | async-start | bytes 1179648 | tf_op jit(solution)/shard_map/all_gather | solution.py:71
  34.5 115.2 %all-reduce.2.cloned.1.call-start = ((), (), s32[]{:S(2)}) async-start(), calls=%async_computation.4 | async-start | bytes 4194304 | tf_op jit(solution)/shard_map/psum | solution.py:83
  78.7 1.1 copy-start.4
  86.8 62.9 %copy-start = (bf16[256,2048]{1,0:T(8,128)(2,1)S(1)}, bf16[256,2048]{1,0:T(8,128)(2,1)}, u32[]{:S(2)}) copy-start(bf16[256,2048]{1,0:T(8,128)(2,1)} %all-gather.3.cloned.1.call-done) | copy-start | bytes 3145732
  86.8 62.9 %copy-start.2 = (f32[2048]{0:T(1024)S(1)}, f32[2048]{0:T(1024)}, u32[]{:S(2)}) copy-start(f32[2048]{0:T(1024)} %param.17) | copy-start | bytes 24580
  86.8 163.0 %reduce-scatter.3.cloned.1.call-start = ((), (), s32[]{:S(2)}) async-start(), calls=%async_computation.5 | async-start | bytes 10485760 | tf_op jit(solution)/shard_map/reduce_scatter | solution.py:97
  149.7 2.2 copy-start.6
  163.6 1.2 copy-start.5
  163.6 175.8 %reduce-scatter.5.cloned.1.call-start = ((), (), s32[]{:S(2)}) async-start(), calls=%async_computation.6 | async-start | bytes 10485760 | tf_op jit(solution)/shard_map/reduce_scatter | solution.py:117
Sparse Core Ops, SparseCore 0:
  34.6 21.8 all-gather.2
  86.9 62.7 all-reduce.1
  163.7 86.0 reduce-scatter.2
  253.0 86.3 reduce-scatter.4
where the time goes:
time: 351 us; the launch traced here: 350 us
  waiting for transfers between devices  243 us (69%)
  matrix products  36.3 us (10%)
  other arithmetic  24.4 us (7%)
  between operations  14.6 us (4%)
  local copies, waits for them, and re-layouts  11.5 us (3%)
  blocking collectives  10.4 us (3%)
  starting transfers between devices  9.66 us (3%)
    reduce_scatter x1, waiting for transfers between devices, shards(): lax.psum_scatter(dec_term.astype(jnp.bfloat16), 'dp', scatter_dimension=1...  85.5 us
    reduce_scatter x1, waiting for transfers between devices, shards(): lax.psum_scatter(lax.dot_general(inputs, grad_pre, (((0,), (0,)), ((), ()...  76.3 us
    psum x1, waiting for transfers between devices, shards(): summed = lax.psum(partial_value, 'latent')  57.3 us
    all_gather x1, waiting for transfers between devices, shards(): gathered = lax.all_gather(arrived, 'latent', axis=0, tiled=True)  21.9 us
    psum x1, blocking collectives, shards(): energy = lax.psum(group_energy, 'dp')  10.4 us
    dot_general x1, matrix products, shards(): jnp.dot(inputs, enc_weight, preferred_element_type=jnp.float32)  8.74 us
    dot_general x1, matrix products, shards(): lax.dot_general(coded_half, residual_half, (((0,), (0,)), ((), ())), pref...  7.96 us
    dot_general x1, matrix products, shards(): jnp.dot(coded_half, dec_weight, preferred_element_type=jnp.float32)  7.03 us
  transfers between devices with their start and end apart: 6, of which 5 were waited for; matrix products, arithmetic and copies ran while one was open for 8% of the time, Pallas kernels for 0%

commit v1 on v0

v1 whole, which is shorter than its diff:
```python
import functools

import jax
import jax.numpy as jnp
from jax import lax
from jax.experimental import pallas as pl
from jax.experimental.pallas import tpu as pltpu
from jax.sharding import PartitionSpec as P

HEAD_DIM = 256


sharpness = 4.0
sparsity_weight = 1.0
epsilon = 1e-06


def attend(queries, cache_keys, cache_values, positions):
    rows_here = queries.shape[0]
    kv_heads = cache_keys.shape[-1] // HEAD_DIM
    grouped = queries.reshape(rows_here, kv_heads, -1, HEAD_DIM)
    keys_local = cache_keys[0].reshape(-1, kv_heads, HEAD_DIM)
    values_local = cache_values[0].reshape(-1, kv_heads, HEAD_DIM)
    scores = jnp.einsum(
        "qgid,kgd->gqik", grouped, keys_local, preferred_element_type=jnp.float32
    ) * HEAD_DIM ** (-0.5)
    slot_index = jnp.arange(keys_local.shape[0])
    visible = slot_index[None, None, None, :] <= positions[None, :, None, None]
    scores = jnp.where(visible, scores, -jnp.inf)
    highest = jnp.max(scores, axis=-1, keepdims=True)
    weights = jnp.exp(scores - highest)
    attn_probs = (weights / jnp.sum(weights, axis=-1, keepdims=True)).astype(jnp.bfloat16)
    head_mix = jnp.einsum(
        "gqik,kgd->qgid", attn_probs, values_local, preferred_element_type=jnp.float32
    )
    return head_mix.reshape(rows_here, -1).astype(jnp.bfloat16)


VMEM_BYTES = 40 * 1024 * 1024


def codes(scaled):
    decay = jnp.exp(-jnp.abs(scaled))
    inverse = 1.0 / ((1.0 + decay) * (2.0 + decay))
    ratio = decay * inverse * (1.0 + decay)
    square = ratio * ratio
    series = 1.0 / 13.0
    for odd in (11, 9, 7, 5, 3, 1):
        series = series * square + 1.0 / odd
    soft = jnp.maximum(scaled, 0.0) + 2.0 * ratio * series
    slope = jnp.where(scaled >= 0.0, 1.0, decay) * (2.0 + decay) * inverse
    return (soft * (1.0 / sharpness)).astype(jnp.bfloat16), slope.astype(jnp.bfloat16)


def encode_body(scale_ref, rows_ref, enc_ref, bias_ref, coded_ref, slope_ref):
    scale = scale_ref[0, 0] * sharpness
    product = jnp.dot(rows_ref[...], enc_ref[...], preferred_element_type=jnp.float32)
    coded, slope = codes(product * scale + bias_ref[...] * sharpness)
    coded_ref[...] = coded
    slope_ref[...] = slope


def rebuild_body(scale_ref, rows_ref, enc_ref, bias_ref, dec_ref, coded_ref, slope_ref, total_ref):
    encode_body(scale_ref, rows_ref, enc_ref, bias_ref, coded_ref, slope_ref)
    term = jnp.dot(coded_ref[...], dec_ref[...], preferred_element_type=jnp.float32)

    @pl.when(pl.program_id(0) == 0)
    def _():
        total_ref[...] = term

    @pl.when(pl.program_id(0) > 0)
    def _():
        total_ref[...] += term


def encode(scale, rows, enc_weight, bias, dec_weight=None):
    count, width = rows.shape
    latents = enc_weight.shape[1]
    tile = min(512, latents)
    flops = 2 * count * width * latents
    wide = jax.ShapeDtypeStruct((count, latents), jnp.bfloat16)
    wide_spec = pl.BlockSpec((count, tile), lambda j: (0, j))
    in_specs = [
        pl.BlockSpec(memory_space=pltpu.SMEM),
        pl.BlockSpec((count, width), lambda j: (0, 0)),
        pl.BlockSpec((width, tile), lambda j: (0, j)),
        pl.BlockSpec((1, tile), lambda j: (0, j)),
    ]
    args, outs, out_specs, body = [scale, rows, enc_weight, bias], [wide, wide], [wide_spec] * 2, encode_body
    if dec_weight is not None:
        body = rebuild_body
        args.append(dec_weight)
        in_specs.append(pl.BlockSpec((tile, width), lambda j: (j, 0)))
        outs.append(jax.ShapeDtypeStruct((count, width), jnp.float32))
        out_specs.append(pl.BlockSpec((count, width), lambda j: (0, 0)))
        flops *= 2
    return pl.pallas_call(
        body,
        grid=(latents // tile,),
        in_specs=in_specs,
        out_specs=out_specs,
        out_shape=outs,
        compiler_params=pltpu.CompilerParams(vmem_limit_bytes=VMEM_BYTES),
        cost_estimate=pl.CostEstimate(flops=flops, bytes_accessed=4 * width * latents, transcendentals=2 * count * latents),
    )(*args)


def slope_body(all_rows, residual_ref, dec_ref, norms_ref, slope_ref, out_ref):
    product = lax.dot_general(
        residual_ref[...], dec_ref[...], (((1,), (1,)), ((), ())), preferred_element_type=jnp.float32
    )
    grad = product * (2.0 / all_rows) + norms_ref[...] * (sparsity_weight / all_rows)
    out_ref[...] = (grad * slope_ref[...].astype(jnp.float32)).astype(jnp.bfloat16)


def pre_gradient(all_rows, residual, dec_weight, norms, slope):
    count, width = residual.shape
    latents = dec_weight.shape[0]
    tile = min(512, latents)
    wide_spec = pl.BlockSpec((count, tile), lambda j: (0, j))
    return pl.pallas_call(
        functools.partial(slope_body, all_rows),
        grid=(latents // tile,),
        in_specs=[
            pl.BlockSpec((count, width), lambda j: (0, 0)),
            pl.BlockSpec((tile, width), lambda j: (j, 0)),
            pl.BlockSpec((1, tile), lambda j: (0, j)),
            wide_spec,
        ],
        out_specs=wide_spec,
        out_shape=jax.ShapeDtypeStruct((count, latents), jnp.bfloat16),
        compiler_params=pltpu.CompilerParams(vmem_limit_bytes=VMEM_BYTES),
        cost_estimate=pl.CostEstimate(flops=2 * count * width * latents, bytes_accessed=2 * width * latents, transcendentals=0),
    )(residual, dec_weight, norms, slope)


def weight_body(groups, all_rows, scale_ref, norms_ref, dec_ref, *refs):
    rows, grads, coded, residual = (refs[i * groups : (i + 1) * groups] for i in range(4))
    enc_ref, out_ref = refs[4 * groups :]
    enc, dec, sums = 0.0, 0.0, 0.0
    ones = jnp.ones((rows[0].shape[0], 128), jnp.bfloat16)
    over_rows = (((0,), (0,)), ((), ()))
    for g in range(groups):
        enc = enc + lax.dot_general(rows[g][...], grads[g][...], over_rows, preferred_element_type=jnp.float32)
        dec = dec + lax.dot_general(coded[g][...], residual[g][...], over_rows, preferred_element_type=jnp.float32)
        sums = sums + lax.dot_general(coded[g][...], ones, over_rows, preferred_element_type=jnp.float32)
    enc_ref[...] = enc * scale_ref[0, 0]
    factor = sums[:, :1] / norms_ref[...] * (sparsity_weight / all_rows)
    out_ref[...] = dec * (2.0 / all_rows) + factor * dec_ref[...].astype(jnp.float32)


def weight_gradients(all_rows, scale, norms, dec_part, rows, grads, coded, residual):
    groups = len(rows)
    count, columns = rows[0].shape
    latents = dec_part.shape[0]
    tile = min(256, latents)
    narrow = [pl.BlockSpec((count, columns), lambda j: (0, 0))] * groups
    wide = [pl.BlockSpec((count, tile), lambda j: (0, j))] * groups
    return pl.pallas_call(
        functools.partial(weight_body, groups, all_rows),
        grid=(latents // tile,),
        in_specs=[
            pl.BlockSpec(memory_space=pltpu.SMEM),
            pl.BlockSpec((tile, 1), lambda j: (j, 0)),
            pl.BlockSpec((tile, columns), lambda j: (j, 0)),
            *narrow,
            *wide,
            *wide,
            *narrow,
        ],
        out_specs=[
            pl.BlockSpec((columns, tile), lambda j: (0, j)),
            pl.BlockSpec((tile, columns), lambda j: (j, 0)),
        ],
        out_shape=[
            jax.ShapeDtypeStruct((columns, latents), jnp.float32),
            jax.ShapeDtypeStruct((latents, columns), jnp.float32),
        ],
        compiler_params=pltpu.CompilerParams(vmem_limit_bytes=VMEM_BYTES),
        cost_estimate=pl.CostEstimate(flops=4 * groups * count * columns * latents, bytes_accessed=16 * columns * latents, transcendentals=0),
    )(scale, norms, dec_part, *rows, *grads, *coded, *residual)


def swap(x, axis, mask):
    size = lax.axis_size(axis)
    return lax.ppermute(x, axis, [(i, i ^ mask) for i in range(size)])


def spread(x, axis, masks):
    return [x] + [swap(x, axis, mask) for mask in masks]


def exchange_cores(x):
    return swap(x, "latent", 1)


def spread_columns_energy(x):
    latent_size = lax.axis_size("latent")
    data_size = lax.axis_size("dp")
    x = x + swap(x, "latent", 1)
    x = sum(spread(x, "dp", range(1, data_size)))
    return sum(spread(x, "latent", range(2, latent_size, 2)))


def place_rows(rows, shuffle):
    data_size = lax.axis_size("dp")
    latent_size = lax.axis_size("latent")
    own = lax.axis_index("dp")
    rows_here = rows.shape[0]
    per_peer = rows_here // data_size
    target = shuffle // (rows_here * latent_size)
    place = shuffle % rows_here
    index = jnp.arange(rows_here)
    same = (target[:, None] == target[None, :]) & (index[None, :] < index[:, None])
    rank = jnp.sum(same.astype(jnp.int32), axis=1)
    arrived, slots = [], []
    for mask in range(data_size):
        chosen = (target == (own ^ mask))[None, :] & (
            rank[None, :] == jnp.arange(per_peer)[:, None]
        )
        sent = jnp.dot(
            chosen.astype(jnp.bfloat16), rows, preferred_element_type=jnp.float32
        ).astype(jnp.bfloat16)
        slot = jnp.sum(jnp.where(chosen, place[None, :], 0), axis=1)
        if mask:
            sent = swap(sent, "dp", mask)
            slot = swap(slot, "dp", mask)
        arrived.append(sent)
        slots.append(slot)
    slots = jnp.concatenate(slots)
    pick = (slots[None, :] == index[:, None]).astype(jnp.bfloat16)
    return jnp.dot(
        pick, jnp.concatenate(arrived), preferred_element_type=jnp.float32
    ).astype(jnp.bfloat16)


def shards(
    queries,
    cache_keys,
    cache_values,
    positions,
    shuffle,
    enc_weight,
    enc_bias,
    dec_weight,
    dec_bias,
):
    rows_here = queries.shape[0]
    att_width = queries.shape[1]
    data_size = lax.axis_size("dp")
    latent_size = lax.axis_size("latent")
    all_rows = rows_here * data_size * latent_size
    columns_here = att_width // data_size
    half = rows_here * latent_size // 2
    z_masks = range(2, latent_size, 2)
    first_column = lax.axis_index("dp") * columns_here

    heads_out = attend(queries, cache_keys, cache_values, positions)
    energy = spread_columns_energy(
        jnp.sum(jnp.square(heads_out.astype(jnp.float32)), axis=0).reshape(-1, 128).sum(axis=0, keepdims=True)
    )
    norm_scale = lax.rsqrt(jnp.sum(energy) / (all_rows * att_width) + epsilon)

    def gather_groups(own_rows):
        mine = jnp.concatenate(spread(own_rows, "latent", z_masks))
        halves = spread(mine, "dp", range(1, data_size))
        return [jnp.concatenate([h, exchange_cores(h)]) for h in halves]

    heads = gather_groups(heads_out)
    dec_float = dec_weight.astype(jnp.float32)
    dec_norms = jnp.sqrt(jnp.sum(jnp.square(dec_float), axis=1) + epsilon)

    scale = norm_scale.reshape(1, 1)
    bias = enc_bias[None, :]
    coded, slopes = [None] * data_size, [None] * data_size
    coded[0], slopes[0], partial_value = encode(scale, heads[0], enc_weight, bias, dec_weight)
    for g in range(1, data_size):
        coded[g], slopes[g] = encode(scale, heads[g], enc_weight, bias)
    paired = partial_value[:half] + exchange_cores(partial_value[half:])
    summed = paired[:rows_here]
    for slot, mask in enumerate(z_masks):
        summed = summed + swap(
            paired[(slot + 1) * rows_here : (slot + 2) * rows_here], "latent", mask
        )
    rebuilt_own = summed + dec_bias[None, :]
    inputs_own = (heads_out.astype(jnp.float32) * norm_scale).astype(jnp.bfloat16)
    residual_own = (rebuilt_own - inputs_own.astype(jnp.float32)).astype(jnp.bfloat16)
    residuals = gather_groups(residual_own)
    rebuilt = place_rows(rebuilt_own.astype(jnp.bfloat16), shuffle)

    def part(x):
        return lax.dynamic_slice_in_dim(x, first_column, columns_here, 1)

    grads = [
        pre_gradient(all_rows, residuals[g], dec_weight, dec_norms[None, :], slopes[g])
        for g in range(data_size)
    ]
    grad_enc, grad_dec = weight_gradients(
        all_rows,
        scale,
        dec_norms[:, None],
        part(dec_weight),
        [part(x) for x in heads],
        grads,
        coded,
        [part(x) for x in residuals],
    )
    return (rebuilt, grad_enc, grad_dec)


def solution(mesh):
    in_specs = (
        P(("dp", "latent"), None),
        P(("dp", "latent"), None, None),
        P(("dp", "latent"), None, None),
        P(("dp", "latent")),
        P(("dp", "latent")),
        P(None, "latent"),
        P("latent"),
        P("latent", None),
        P(),
    )
    out_specs = (P(("dp", "latent"), None), P("dp", "latent"), P("latent", "dp"))
    return jax.shard_map(shards, mesh=mesh, in_specs=in_specs, out_specs=out_specs, check_vma=False)
```

time: 351 us -> 187 us (0.53)
  waiting for transfers between devices: 243 us -> 55.3 us
  Pallas kernels: 0 us -> 51.6 us
  matrix products: 36.3 us -> 5.45 us
  starting transfers between devices: 9.66 us -> 36.9 us
  between operations: 14.6 us -> 2.12 us
  other arithmetic: 24.4 us -> 12.7 us
  local copies, waits for them, and re-layouts: 11.5 us -> 22.1 us
  blocking collectives: 10.4 us -> 0 us
    reduce_scatter x2 -> x0, waiting for transfers between devices: 162 us -> none  [the longest x1 85.5 us: shards(): lax.psum_scatter(dec_term.astype(jnp.bfloat16), 'dp', scatter_dimension=1...]
    psum x1 -> x0, waiting for transfers between devices: 57.3 us -> none  [shards(): summed = lax.psum(partial_value, 'latent')]
    ppermute x0 -> x37, waiting for transfers between devices: none -> 55.3 us  [swap(): return lax.ppermute(x, axis, [(i, i ^ mask) for i in range(size)])]
    pallas_call x0 -> x9, Pallas kernels: none -> 51.6 us  [the longest x4 28.6 us: encode(): pl.pallas_call(body, grid=(latents // tile,), in_specs=in_specs, out_spec...]
    ppermute x0 -> x37, starting transfers between devices: none -> 36.9 us  [swap(): return lax.ppermute(x, axis, [(i, i ^ mask) for i in range(size)])]
    dot_general x5, matrix products: 35.4 us -> 4.48 us  [the longest x4 3.04 us: place_rows(): jnp.dot(chosen.astype(jnp.bfloat16), rows, preferred_element_type=jnp.flo...]
    all_gather x1 -> x0, waiting for transfers between devices: 21.9 us -> none  [shards(): gathered = lax.all_gather(arrived, 'latent', axis=0, tiled=True)]
    convert_element_type x3 -> x0, other arithmetic: 10.6 us -> none  [the longest x1 4.2 us: shards(): grad_dec = lax.psum_scatter(dec_term.astype(jnp.bfloat16), 'dp', scatter_...]
  transfers between devices with their start and end apart: 6 -> 37, of which waited for: 5 -> 11; matrix products, arithmetic and copies ran while one was open for 8% -> 12% of each run, Pallas kernels for 0% -> 21%
where the time goes in v1:
time: 187 us; the launch traced here: 186 us
  waiting for transfers between devices  55.3 us (30%)
  Pallas kernels  51.6 us (28%)
  starting transfers between devices  36.9 us (20%)
  local copies, waits for them, and re-layouts  22.1 us (12%)
  other arithmetic  12.7 us (7%)
  matrix products  5.45 us (3%)
  between operations  2.12 us (1%)
    ppermute x37, waiting for transfers between devices, swap(): return lax.ppermute(x, axis, [(i, i ^ mask) for i in range(size)])  55.3 us
    ppermute x37, starting transfers between devices, swap(): return lax.ppermute(x, axis, [(i, i ^ mask) for i in range(size)])  36.9 us
    pallas_call x4, Pallas kernels, encode(): pl.pallas_call(body, grid=(latents // tile,), in_specs=in_specs, out_spec...  28.6 us
    pallas_call x4, Pallas kernels, pre_gradient(): pl.pallas_call(functools.partial(slope_body, all_rows), grid=(latents //...  13 us
    pallas_call x1, Pallas kernels, weight_gradients(): pl.pallas_call(functools.partial(weight_body, groups, all_rows), grid=(la...  10.1 us
    unnamed x66, local copies, waits for them, and re-layouts  8.79 us
    reduce_sum x1, other arithmetic, shards(): dec_norms = jnp.sqrt(jnp.sum(jnp.square(dec_float), axis=1) + epsilon)  5.08 us
  transfers between devices with their start and end apart: 37, of which 11 were waited for; matrix products, arithmetic and copies ran while one was open for 12% of the time, Pallas kernels for 21%

profile of v1, /device:TPU:0, one launch (start us, length us, event | category | flops | bytes accessed | tf_op | source)
XLA Modules:
  0.0 186.3 jit_solution(11704457305612317506)
XLA Ops:
  2.4 1.9 reshape_squeeze.6
  4.9 1.9 reshape_squeeze.7
  7.6 5.1 %collective-permute-start.12 = (bf16[32,2048]{1,0:T(8,128)(2,1)S(1)}, bf16[32,2048]{1,0:T(8,128)(2,1)S(1)}, u32[]{:S(2)}, u32[]{:S(2)}) collective-permute-start(bf16[32,2048]{1,0:T(8,128)(2,1)S(1)} %convert_element_type.65), channel_id=1, source_target_pairs={{0,6},{1,7},{2,4},{3,5},{4,2},{5,3},{6,0},{7,1},{8,14},{9,15},{10,... | collective-permute-start | bytes 393224 | tf_op jit(solution)/shard_map/ppermute | solution.py:186
  14.3 1.6 collective-permute-start
  16.5 5.1 %multiply_reduce_fusion = f32[2048]{0:T(1024)S(1)} fusion(bf16[2048,2048]{1,0:T(8,128)(2,1)} %dec_ref.9), kind=kLoop, calls=%fused_computation.1 | loop fusion | flops 12580864 | bytes 8396800 | tf_op jit(solution)/shard_map/reduce_sum | solution.py:271
  21.6 1.7 constant_dynamic-slice_fusion.8.dec_ref
  27.1 1.6 constant_dynamic-update-slice_fusion.2
  28.7 1.6 collective-permute-start.4
  35.6 3.7 %collective-permute-start.9 = (f32[1,128]{1,0:T(1,128)S(1)}, f32[1,128]{1,0:T(1,128)S(1)}, u32[]{:S(2)}, u32[]{:S(2)}) collective-permute-start(f32[1,128]{1,0:T(1,128)S(1)} %add_add_fusion), channel_id=1, source_target_pairs={{0,6},{1,7},{2,4},{3,5},{4,2},{5,3},{6,0},{7,1},{8,14},{9,15},{10,... | collective-permute-start | bytes 1544 | tf_op jit(solution)/shard_map/ppermute | solution.py:186
  41.3 2.5 %collective-permute-done.8 = f32[1,128]{1,0:T(1,128)S(1)} collective-permute-done((f32[1,128]{1,0:T(1,128)S(1)}, f32[1,128]{1,0:T(1,128)S(1)}, u32[]{:S(2)}, u32[]{:S(2)}) %collective-permute-start.8) | collective-permute-done | bytes 544 | tf_op jit(solution)/shard_map/ppermute | solution.py:186
  45.1 2.5 %collective-permute-start.25 = (bf16[128,2048]{1,0:T(8,128)(2,1)}, bf16[128,2048]{1,0:T(8,128)(2,1)S(1)}, u32[]{:S(2)}, u32[]{:S(2)}) collective-permute-start(bf16[128,2048]{1,0:T(8,128)(2,1)} %get-tuple-element.37), channel_id=1, source_target_pairs={{0,24},{8,16},{16,8},{24,0},{1,25},{9,17},{17,9},{25,1},{2,26},{10... | collective-permute-start | bytes 1572872 | tf_op jit(solution)/shard_map/ppermute | solution.py:186
  49.8 3.4 %copy-done = bf16[2048,2048]{1,0:T(8,128)(2,1)S(1)} copy-done((bf16[2048,2048]{1,0:T(8,128)(2,1)S(1)}, bf16[2048,2048]{1,0:T(8,128)(2,1)}, u32[]{:S(2)}) %copy-start) | copy-done | bytes 8388632
  53.1 10.8 %shard_map.112 = (bf16[256,2048]{1,0:T(8,128)(2,1)S(1)}, bf16[256,2048]{1,0:T(8,128)(2,1)S(1)}, f32[256,2048]{1,0:T(8,128)S(1)}) custom-call(f32[1,1]{1,0:T(1,128)} %bitcast.3.scale_ref, bf16[256,2048]{1,0:T(8,128)(2,1)S(1)} %constant_dynamic-update-slice_fusion.4.rows_ref, bf16[2048,2048]{1,0:T(8,128)(2,1)S(1)} %copy-done, f32[1,2048]{1,0:T(1,128)S(1)} %bitcast.22, ...), custom_call_target="tpu_custom_call" | custom-call | flops 4294967296 | bytes 16777216 | tf_op jit(solution)/shard_map/pallas_call | solution.py:97
  64.1 5.8 %collective-permute-done.23 = bf16[128,2048]{1,0:T(8,128)(2,1)S(1)} collective-permute-done((bf16[128,2048]{1,0:T(8,128)(2,1)}, bf16[128,2048]{1,0:T(8,128)(2,1)S(1)}, u32[]{:S(2)}, u32[]{:S(2)}) %collective-permute-start.23) | collective-permute-done | bytes 524320 | tf_op jit(solution)/shard_map/ppermute | solution.py:186
  73.4 5.9 %shard_map.118 = (bf16[256,2048]{1,0:T(8,128)(2,1)S(1)}, bf16[256,2048]{1,0:T(8,128)(2,1)S(1)}) custom-call(f32[1,1]{1,0:T(1,128)} %bitcast.3.scale_ref, bf16[256,2048]{1,0:T(8,128)(2,1)S(1)} %constant_dynamic-update-slice_fusion.13.rows_ref, bf16[2048,2048]{1,0:T(8,128)(2,1)S(1)} %copy-done, f32[1,2048]{1,0:T(1,128)S(1)} %bitcast.23), custom_call_target="tpu_custom_call" | custom-call | flops 2147483648 | bytes 16777216 | tf_op jit(solution)/shard_map/pallas_call | solution.py:97
  80.3 5.9 %shard_map.116 = (bf16[256,2048]{1,0:T(8,128)(2,1)S(1)}, bf16[256,2048]{1,0:T(8,128)(2,1)S(1)}) custom-call(f32[1,1]{1,0:T(1,128)} %bitcast.3.scale_ref, bf16[256,2048]{1,0:T(8,128)(2,1)S(1)} %constant_dynamic-update-slice_fusion.11.rows_ref, bf16[2048,2048]{1,0:T(8,128)(2,1)S(1)} %copy-done, f32[1,2048]{1,0:T(1,128)S(1)} %bitcast.24), custom_call_target="tpu_custom_call" | custom-call | flops 2147483648 | bytes 16777216 | tf_op jit(solution)/shard_map/pallas_call | solution.py:97
  87.6 3.2 %collective-permute-start.17 = (f32[32,2048]{1,0:T(8,128)}, f32[32,2048]{1,0:T(8,128)}, u32[]{:S(2)}, u32[]{:S(2)}) collective-permute-start(f32[32,2048]{1,0:T(8,128)} %get-tuple-element.35), channel_id=1, source_target_pairs={{0,6},{1,7},{2,4},{3,5},{4,2},{5,3},{6,0},{7,1},{8,14},{9,15},{10,... | collective-permute-start | bytes 786440 | tf_op jit(solution)/shard_map/ppermute | solution.py:186
  91.8 5.9 %shard_map.114 = (bf16[256,2048]{1,0:T(8,128)(2,1)S(1)}, bf16[256,2048]{1,0:T(8,128)(2,1)S(1)}) custom-call(f32[1,1]{1,0:T(1,128)} %bitcast.3.scale_ref, bf16[256,2048]{1,0:T(8,128)(2,1)S(1)} %constant_dynamic-update-slice_fusion.9.rows_ref, bf16[2048,2048]{1,0:T(8,128)(2,1)S(1)} %copy-done, f32[1,2048]{1,0:T(1,128)S(1)} %bitcast.25), custom_call_target="tpu_custom_call" | custom-call | flops 2147483648 | bytes 16777216 | tf_op jit(solution)/shard_map/pallas_call | solution.py:97
  97.8 6.2 %collective-permute-done.17 = f32[32,2048]{1,0:T(8,128)} collective-permute-done((f32[32,2048]{1,0:T(8,128)}, f32[32,2048]{1,0:T(8,128)}, u32[]{:S(2)}, u32[]{:S(2)}) %collective-permute-start.17) | collective-permute-done | bytes 262176 | tf_op jit(solution)/shard_map/ppermute | solution.py:186
  104.0 10.3 %collective-permute-done.16 = f32[32,2048]{1,0:T(8,128)} collective-permute-done((f32[32,2048]{1,0:T(8,128)}, f32[32,2048]{1,0:T(8,128)}, u32[]{:S(2)}, u32[]{:S(2)}) %collective-permute-start.16) | collective-permute-done | bytes 262176 | tf_op jit(solution)/shard_map/ppermute | solution.py:186
  117.8 1.8 collective-permute-start.20
  122.2 1.8 collective-permute-start.29
  124.0 2.6 %collective-permute-start.27 = (bf16[32,2048]{1,0:T(8,128)(2,1)S(1)}, bf16[32,2048]{1,0:T(8,128)(2,1)S(1)}, u32[]{:S(2)}, u32[]{:S(2)}) collective-permute-start(bf16[32,2048]{1,0:T(8,128)(2,1)S(1)} %get-tuple-element.30), channel_id=1, source_target_pairs={{0,2},{1,3},{2,0},{3,1},{4,6},{5,7},{6,4},{7,5},{8,10},{9,11},{10,... | collective-permute-start | bytes 393224 | tf_op jit(solution)/shard_map/ppermute | solution.py:186
  128.0 2.4 %collective-permute-done.29 = bf16[32,2048]{1,0:T(8,128)(2,1)S(1)} collective-permute-done((bf16[32,2048]{1,0:T(8,128)(2,1)S(1)}, bf16[32,2048]{1,0:T(8,128)(2,1)S(1)}, u32[]{:S(2)}, u32[]{:S(2)}) %collective-permute-start.29) | collective-permute-done | bytes 131104 | tf_op jit(solution)/shard_map/ppermute | solution.py:186
  130.4 3.6 %collective-permute-done.28 = bf16[32,2048]{1,0:T(8,128)(2,1)S(1)} collective-permute-done((bf16[32,2048]{1,0:T(8,128)(2,1)S(1)}, bf16[32,2048]{1,0:T(8,128)(2,1)S(1)}, u32[]{:S(2)}, u32[]{:S(2)}) %collective-permute-start.28) | collective-permute-done | bytes 131104 | tf_op jit(solution)/shard_map/ppermute | solution.py:186
  134.0 1.8 collective-permute-start.35
  137.7 21.8 %collective-permute-done.33 = bf16[128,2048]{1,0:T(8,128)(2,1)S(1)} collective-permute-done((bf16[128,2048]{1,0:T(8,128)(2,1)S(1)}, bf16[128,2048]{1,0:T(8,128)(2,1)S(1)}, u32[]{:S(2)}, u32[]{:S(2)}) %collective-permute-start.33) | collective-permute-done | bytes 524320 | tf_op jit(solution)/shard_map/ppermute | solution.py:186
  160.2 3.2 %shard_map.113.refs_4_ = bf16[256,2048]{1,0:T(8,128)(2,1)S(1)} custom-call(bf16[256,2048]{1,0:T(8,128)(2,1)S(1)} %constant_dynamic-update-slice_fusion.15.residual_ref, bf16[2048,2048]{1,0:T(8,128)(2,1)S(1)} %bitcast.16, f32[1,2048]{1,0:T(1,128)S(1)} %bitcast.18, bf16[256,2048]{1,0:T(8,128)(2,1)S(1)} %get-tuple-element.15.slope_ref), custom_call_target="tpu_custom_call" | custom-call | flops 2147483648 | bytes 8388608 | tf_op jit(solution)/shard_map/pallas_call | solution.py:121
  165.0 3.2 %shard_map.115.refs_5_ = bf16[256,2048]{1,0:T(8,128)(2,1)S(1)} custom-call(bf16[256,2048]{1,0:T(8,128)(2,1)S(1)} %constant_dynamic-update-slice_fusion.20.residual_ref, bf16[2048,2048]{1,0:T(8,128)(2,1)S(1)} %bitcast.16, f32[1,2048]{1,0:T(1,128)S(1)} %bitcast.19, bf16[256,2048]{1,0:T(8,128)(2,1)S(1)} %copy-done.4), custom_call_target="tpu_custom_call" | custom-call | flops 2147483648 | bytes 8388608 | tf_op jit(solution)/shard_map/pallas_call | solution.py:121
  168.3 3.2 %shard_map.117.refs_6_ = bf16[256,2048]{1,0:T(8,128)(2,1)S(1)} custom-call(bf16[256,2048]{1,0:T(8,128)(2,1)S(1)} %constant_dynamic-update-slice_fusion.22.residual_ref, bf16[2048,2048]{1,0:T(8,128)(2,1)S(1)} %bitcast.16, f32[1,2048]{1,0:T(1,128)S(1)} %bitcast.20, bf16[256,2048]{1,0:T(8,128)(2,1)S(1)} %copy-done.2), custom_call_target="tpu_custom_call" | custom-call | flops 2147483648 | bytes 8388608 | tf_op jit(solution)/shard_map/pallas_call | solution.py:121
  172.9 3.2 %shard_map.119.refs_7_ = bf16[256,2048]{1,0:T(8,128)(2,1)S(1)} custom-call(bf16[256,2048]{1,0:T(8,128)(2,1)S(1)} %constant_dynamic-update-slice_fusion.24.residual_ref, bf16[2048,2048]{1,0:T(8,128)(2,1)S(1)} %bitcast.16, f32[1,2048]{1,0:T(1,128)S(1)} %bitcast.21, bf16[256,2048]{1,0:T(8,128)(2,1)S(1)} %get-tuple-element.18.slope_ref), custom_call_target="tpu_custom_call" | custom-call | flops 2147483648 | bytes 8388608 | tf_op jit(solution)/shard_map/pallas_call | solution.py:121
  176.2 10.1 %shard_map.120 = (f32[512,2048]{1,0:T(8,128)}, f32[2048,512]{1,0:T(8,128)}) custom-call(f32[1,1]{1,0:T(1,128)} %bitcast.3.scale_ref, f32[2048,1]{1,0:T(8,128)S(1)} %copy-done.5, bf16[2048,512]{1,0:T(8,128)(2,1)S(1)} %constant_dynamic-slice_fusion.8.dec_ref, bf16[256,512]{1,0:T(8,128)(2,1)S(1)} %constant_dynamic-slice_fusion.7.refs_0_, ...), custom_call_target="tpu_custom_call" | custom-call | flops 4294967296 | bytes 16777216 | tf_op jit(solution)/shard_map/pallas_call | solution.py:159
  (169 shorter events, 38.6 us)
Async XLA Ops:
  7.6 23.5 %collective-permute-start.12 = (bf16[32,2048]{1,0:T(8,128)(2,1)S(1)}, bf16[32,2048]{1,0:T(8,128)(2,1)S(1)}, u32[]{:S(2)}, u32[]{:S(2)}) collective-permute-start(bf16[32,2048]{1,0:T(8,128)(2,1)S(1)} %convert_element_type.65), channel_id=1, source_target_pairs={{0,6},{1,7},{2,4},{3,5},{4,2},{5,3},{6,0},{7,1},{8,14},{9,15},{10,... | collective-permute-start | bytes 393224 | tf_op jit(solution)/shard_map/ppermute | solution.py:186
  12.7 16.1 %collective-permute-start.11 = (bf16[32,2048]{1,0:T(8,128)(2,1)S(1)}, bf16[32,2048]{1,0:T(8,128)(2,1)S(1)}, u32[]{:S(2)}, u32[]{:S(2)}) collective-permute-start(bf16[32,2048]{1,0:T(8,128)(2,1)S(1)} %convert_element_type.65), channel_id=1, source_target_pairs={{0,4},{1,5},{2,6},{3,7},{4,0},{5,1},{6,2},{7,3},{8,12},{9,13},{10,... | collective-permute-start | bytes 393224 | tf_op jit(solution)/shard_map/ppermute | solution.py:186
  12.7 14.1 %collective-permute-start.10 = (bf16[32,2048]{1,0:T(8,128)(2,1)S(1)}, bf16[32,2048]{1,0:T(8,128)(2,1)}, u32[]{:S(2)}, u32[]{:S(2)}) collective-permute-start(bf16[32,2048]{1,0:T(8,128)(2,1)S(1)} %convert_element_type.65), channel_id=1, source_target_pairs={{0,2},{1,3},{2,0},{3,1},{4,6},{5,7},{6,4},{7,5},{8,10},{9,11},{10,... | collective-permute-start | bytes 393224 | tf_op jit(solution)/shard_map/ppermute | solution.py:186
  14.3 25.0 %collective-permute-start = (s32[8]{0:T(128)}, s32[8]{0:T(128)}, u32[]{:S(2)}, u32[]{:S(2)}) collective-permute-start(s32[8]{0:T(128)} %get-tuple-element.26), channel_id=1, source_target_pairs={{0,8},{8,0},{16,24},{24,16},{1,9},{9,1},{17,25},{25,17},{2,10},{10... | collective-permute-start | bytes 104 | tf_op jit(solution)/shard_map/ppermute | solution.py:186
  16.5 7.5 %collective-permute-start.3 = (f32[1,128]{1,0:T(1,128)}, f32[1,128]{1,0:T(1,128)}, u32[]{:S(2)}, u32[]{:S(2)}) collective-permute-start(f32[1,128]{1,0:T(1,128)} %bitcast.2), channel_id=1, source_target_pairs={{0,1},{1,0},{2,3},{3,2},{4,5},{5,4},{6,7},{7,6},{8,9},{9,8},{10,11... | collective-permute-start | bytes 1544 | tf_op jit(solution)/shard_map/ppermute | solution.py:186
  25.3 7.8 %collective-permute-start.6 = (f32[1,128]{1,0:T(1,128)}, f32[1,128]{1,0:T(1,128)}, u32[]{:S(2)}, u32[]{:S(2)}) collective-permute-start(f32[1,128]{1,0:T(1,128)} %bitcast_add_fusion), channel_id=1, source_target_pairs={{0,24},{8,16},{16,8},{24,0},{1,25},{9,17},{17,9},{25,1},{2,26},{10... | collective-permute-start | bytes 1544 | tf_op jit(solution)/shard_map/ppermute | solution.py:186
  26.8 7.8 %collective-permute-start.5 = (f32[1,128]{1,0:T(1,128)}, f32[1,128]{1,0:T(1,128)}, u32[]{:S(2)}, u32[]{:S(2)}) collective-permute-start(f32[1,128]{1,0:T(1,128)} %bitcast_add_fusion), channel_id=1, source_target_pairs={{0,16},{8,24},{16,0},{24,8},{1,17},{9,25},{17,1},{25,9},{2,18},{10... | collective-permute-start | bytes 1544 | tf_op jit(solution)/shard_map/ppermute | solution.py:186
  28.7 6.2 %collective-permute-start.4 = (f32[1,128]{1,0:T(1,128)}, f32[1,128]{1,0:T(1,128)}, u32[]{:S(2)}, u32[]{:S(2)}) collective-permute-start(f32[1,128]{1,0:T(1,128)} %bitcast_add_fusion), channel_id=1, source_target_pairs={{0,8},{8,0},{16,24},{24,16},{1,9},{9,1},{17,25},{25,17},{2,10},{10... | collective-permute-start | bytes 1544 | tf_op jit(solution)/shard_map/ppermute | solution.py:186
  31.7 17.0 %collective-permute-start.13 = (bf16[128,2048]{1,0:T(8,128)(2,1)}, bf16[128,2048]{1,0:T(8,128)(2,1)}, u32[]{:S(2)}, u32[]{:S(2)}) collective-permute-start(bf16[128,2048]{1,0:T(8,128)(2,1)} %get-tuple-element.37), channel_id=1, source_target_pairs={{0,1},{1,0},{2,3},{3,2},{4,5},{5,4},{6,7},{7,6},{8,9},{9,8},{10,11... | collective-permute-start | bytes 1572872 | tf_op jit(solution)/shard_map/ppermute | solution.py:186
  33.1 6.3 %collective-permute-start.1 = (s32[8]{0:T(128)}, s32[8]{0:T(128)S(1)}, u32[]{:S(2)}, u32[]{:S(2)}) collective-permute-start(s32[8]{0:T(128)} %get-tuple-element.27), channel_id=1, source_target_pairs={{0,16},{8,24},{16,0},{24,8},{1,17},{9,25},{17,1},{25,9},{2,18},{10... | collective-permute-start | bytes 104 | tf_op jit(solution)/shard_map/ppermute | solution.py:186
  34.6 5.4 %collective-permute-start.2 = (s32[8]{0:T(128)}, s32[8]{0:T(128)S(1)}, u32[]{:S(2)}, u32[]{:S(2)}) collective-permute-start(s32[8]{0:T(128)} %get-tuple-element.28), channel_id=1, source_target_pairs={{0,24},{8,16},{16,8},{24,0},{1,25},{9,17},{17,9},{25,1},{2,26},{10... | collective-permute-start | bytes 104 | tf_op jit(solution)/shard_map/ppermute | solution.py:186
  35.6 5.6 %collective-permute-start.9 = (f32[1,128]{1,0:T(1,128)S(1)}, f32[1,128]{1,0:T(1,128)S(1)}, u32[]{:S(2)}, u32[]{:S(2)}) collective-permute-start(f32[1,128]{1,0:T(1,128)S(1)} %add_add_fusion), channel_id=1, source_target_pairs={{0,6},{1,7},{2,4},{3,5},{4,2},{5,3},{6,0},{7,1},{8,14},{9,15},{10,... | collective-permute-start | bytes 1544 | tf_op jit(solution)/shard_map/ppermute | solution.py:186
  45.1 25.3 %collective-permute-start.25 = (bf16[128,2048]{1,0:T(8,128)(2,1)}, bf16[128,2048]{1,0:T(8,128)(2,1)S(1)}, u32[]{:S(2)}, u32[]{:S(2)}) collective-permute-start(bf16[128,2048]{1,0:T(8,128)(2,1)} %get-tuple-element.37), channel_id=1, source_target_pairs={{0,24},{8,16},{16,8},{24,0},{1,25},{9,17},{17,9},{25,1},{2,26},{10... | collective-permute-start | bytes 1572872 | tf_op jit(solution)/shard_map/ppermute | solution.py:186
  47.6 22.2 %collective-permute-start.23 = (bf16[128,2048]{1,0:T(8,128)(2,1)}, bf16[128,2048]{1,0:T(8,128)(2,1)S(1)}, u32[]{:S(2)}, u32[]{:S(2)}) collective-permute-start(bf16[128,2048]{1,0:T(8,128)(2,1)} %get-tuple-element.37), channel_id=1, source_target_pairs={{0,16},{8,24},{16,0},{24,8},{1,17},{9,25},{17,1},{25,9},{2,18},{10... | collective-permute-start | bytes 1572872 | tf_op jit(solution)/shard_map/ppermute | solution.py:186
  48.1 21.8 %collective-permute-start.21 = (bf16[128,2048]{1,0:T(8,128)(2,1)}, bf16[128,2048]{1,0:T(8,128)(2,1)S(1)}, u32[]{:S(2)}, u32[]{:S(2)}) collective-permute-start(bf16[128,2048]{1,0:T(8,128)(2,1)} %get-tuple-element.37), channel_id=1, source_target_pairs={{0,8},{8,0},{16,24},{24,16},{1,9},{9,1},{17,25},{25,17},{2,10},{10... | collective-permute-start | bytes 1572872 | tf_op jit(solution)/shard_map/ppermute | solution.py:186
  64.0 22.4 %collective-permute-start.14 = (f32[128,2048]{1,0:T(8,128)S(1)}, f32[128,2048]{1,0:T(8,128)S(1)}, u32[]{:S(2)}, u32[]{:S(2)}) collective-permute-start(f32[128,2048]{1,0:T(8,128)S(1)} %slice.19), channel_id=1, source_target_pairs={{0,1},{1,0},{2,3},{3,2},{4,5},{5,4},{6,7},{7,6},{8,9},{9,8},{10,11... | collective-permute-start | bytes 3145736 | tf_op jit(solution)/shard_map/ppermute | solution.py:186
  70.0 16.3 %collective-permute-start.22 = (bf16[128,2048]{1,0:T(8,128)(2,1)S(1)}, bf16[128,2048]{1,0:T(8,128)(2,1)S(1)}, u32[]{:S(2)}, u32[]{:S(2)}) collective-permute-start(bf16[128,2048]{1,0:T(8,128)(2,1)S(1)} %collective-permute-done.21), channel_id=1, source_target_pairs={{0,1},{1,0},{2,3},{3,2},{4,5},{5,4},{6,7},{7,6},{8,9},{9,8},{10,11... | collective-permute-start | bytes 1572872 | tf_op jit(solution)/shard_map/ppermute | solution.py:186
  87.6 10.2 %collective-permute-start.15 = (f32[32,2048]{1,0:T(8,128)}, f32[32,2048]{1,0:T(8,128)}, u32[]{:S(2)}, u32[]{:S(2)}) collective-permute-start(f32[32,2048]{1,0:T(8,128)} %get-tuple-element.34), channel_id=1, source_target_pairs={{0,2},{1,3},{2,0},{3,1},{4,6},{5,7},{6,4},{7,5},{8,10},{9,11},{10,... | collective-permute-start | bytes 786440 | tf_op jit(solution)/shard_map/ppermute | solution.py:186
  87.6 16.4 %collective-permute-start.17 = (f32[32,2048]{1,0:T(8,128)}, f32[32,2048]{1,0:T(8,128)}, u32[]{:S(2)}, u32[]{:S(2)}) collective-permute-start(f32[32,2048]{1,0:T(8,128)} %get-tuple-element.35), channel_id=1, source_target_pairs={{0,6},{1,7},{2,4},{3,5},{4,2},{5,3},{6,0},{7,1},{8,14},{9,15},{10,... | collective-permute-start | bytes 786440 | tf_op jit(solution)/shard_map/ppermute | solution.py:186
  90.8 23.5 %collective-permute-start.16 = (f32[32,2048]{1,0:T(8,128)}, f32[32,2048]{1,0:T(8,128)}, u32[]{:S(2)}, u32[]{:S(2)}) collective-permute-start(f32[32,2048]{1,0:T(8,128)} %get-tuple-element.36), channel_id=1, source_target_pairs={{0,4},{1,5},{2,6},{3,7},{4,0},{5,1},{6,2},{7,3},{8,12},{9,13},{10,... | collective-permute-start | bytes 786440 | tf_op jit(solution)/shard_map/ppermute | solution.py:186
  117.8 6.2 %collective-permute-start.20 = (bf16[8,2048]{1,0:T(8,128)(2,1)S(1)}, bf16[8,2048]{1,0:T(8,128)(2,1)S(1)}, u32[]{:S(2)}, u32[]{:S(2)}) collective-permute-start(bf16[8,2048]{1,0:T(8,128)(2,1)S(1)} %convolution_convert_fusion.1), channel_id=1, source_target_pairs={{0,24},{8,16},{16,8},{24,0},{1,25},{9,17},{17,9},{25,1},{2,26},{10... | collective-permute-start | bytes 98312 | tf_op jit(solution)/shard_map/ppermute | solution.py:186
  119.6 7.0 %collective-permute-start.18 = (bf16[8,2048]{1,0:T(8,128)(2,1)S(1)}, bf16[8,2048]{1,0:T(8,128)(2,1)S(1)}, u32[]{:S(2)}, u32[]{:S(2)}) collective-permute-start(bf16[8,2048]{1,0:T(8,128)(2,1)S(1)} %convolution_convert_fusion.3), channel_id=1, source_target_pairs={{0,8},{8,0},{16,24},{24,16},{1,9},{9,1},{17,25},{25,17},{2,10},{10... | collective-permute-start | bytes 98312 | tf_op jit(solution)/shard_map/ppermute | solution.py:186
  120.8 5.7 %collective-permute-start.19 = (bf16[8,2048]{1,0:T(8,128)(2,1)S(1)}, bf16[8,2048]{1,0:T(8,128)(2,1)S(1)}, u32[]{:S(2)}, u32[]{:S(2)}) collective-permute-start(bf16[8,2048]{1,0:T(8,128)(2,1)S(1)} %convolution_convert_fusion.2), channel_id=1, source_target_pairs={{0,16},{8,24},{16,0},{24,8},{1,17},{9,25},{17,1},{25,9},{2,18},{10... | collective-permute-start | bytes 98312 | tf_op jit(solution)/shard_map/ppermute | solution.py:186
  122.2 8.2 %collective-permute-start.29 = (bf16[32,2048]{1,0:T(8,128)(2,1)S(1)}, bf16[32,2048]{1,0:T(8,128)(2,1)S(1)}, u32[]{:S(2)}, u32[]{:S(2)}) collective-permute-start(bf16[32,2048]{1,0:T(8,128)(2,1)S(1)} %get-tuple-element.30), channel_id=1, source_target_pairs={{0,6},{1,7},{2,4},{3,5},{4,2},{5,3},{6,0},{7,1},{8,14},{9,15},{10,... | collective-permute-start | bytes 393224 | tf_op jit(solution)/shard_map/ppermute | solution.py:186
  124.0 10.0 %collective-permute-start.28 = (bf16[32,2048]{1,0:T(8,128)(2,1)S(1)}, bf16[32,2048]{1,0:T(8,128)(2,1)S(1)}, u32[]{:S(2)}, u32[]{:S(2)}) collective-permute-start(bf16[32,2048]{1,0:T(8,128)(2,1)S(1)} %get-tuple-element.30), channel_id=1, source_target_pairs={{0,4},{1,5},{2,6},{3,7},{4,0},{5,1},{6,2},{7,3},{8,12},{9,13},{10,... | collective-permute-start | bytes 393224 | tf_op jit(solution)/shard_map/ppermute | solution.py:186
  124.0 10.0 %collective-permute-start.27 = (bf16[32,2048]{1,0:T(8,128)(2,1)S(1)}, bf16[32,2048]{1,0:T(8,128)(2,1)S(1)}, u32[]{:S(2)}, u32[]{:S(2)}) collective-permute-start(bf16[32,2048]{1,0:T(8,128)(2,1)S(1)} %get-tuple-element.30), channel_id=1, source_target_pairs={{0,2},{1,3},{2,0},{3,1},{4,6},{5,7},{6,4},{7,5},{8,10},{9,11},{10,... | collective-permute-start | bytes 393224 | tf_op jit(solution)/shard_map/ppermute | solution.py:186
  134.0 29.4 %collective-permute-start.35 = (bf16[128,2048]{1,0:T(8,128)(2,1)S(1)}, bf16[128,2048]{1,0:T(8,128)(2,1)}, u32[]{:S(2)}, u32[]{:S(2)}) collective-permute-start(bf16[128,2048]{1,0:T(8,128)(2,1)S(1)} %pad_maximum_fusion), channel_id=1, source_target_pairs={{0,24},{8,16},{16,8},{24,0},{1,25},{9,17},{17,9},{25,1},{2,26},{10... | collective-permute-start | bytes 1572872 | tf_op jit(solution)/shard_map/ppermute | solution.py:186
  135.9 23.6 %collective-permute-start.33 = (bf16[128,2048]{1,0:T(8,128)(2,1)S(1)}, bf16[128,2048]{1,0:T(8,128)(2,1)S(1)}, u32[]{:S(2)}, u32[]{:S(2)}) collective-permute-start(bf16[128,2048]{1,0:T(8,128)(2,1)S(1)} %pad_maximum_fusion), channel_id=1, source_target_pairs={{0,16},{8,24},{16,0},{24,8},{1,17},{9,25},{17,1},{25,9},{2,18},{10... | collective-permute-start | bytes 1572872 | tf_op jit(solution)/shard_map/ppermute | solution.py:186
  137.1 22.5 %collective-permute-start.31 = (bf16[128,2048]{1,0:T(8,128)(2,1)S(1)}, bf16[128,2048]{1,0:T(8,128)(2,1)S(1)}, u32[]{:S(2)}, u32[]{:S(2)}) collective-permute-start(bf16[128,2048]{1,0:T(8,128)(2,1)S(1)} %pad_maximum_fusion), channel_id=1, source_target_pairs={{0,8},{8,0},{16,24},{24,16},{1,9},{9,1},{17,25},{25,17},{2,10},{10... | collective-permute-start | bytes 1572872 | tf_op jit(solution)/shard_map/ppermute | solution.py:186
  137.6 22.5 %collective-permute-start.30 = (bf16[128,2048]{1,0:T(8,128)(2,1)S(1)}, bf16[128,2048]{1,0:T(8,128)(2,1)S(1)}, u32[]{:S(2)}, u32[]{:S(2)}) collective-permute-start(bf16[128,2048]{1,0:T(8,128)(2,1)S(1)} %pad_maximum_fusion), channel_id=1, source_target_pairs={{0,1},{1,0},{2,3},{3,2},{4,5},{5,4},{6,7},{7,6},{8,9},{9,8},{10,11... | collective-permute-start | bytes 1572872 | tf_op jit(solution)/shard_map/ppermute | solution.py:186
  159.5 5.4 %collective-permute-start.34 = (bf16[128,2048]{1,0:T(8,128)(2,1)S(1)}, bf16[128,2048]{1,0:T(8,128)(2,1)S(1)}, u32[]{:S(2)}, u32[]{:S(2)}) collective-permute-start(bf16[128,2048]{1,0:T(8,128)(2,1)S(1)} %collective-permute-done.33), channel_id=1, source_target_pairs={{0,1},{1,0},{2,3},{3,2},{4,5},{5,4},{6,7},{7,6},{8,9},{9,8},{10,11... | collective-permute-start | bytes 1572872 | tf_op jit(solution)/shard_map/ppermute | solution.py:186
  163.5 8.1 %collective-permute-start.36 = (bf16[128,2048]{1,0:T(8,128)(2,1)}, bf16[128,2048]{1,0:T(8,128)(2,1)}, u32[]{:S(2)}, u32[]{:S(2)}) collective-permute-start(bf16[128,2048]{1,0:T(8,128)(2,1)} %collective-permute-done.35), channel_id=1, source_target_pairs={{0,1},{1,0},{2,3},{3,2},{4,5},{5,4},{6,7},{7,6},{8,9},{9,8},{10,11... | collective-permute-start | bytes 1572872 | tf_op jit(solution)/shard_map/ppermute | solution.py:186
  (32 other events, 487.3 us)

commit v2 on v0

v2 whole, which is shorter than its diff:
```python
import functools

import jax
import jax.numpy as jnp
from jax import lax
from jax.experimental import pallas as pl
from jax.experimental.pallas import tpu as pltpu
from jax.sharding import PartitionSpec as P

HEAD_DIM = 256


sharpness = 4.0
sparsity_weight = 1.0
epsilon = 1e-06

MIB = 1024 * 1024
LOG2E = 1.4426950408889634
IN_VMEM = pl.BlockSpec(memory_space=pltpu.VMEM)
IN_HBM = pl.BlockSpec(memory_space=pltpu.HBM)
IN_SMEM = pl.BlockSpec(memory_space=pltpu.SMEM)


def kernel_call(body, args, specs, outs, scratch=(), out_specs=None, flops=0, limit=24):
    return pl.pallas_call(
        body,
        in_specs=specs,
        out_specs=out_specs or [IN_VMEM] * len(outs),
        out_shape=outs,
        scratch_shapes=list(scratch),
        compiler_params=pltpu.CompilerParams(vmem_limit_bytes=limit * MIB),
        cost_estimate=pl.CostEstimate(flops=flops, bytes_accessed=0, transcendentals=0),
    )(*args)


def held(x):
    return pltpu.with_memory_space_constraint(x, pltpu.VMEM)


def half_array(*shape):
    return jax.ShapeDtypeStruct(shape, jnp.bfloat16)


def float_array(*shape):
    return jax.ShapeDtypeStruct(shape, jnp.float32)


def attend_body(
    kv_heads, parts, positions_ref, queries, keys, values, enc, heads_ref, energy_ref, enc_ref, q, k, v, sems, enc_sems
):
    rows, width = q.shape
    per_head = width // kv_heads // HEAD_DIM
    whole = pltpu.make_async_copy(queries, q, sems.at[2 * kv_heads])
    whole.start()
    copies = []
    for g in range(kv_heads):
        here = pl.ds(g * HEAD_DIM, HEAD_DIM)
        copies.append(pltpu.make_async_copy(keys.at[0, :, here], k.at[:, here], sems.at[2 * g]))
        copies.append(pltpu.make_async_copy(values.at[0, :, here], v.at[:, here], sems.at[2 * g + 1]))
    size = enc.shape[0] // parts
    weights = []
    for part in range(parts):
        here = pl.ds(part * size, size)
        weights.append(pltpu.make_async_copy(enc.at[here], enc_ref.at[here], enc_sems.at[part]))
    for copy in copies + weights:
        copy.start()
    whole.wait()
    shape = (rows, keys.shape[1])
    row_index = lax.broadcasted_iota(jnp.int32, shape, 0)
    visible = lax.broadcasted_iota(jnp.int32, shape, 1) <= positions_ref[0] + row_index
    visible = jnp.concatenate([visible] * per_head, axis=0)
    energy = jnp.zeros((1, 128), jnp.float32)
    for g in range(kv_heads):
        heads = [slice((g * per_head + i) * HEAD_DIM, (g * per_head + i + 1) * HEAD_DIM) for i in range(per_head)]
        grouped = jnp.concatenate([q[:, head] for head in heads], axis=0)
        here = slice(g * HEAD_DIM, (g + 1) * HEAD_DIM)
        copies[2 * g].wait()
        scores = lax.dot_general(
            grouped, k[:, here], (((1,), (1,)), ((), ())), preferred_element_type=jnp.float32
        ) * HEAD_DIM ** (-0.5)
        scores = jnp.where(visible, scores, -jnp.inf)
        weight = jnp.exp(scores - jnp.max(scores, axis=1, keepdims=True))
        probs = (weight / jnp.sum(weight, axis=1, keepdims=True)).astype(jnp.bfloat16)
        copies[2 * g + 1].wait()
        mix = jnp.dot(probs, v[:, here], preferred_element_type=jnp.float32).astype(jnp.bfloat16)
        for i, head in enumerate(heads):
            part = mix[i * rows : (i + 1) * rows]
            heads_ref[:, head] = part
            square = jnp.sum(jnp.square(part.astype(jnp.float32)), axis=0, keepdims=True)
            for lane in range(0, HEAD_DIM, 128):
                energy = energy + square[:, lane : lane + 128]
    energy_ref[...] = energy
    for copy in weights:
        copy.wait()


def attend(queries, cache_keys, cache_values, positions, enc, parts=8):
    rows, width = queries.shape
    slots, kv_width = cache_keys.shape[1:]
    kv_heads = kv_width // HEAD_DIM
    hbm = [pltpu.with_memory_space_constraint(x, pltpu.HBM) for x in (queries, cache_keys, cache_values, enc)]
    return kernel_call(
        functools.partial(attend_body, kv_heads, parts),
        [positions, *hbm],
        [IN_SMEM] + [IN_HBM] * 4,
        [half_array(rows, width), float_array(1, 128), pltpu.VMEM(enc.shape, enc.dtype)],
        [
            pltpu.VMEM((rows, width), jnp.bfloat16),
            pltpu.VMEM((slots, kv_width), jnp.bfloat16),
            pltpu.VMEM((slots, kv_width), jnp.bfloat16),
            pltpu.SemaphoreType.DMA((2 * kv_heads + 1,)),
            pltpu.SemaphoreType.DMA((parts,)),
        ],
        flops=4 * rows * slots * width,
    )


def norms_body(block, dec_ref, column_ref, row_ref):
    for first in range(0, dec_ref.shape[0], block):
        here = slice(first, first + block)
        square = jnp.square(dec_ref[here, :].astype(jnp.float32))
        norms = jnp.sqrt(jnp.sum(square, axis=1, keepdims=True) + epsilon)
        column_ref[here, :] = norms
        row_ref[:, here] = jnp.broadcast_to(norms, (block, 128)).T[:1]


def decoder_norms(dec):
    latents = dec.shape[0]
    return kernel_call(
        functools.partial(norms_body, 256),
        [held(dec)],
        [IN_VMEM],
        [float_array(latents, 1), float_array(1, latents)],
    )


def codes(scaled):
    decay = jnp.exp2(-jnp.abs(scaled))
    small = decay * (LOG2E - (0.5 * LOG2E) * decay)
    soft = jnp.maximum(scaled, 0.0) + jnp.where(decay < 1e-3, small, jnp.log2(1.0 + decay))
    slope = jnp.exp2(scaled - soft)
    return soft * (1.0 / (sharpness * LOG2E)), slope.astype(jnp.bfloat16)


def norm_scale(energy_ref, entries):
    return lax.rsqrt(jnp.sum(energy_ref[...], axis=1, keepdims=True) / entries + epsilon)


def add_body(a_ref, b_ref, sum_ref):
    sum_ref[...] = a_ref[...] + b_ref[...]


def add(a, b):
    return kernel_call(add_body, [a, b], [IN_VMEM] * 2, [float_array(*a.shape)], limit=4)[0]


def join_body(*refs):
    join(refs[:-1], refs[-1])


def joined(*pieces):
    count = sum(piece.shape[0] for piece in pieces)
    out = [half_array(count, pieces[0].shape[1])]
    return kernel_call(join_body, pieces, [IN_VMEM] * len(pieces), out, limit=4)[0]


def add_split_body(a_ref, b_ref, keep_ref, send_ref):
    half = keep_ref.shape[0]
    keep_ref[...] = a_ref[:half] + b_ref[:half].astype(jnp.float32)
    send_ref[...] = (a_ref[half:] + b_ref[half:].astype(jnp.float32)).astype(jnp.bfloat16)


def add_split(a, b):
    half, width = a.shape[0] // 2, a.shape[1]
    outs = [float_array(half, width), half_array(half, width)]
    return kernel_call(add_split_body, [a, b], [IN_VMEM] * 2, outs, limit=4)


def residual_body(entries, a_ref, b_ref, bias_ref, heads_ref, energy_ref, rebuilt_ref, residual_ref):
    rebuilt = a_ref[...] + b_ref[...].astype(jnp.float32) + bias_ref[...]
    inputs = (heads_ref[...].astype(jnp.float32) * norm_scale(energy_ref, entries)).astype(jnp.bfloat16)
    rebuilt_ref[...] = rebuilt.astype(jnp.bfloat16)
    residual_ref[...] = (rebuilt - inputs.astype(jnp.float32)).astype(jnp.bfloat16)


def own_residual(entries, *args):
    shape = args[0].shape
    body = functools.partial(residual_body, entries)
    return kernel_call(body, args, [IN_VMEM] * 5, [half_array(*shape), half_array(*shape)], limit=4)


def own_columns(x, own_ref, columns):
    return x[:, pl.ds(pl.multiple_of(own_ref[0] * columns, 128), columns)]


def join(pieces, rows):
    start = 0
    for piece in pieces:
        rows[start : start + piece.shape[0]] = piece[...]
        start += piece.shape[0]


def encode_body(count, tile, entries, energy_ref, own_ref, enc_ref, bias_ref, *refs):
    pieces, (codes_ref, slope_ref, part_ref), (rows, *rest) = refs[:count], refs[count : count + 3], refs[count + 3 :]
    if rest:
        dec_hbm, keep_ref, send_ref, dec_ref, rows, coded_ref, sems = rows, *rest
        parts = sems.shape[0]
        size = dec_hbm.shape[0] // parts
        copies = []
        for part in range(parts):
            here = pl.ds(part * size, size)
            copies.append(pltpu.make_async_copy(dec_hbm.at[here], dec_ref.at[here], sems.at[part]))
        for copy in copies:
            copy.start()
    join(pieces, rows)
    factor = sharpness * LOG2E
    scale = norm_scale(energy_ref, entries) * factor
    for first in range(0, enc_ref.shape[1], tile):
        here = slice(first, first + tile)
        product = jnp.dot(rows[...], enc_ref[:, here], preferred_element_type=jnp.float32)
        coded, slope = codes(product * scale + bias_ref[:, here] * factor)
        codes_ref[here, :] = coded.T.astype(jnp.bfloat16)
        slope_ref[:, here] = slope
        if rest:
            coded_ref[:, here] = coded.astype(jnp.bfloat16)
    part = own_columns(rows, own_ref, part_ref.shape[0])
    part_ref[...] = part.astype(jnp.float32).T.astype(jnp.bfloat16)
    if rest:
        half = keep_ref.shape[0]
        for copy in copies:
            copy.wait()
        for first in range(0, dec_ref.shape[1], tile):
            here = slice(first, first + tile)
            total = jnp.dot(coded_ref[...], dec_ref[:, here], preferred_element_type=jnp.float32)
            keep_ref[:, here] = total[:half]
            send_ref[:, here] = total[half:]


def encode(entries, energy, own, enc, bias, pieces, columns):
    width, latents = enc.shape
    count = sum(piece.shape[0] for piece in pieces)
    return kernel_call(
        functools.partial(encode_body, len(pieces), min(512, latents), entries),
        [energy, own, held(enc), bias, *pieces],
        [IN_VMEM, IN_SMEM] + [IN_VMEM] * (2 + len(pieces)),
        [half_array(latents, count), half_array(count, latents), half_array(columns, count)],
        [pltpu.VMEM((count, width), jnp.bfloat16)],
        flops=2 * count * width * latents,
    )


def rebuild_body(count, tile, entries, energy_ref, own_ref, enc_ref, bias_ref, dec_hbm, *refs):
    pieces, outs, scratch = refs[:count], refs[count : count + 6], refs[count + 6 :]
    encode_body(
        count, tile, entries, energy_ref, own_ref, enc_ref, bias_ref, *pieces, *outs[:3], dec_hbm, *outs[3:], *scratch
    )


def encode_and_rebuild(entries, energy, own, enc, bias, dec, pieces, columns):
    width, latents = enc.shape
    count = sum(piece.shape[0] for piece in pieces)
    return kernel_call(
        functools.partial(rebuild_body, len(pieces), min(512, latents), entries),
        [energy, own, held(enc), bias, pltpu.with_memory_space_constraint(dec, pltpu.HBM), *pieces],
        [IN_VMEM, IN_SMEM, IN_VMEM, IN_VMEM, IN_HBM] + [IN_VMEM] * len(pieces),
        [
            half_array(latents, count),
            half_array(count, latents),
            half_array(columns, count),
            float_array(count // 2, width),
            float_array(count // 2, width),
            pltpu.VMEM(dec.shape, dec.dtype),
        ],
        [
            pltpu.VMEM((count, width), jnp.bfloat16),
            pltpu.VMEM((count, latents), jnp.bfloat16),
            pltpu.SemaphoreType.DMA((8,)),
        ],
        flops=4 * count * width * latents,
    )


def slope_body(count, tile, all_rows, own_ref, dec_ref, norms_ref, slope_ref, *refs):
    pieces, (grad_ref, part_ref, rows) = refs[:count], refs[count:]
    join(pieces, rows)
    for first in range(0, dec_ref.shape[0], tile):
        here = slice(first, first + tile)
        product = lax.dot_general(
            rows[...], dec_ref[here, :], (((1,), (1,)), ((), ())), preferred_element_type=jnp.float32
        )
        grad = product * (2.0 / all_rows) + norms_ref[:, here] * (sparsity_weight / all_rows)
        grad_ref[:, here] = (grad * slope_ref[:, here].astype(jnp.float32)).astype(jnp.bfloat16)
    part_ref[...] = own_columns(rows, own_ref, part_ref.shape[1])


def pre_gradient(all_rows, own, dec, norms, slope, pieces, columns):
    latents, width = dec.shape
    count = sum(piece.shape[0] for piece in pieces)
    return kernel_call(
        functools.partial(slope_body, len(pieces), min(512, latents), all_rows),
        [own, held(dec), norms, slope, *pieces],
        [IN_SMEM] + [IN_VMEM] * (3 + len(pieces)),
        [half_array(count, latents), half_array(count, columns)],
        [pltpu.VMEM((count, width), jnp.bfloat16)],
        flops=2 * count * width * latents,
    )


def weight_body(groups, tile, all_rows, entries, energy_ref, own_ref, norms_ref, dec_ref, *refs):
    rows, grads, coded, residual = (refs[i * groups : (i + 1) * groups] for i in range(4))
    enc_out, dec_out, enc_buffer, dec_buffer, sems = refs[4 * groups :]
    columns = dec_buffer.shape[2]
    steps = dec_ref.shape[0] // tile
    scale = norm_scale(energy_ref, entries)

    def copies(step):
        slot, here = step % 2, pl.ds(step * tile, tile)
        return (
            pltpu.make_async_copy(enc_buffer.at[slot], enc_out.at[:, here], sems.at[slot, 0]),
            pltpu.make_async_copy(dec_buffer.at[slot], dec_out.at[here], sems.at[slot, 1]),
        )

    for step in range(steps):
        if step >= 2:
            for copy in copies(step - 2):
                copy.wait()
        here = slice(step * tile, (step + 1) * tile)
        enc, dec, sums = 0.0, 0.0, 0.0
        for g in range(groups):
            enc = enc + jnp.dot(rows[g][...], grads[g][:, here], preferred_element_type=jnp.float32)
            dec = dec + jnp.dot(coded[g][here, :], residual[g][...], preferred_element_type=jnp.float32)
            sums = sums + jnp.sum(coded[g][here, :].astype(jnp.float32), axis=1, keepdims=True)
        enc_buffer[step % 2] = enc * scale
        part = own_columns(dec_ref.at[here, :], own_ref, columns).astype(jnp.float32)
        factor = sums / norms_ref[here, :] * (sparsity_weight / all_rows)
        dec_buffer[step % 2] = dec * (2.0 / all_rows) + factor * part
        for copy in copies(step):
            copy.start()
    for step in range(max(steps - 2, 0), steps):
        for copy in copies(step):
            copy.wait()


def weight_gradients(all_rows, entries, energy, own, norms, dec, rows, grads, coded, residual):
    columns = rows[0].shape[0]
    latents = dec.shape[0]
    count = sum(x.shape[0] for x in grads)
    tile = min(512, latents)
    args = [norms, held(dec), *rows, *grads, *coded, *residual]
    return kernel_call(
        functools.partial(weight_body, len(rows), tile, all_rows, entries),
        [energy, own, *args],
        [IN_VMEM, IN_SMEM] + [IN_VMEM] * len(args),
        [pltpu.HBM((columns, latents), jnp.float32), pltpu.HBM((latents, columns), jnp.float32)],
        [
            pltpu.VMEM((2, columns, tile), jnp.float32),
            pltpu.VMEM((2, tile, columns), jnp.float32),
            pltpu.SemaphoreType.DMA((2, 2)),
        ],
        [IN_HBM, IN_HBM],
        flops=4 * count * columns * latents,
    )


def bits(size):
    found, bit = [], 1
    while bit < size:
        found.append(bit)
        bit *= 2
    return found


def swap(x, even, odd=None):
    count = lax.axis_size("dp") * lax.axis_size("latent")
    odd = even if odd is None else odd
    return lax.ppermute(
        x, ("dp", "latent"), [(i, i ^ (odd if i & 1 else even)) for i in range(count)]
    )


def line_steps():
    steps = bits(lax.axis_size("latent"))[1:]
    return list(zip(steps[::-1], steps, strict=True))


def plane_steps():
    latent_size = lax.axis_size("latent")
    steps = [bit * latent_size for bit in bits(lax.axis_size("dp"))]
    return list(zip(steps, steps[::-1], strict=True))


def after(value, *done):
    return lax.optimization_barrier((value, *done))[0]


def after(value, *done):
    return lax.optimization_barrier((value, *done))[0]


def send_body(group_bits, own_ref, shuffle_ref, rows_ref, *outs):
    count, width = rows_ref.shape
    per_peer = outs[0].shape[0]
    goes_to = lax.shift_right_logical(shuffle_ref[...], group_bits) ^ own_ref[0]
    slot = shuffle_ref[...] & (count - 1)
    over_lanes = (((1,), (1,)), ((), ()))
    sublane = lax.broadcasted_iota(jnp.int32, (count, count), 0)
    lane = lax.broadcasted_iota(jnp.int32, (count, count), 1)
    peer_row = jnp.broadcast_to(goes_to, (count, count)).astype(jnp.float32)
    one_hot = (sublane == lane).astype(jnp.bfloat16)
    peer_column = lax.dot_general(
        one_hot, peer_row.astype(jnp.bfloat16), over_lanes, preferred_element_type=jnp.float32
    )
    before = (peer_column == peer_row) & (sublane < lane)
    rank = jnp.sum(before.astype(jnp.float32), axis=0, keepdims=True)
    order = goes_to.astype(jnp.float32) * per_peer + rank
    pick = (order == sublane.astype(jnp.float32)).astype(jnp.bfloat16)
    rows = jnp.dot(pick, rows_ref[...], preferred_element_type=jnp.float32)
    slot_rows = jnp.broadcast_to(slot, (128, count)).astype(jnp.float32).astype(jnp.bfloat16)
    slots = lax.dot_general(pick, slot_rows, over_lanes, preferred_element_type=jnp.float32)
    for peer, out in enumerate(outs):
        here = slice(peer * per_peer, (peer + 1) * per_peer)
        out[:, :width] = rows[here]
        out[:, width:] = slots[here]


def place_body(*refs):
    *pieces, out_ref, rows = refs
    join(pieces, rows)
    width = out_ref.shape[1]
    index = lax.broadcasted_iota(jnp.int32, (rows.shape[0], rows.shape[0]), 1).astype(jnp.float32)
    pick = (rows[:, width : width + 1] == index).astype(jnp.bfloat16)
    out_ref[...] = lax.dot_general(
        pick, rows[:, :width].astype(jnp.bfloat16), (((0,), (0,)), ((), ())), preferred_element_type=jnp.float32
    ).astype(jnp.bfloat16)


def send_rows(own, rows, shuffle):
    data_size = lax.axis_size("dp")
    latent_size = lax.axis_size("latent")
    count, width = rows.shape
    out = float_array(count // data_size, width + 128)
    body = functools.partial(send_body, len(bits(count * latent_size)))
    specs = [IN_SMEM, IN_VMEM, IN_VMEM]
    sent = kernel_call(body, [own, shuffle, rows], specs, [out] * data_size, limit=4)
    return [swap(x, peer * latent_size) if peer else x for peer, x in enumerate(sent)]


def place_rows(arrived, count, width):
    scratch = [pltpu.VMEM((count, width + 128), jnp.float32)]
    specs = [IN_VMEM] * len(arrived)
    return kernel_call(place_body, arrived, specs, [half_array(count, width)], scratch, limit=4)[0]


def shards(
    queries,
    cache_keys,
    cache_values,
    positions,
    shuffle,
    enc_weight,
    enc_bias,
    dec_weight,
    dec_bias,
):
    rows_here = queries.shape[0]
    att_width = queries.shape[1]
    data_size = lax.axis_size("dp")
    latent_size = lax.axis_size("latent")
    all_rows = rows_here * data_size * latent_size
    columns = att_width // data_size
    entries = all_rows * att_width
    core = (1, 1)
    line, plane = line_steps(), plane_steps()
    own = lax.axis_index("dp").astype(jnp.int32).reshape(1)
    bias, out_bias, places, own = lax.optimization_barrier(
        (enc_bias[None, :], dec_bias[None, :], shuffle[None, :], own)
    )
    heads_out, energy, enc = attend(queries, cache_keys, cache_values, positions, after(enc_weight, bias, out_bias, places, own))

    small_steps = plane + [core] + line
    rows = heads_out
    for number, mask in enumerate(line):
        arrived = swap(rows, *mask)
        count = len(plane) if number == 0 else 1
        if number == len(line) - 1:
            count = len(small_steps)
        for small in small_steps[:count]:
            energy = add(energy, swap(energy, *small))
        small_steps = small_steps[count:]
        rows = joined(rows, after(arrived, energy))

    pieces = [rows, swap(rows, *plane[0])]
    group = [rows, swap(rows, *core)]
    *first_set, keep, send, dec = encode_and_rebuild(entries, energy, own, enc, bias, dec_weight, group, columns)
    encoded = [first_set]

    def cut(part, largest=512):
        return [part[i : i + largest] for i in range(0, part.shape[0], largest)]

    def encode_next(parts, now):
        parts = [after(part, now) for part in parts]
        encoded.append(encode(entries, energy, own, enc, bias, parts, columns))
        return encoded[-1][0]

    total, sent = add_split(keep, swap(send, *core))
    for number, mask in enumerate(line[::-1]):
        arrived = swap(sent, *mask)
        if number == 0:
            for step in plane[1:]:
                pieces = [after(piece, sent) for piece in pieces]
                pieces.append(swap(joined(*pieces), *step))
            second = [pieces[1], swap(pieces[1], *core)]
        if number == len(line) - 1:
            arrived = after(arrived, encode_next(second, sent))
        else:
            total, sent = add_split(total, arrived)
    rebuilt_own, residual_own = own_residual(entries, total, arrived, out_bias, heads_out, energy)

    rows = residual_own
    for number, mask in enumerate(line):
        arrived = swap(rows, *mask)
        if number == 0:
            norms_column, norms_row = decoder_norms(after(dec, rows))
            arrived = after(arrived, norms_row)
            far = [after(piece, rows) for piece in pieces[2:]]
            far = [part for piece in far for part in (piece, swap(piece, *core))]
        if number == len(line) - 1:
            done = [encode_next([part], rows) for piece in far for part in cut(piece)]
            arrived = after(arrived, *done)
        rows = joined(rows, arrived)
    grads = []

    def pre(parts, now):
        slope = encoded[len(grads)][1]
        parts = [after(part, now) for part in parts]
        grads.append(pre_gradient(all_rows, own, dec, norms_row, slope, parts, columns))
        return grads[-1][0]

    group = [rows, swap(rows, *core)]
    pieces = [rows]
    for number, mask in enumerate(plane):
        sent = pieces[0] if number == 0 else joined(*pieces)
        arrived = swap(sent, *mask)
        if number == 0:
            moved = send_rows(own, after(rebuilt_own, sent), places)
            arrived = after(arrived, pre(group, sent))
        elif number == 1:
            arrived = after(arrived, pre([pieces[1], swap(pieces[1], *core)], sent))
        pieces.append(arrived)
    far = [part for piece in pieces[2:] for part in (piece, swap(piece, *core))]
    for piece in far:
        for part in cut(piece):
            last = pre([part], pieces[-1])
    moved = [after(part, last) for part in moved]
    rebuilt = place_rows(moved, rows_here, att_width)
    grad_enc, grad_dec = weight_gradients(
        all_rows,
        entries,
        energy,
        own,
        norms_column,
        dec,
        [x[2] for x in encoded],
        [x[0] for x in grads],
        [x[0] for x in encoded],
        [x[1] for x in grads],
    )
    return (rebuilt, grad_enc, grad_dec)


def solution(mesh):
    in_specs = (
        P(("dp", "latent"), None),
        P(("dp", "latent"), None, None),
        P(("dp", "latent"), None, None),
        P(("dp", "latent")),
        P(("dp", "latent")),
        P(None, "latent"),
        P("latent"),
        P("latent", None),
        P(),
    )
    out_specs = (P(("dp", "latent"), None), P("dp", "latent"), P("latent", "dp"))
    return jax.shard_map(shards, mesh=mesh, in_specs=in_specs, out_specs=out_specs, check_vma=False)
```

time: 351 us -> 122 us (0.35)
  waiting for transfers between devices: 243 us -> 53.2 us
  Pallas kernels: 0 us -> 44.5 us
  matrix products: 36.3 us -> 0 us
  other arithmetic: 24.4 us -> 0 us
  between operations: 14.6 us -> 1.06 us
  starting transfers between devices: 9.66 us -> 22.3 us
  local copies, waits for them, and re-layouts: 11.5 us -> 0.67 us
  blocking collectives: 10.4 us -> 0 us
    reduce_scatter x2 -> x0, waiting for transfers between devices: 162 us -> none  [the longest x1 85.5 us: shards(): lax.psum_scatter(dec_term.astype(jnp.bfloat16), 'dp', scatter_dimension=1...]
    psum x1 -> x0, waiting for transfers between devices: 57.3 us -> none  [shards(): summed = lax.psum(partial_value, 'latent')]
    ppermute x0 -> x25, waiting for transfers between devices: none -> 53.2 us  [swap(): lax.ppermute(x, ('dp', 'latent'), [(i, i ^ (odd if i & 1 else even)) for...]
    pallas_call x0 -> x27, Pallas kernels: none -> 44.5 us  [kernel_call(): pl.pallas_call(body, in_specs=specs, out_specs=out_specs or [IN_VMEM] * l...]
    dot_general x7 -> x0, matrix products: 36.3 us -> none  [the longest x1 8.74 us: shards(): jnp.dot(inputs, enc_weight, preferred_element_type=jnp.float32)]
    ppermute x0 -> x25, starting transfers between devices: none -> 22.3 us  [swap(): lax.ppermute(x, ('dp', 'latent'), [(i, i ^ (odd if i & 1 else even)) for...]
    all_gather x1 -> x0, waiting for transfers between devices: 21.9 us -> none  [shards(): gathered = lax.all_gather(arrived, 'latent', axis=0, tiled=True)]
    convert_element_type x3 -> x0, other arithmetic: 10.6 us -> none  [the longest x1 4.2 us: shards(): grad_dec = lax.psum_scatter(dec_term.astype(jnp.bfloat16), 'dp', scatter_...]
  transfers between devices with their start and end apart: 6 -> 25, of which waited for: 5 -> 16; matrix products, arithmetic and copies ran while one was open for 8% -> 0% of each run, Pallas kernels for 0% -> 20%
where the time goes in v2:
time: 122 us
  waiting for transfers between devices  53.2 us (44%)
  Pallas kernels  44.5 us (36%)
  starting transfers between devices  22.3 us (18%)
    ppermute x25, waiting for transfers between devices, swap(): lax.ppermute(x, ('dp', 'latent'), [(i, i ^ (odd if i & 1 else even)) for...  53.2 us
    pallas_call x27, Pallas kernels, kernel_call(): pl.pallas_call(body, in_specs=specs, out_specs=out_specs or [IN_VMEM] * l...  44.5 us
    ppermute x25, starting transfers between devices, swap(): lax.ppermute(x, ('dp', 'latent'), [(i, i ^ (odd if i & 1 else even)) for...  22.3 us
  transfers between devices with their start and end apart: 25, of which 16 were waited for; matrix products, arithmetic and copies ran while one was open for 0% of the time, Pallas kernels for 20%

profile of v2, /device:TPU:0, one launch (start us, length us, event | category | flops | bytes accessed | tf_op | source)
XLA Modules:
  0.0 121.7 jit_solution(18259455973840472782)
XLA Ops:
  1.3 4.8 %shard_map.112 = (bf16[32,2048]{1,0:T(8,128)(2,1)S(1)}, f32[1,128]{1,0:T(1,128)S(1)}, bf16[2048,2048]{1,0:T(8,128)(2,1)S(1)}) custom-call(s32[32]{0:T(128)S(1)} %copy-done.2, bf16[32,2048]{1,0:T(8,128)(2,1)} %queries.1, bf16[1,512,1024]{2,1,0:T(8,128)(2,1)} %keys.1, bf16[1,512,1024]{2,1,0:T(8,128)(2,1)} %values.1, bf16[2048,2048]{1,0:T(8,128)(2,1)} %enc), custom_call_target="tpu_custom_call" | custom-call | flops 134217728 | tf_op jit(solution)/shard_map/pallas_call | solution.py:25
  6.1 4.1 %collective-permute-start.5 = (bf16[32,2048]{1,0:T(8,128)(2,1)S(1)}, bf16[32,2048]{1,0:T(8,128)(2,1)S(1)}, u32[]{:S(2)}, u32[]{:S(2)}) collective-permute-start(bf16[32,2048]{1,0:T(8,128)(2,1)S(1)} %get-tuple-element.81.refs_0_.heads_ref), channel_id=1, source_target_pairs={{0,4},{1,3},{2,6},{3,1},{4,0},{5,7},{6,2},{7,5},{8,12},{9,11},{10,... | collective-permute-start | bytes 393224 | tf_op jit(solution)/shard_map/ppermute | solution.py:376
  10.2 1.5 %collective-permute-start = (f32[1,128]{1,0:T(1,128)S(1)}, f32[1,128]{1,0:T(1,128)S(1)}, u32[]{:S(2)}, u32[]{:S(2)}) collective-permute-start(f32[1,128]{1,0:T(1,128)S(1)} %get-tuple-element.79.a_ref), channel_id=1, source_target_pairs={{0,8},{1,17},{2,10},{3,19},{4,12},{5,21},{6,14},{7,23},{8,0},{9,25... | collective-permute-start | bytes 1544 | tf_op jit(solution)/shard_map/ppermute | solution.py:376
  11.7 2.0 %collective-permute-done.b_ref = f32[1,128]{1,0:T(1,128)S(1)} collective-permute-done((f32[1,128]{1,0:T(1,128)S(1)}, f32[1,128]{1,0:T(1,128)S(1)}, u32[]{:S(2)}, u32[]{:S(2)}) %collective-permute-start) | collective-permute-done | bytes 544 | tf_op jit(solution)/shard_map/ppermute | solution.py:376
  13.8 1.5 %collective-permute-start.1 = (f32[1,128]{1,0:T(1,128)S(1)}, f32[1,128]{1,0:T(1,128)S(1)}, u32[]{:S(2)}, u32[]{:S(2)}) collective-permute-start(f32[1,128]{1,0:T(1,128)S(1)} %shard_map.113.a_ref), channel_id=1, source_target_pairs={{0,16},{1,9},{2,18},{3,11},{4,20},{5,13},{6,22},{7,15},{8,24},{9,1... | collective-permute-start | bytes 1544 | tf_op jit(solution)/shard_map/ppermute | solution.py:376
  15.3 2.0 %collective-permute-done.1.b_ref = f32[1,128]{1,0:T(1,128)S(1)} collective-permute-done((f32[1,128]{1,0:T(1,128)S(1)}, f32[1,128]{1,0:T(1,128)S(1)}, u32[]{:S(2)}, u32[]{:S(2)}) %collective-permute-start.1) | collective-permute-done | bytes 544 | tf_op jit(solution)/shard_map/ppermute | solution.py:376
  17.3 1.6 %collective-permute-start.6 = (bf16[64,2048]{1,0:T(8,128)(2,1)S(1)}, bf16[64,2048]{1,0:T(8,128)(2,1)S(1)}, u32[]{:S(2)}, u32[]{:S(2)}) collective-permute-start(bf16[64,2048]{1,0:T(8,128)(2,1)S(1)} %shard_map.118.refs_0_), channel_id=1, source_target_pairs={{0,2},{1,5},{2,0},{3,7},{4,6},{5,1},{6,4},{7,3},{8,10},{9,13},{10,... | collective-permute-start | bytes 786440 | tf_op jit(solution)/shard_map/ppermute | solution.py:376
  20.4 4.1 %collective-permute-done.3.b_ref = f32[1,128]{1,0:T(1,128)S(1)} collective-permute-done((f32[1,128]{1,0:T(1,128)S(1)}, f32[1,128]{1,0:T(1,128)S(1)}, u32[]{:S(2)}, u32[]{:S(2)}) %collective-permute-start.3) | collective-permute-done | bytes 544 | tf_op jit(solution)/shard_map/ppermute | solution.py:376
  25.0 3.1 %collective-permute-done.4.b_ref = f32[1,128]{1,0:T(1,128)S(1)} collective-permute-done((f32[1,128]{1,0:T(1,128)S(1)}, f32[1,128]{1,0:T(1,128)S(1)}, u32[]{:S(2)}, u32[]{:S(2)}) %collective-permute-start.4) | collective-permute-done | bytes 544 | tf_op jit(solution)/shard_map/ppermute | solution.py:376
  28.2 1.9 %collective-permute-done.7.refs_1_ = bf16[128,2048]{1,0:T(8,128)(2,1)S(1)} collective-permute-done((bf16[128,2048]{1,0:T(8,128)(2,1)S(1)}, bf16[128,2048]{1,0:T(8,128)(2,1)S(1)}, u32[]{:S(2)}, u32[]{:S(2)}) %collective-permute-start.7) | collective-permute-done | bytes 524320 | tf_op jit(solution)/shard_map/ppermute | solution.py:376
  30.1 8.1 %shard_map.120 = (bf16[2048,256]{1,0:T(8,128)(2,1)S(1)}, bf16[256,2048]{1,0:T(8,128)(2,1)S(1)}, bf16[512,256]{1,0:T(8,128)(2,1)S(1)}, f32[128,2048]{1,0:T(8,128)...) custom-call(f32[1,128]{1,0:T(1,128)S(1)} %shard_map.117.energy_ref, s32[1]{0:T(128)} %bitcast.3.own_ref, ...), custom_call_target="tpu_custom_call" | custom-call | flops 4294967296 | tf_op jit(solution)/shard_map/pallas_call | solution.py:25
  41.1 6.5 %collective-permute-done.11.refs_0_.refs_1_ = bf16[128,2048]{1,0:T(8,128)(2,1)S(1)} collective-permute-done((bf16[128,2048]{1,0:T(8,128)(2,1)S(1)}, bf16[128,2048]{1,0:T(8,128)(2,1)S(1)}, u32[]{:S(2)}, u32[]{:S(2)}) %collective-permute-start.11) | collective-permute-done | bytes 524320 | tf_op jit(solution)/shard_map/ppermute | solution.py:376
  47.7 1.6 %collective-permute-start.15 = (bf16[256,2048]{1,0:T(8,128)(2,1)S(1)}, bf16[256,2048]{1,0:T(8,128)(2,1)S(1)}, u32[]{:S(2)}, u32[]{:S(2)}) collective-permute-start(bf16[256,2048]{1,0:T(8,128)(2,1)S(1)} %shard_map.127), channel_id=1, source_target_pairs={{0,16},{1,9},{2,18},{3,11},{4,20},{5,13},{6,22},{7,15},{8,24},{9,1... | collective-permute-start | bytes 3145736 | tf_op jit(solution)/shard_map/ppermute | solution.py:376
  49.8 7.6 %collective-permute-done.9.b_ref = bf16[64,2048]{1,0:T(8,128)(2,1)S(1)} collective-permute-done((bf16[64,2048]{1,0:T(8,128)(2,1)S(1)}, bf16[64,2048]{1,0:T(8,128)(2,1)S(1)}, u32[]{:S(2)}, u32[]{:S(2)}) %collective-permute-start.9) | collective-permute-done | bytes 262176 | tf_op jit(solution)/shard_map/ppermute | solution.py:376
  57.5 2.0 %collective-permute-start.10 = (bf16[32,2048]{1,0:T(8,128)(2,1)S(1)}, bf16[32,2048]{1,0:T(8,128)(2,1)S(1)}, u32[]{:S(2)}, u32[]{:S(2)}) collective-permute-start(bf16[32,2048]{1,0:T(8,128)(2,1)S(1)} %get-tuple-element.89), channel_id=1, source_target_pairs={{0,4},{1,3},{2,6},{3,1},{4,0},{5,7},{6,2},{7,5},{8,12},{9,11},{10,... | collective-permute-start | bytes 393224 | tf_op jit(solution)/shard_map/ppermute | solution.py:376
  59.5 3.6 %shard_map.123 = (bf16[2048,256]{1,0:T(8,128)(2,1)S(1)}, bf16[256,2048]{1,0:T(8,128)(2,1)S(1)}, bf16[512,256]{1,0:T(8,128)(2,1)S(1)}) custom-call(f32[1,128]{1,0:T(1,128)S(1)} %shard_map.117.energy_ref, s32[1]{0:T(128)} %bitcast.3.own_ref, bf16[2048,2048]{1,0:T(8,128)(2,1)S(1)} %get-tuple-element.80.enc_ref, f32[1,2048]{1,0:T(1,128)S(1)} %bitcast.5, ...), custom_call_target="tpu_custom_call" | custom-call | flops 2147483648 | tf_op jit(solution)/shard_map/pallas_call | solution.py:25
  63.1 1.7 %collective-permute-done.10.b_ref = bf16[32,2048]{1,0:T(8,128)(2,1)S(1)} collective-permute-done((bf16[32,2048]{1,0:T(8,128)(2,1)S(1)}, bf16[32,2048]{1,0:T(8,128)(2,1)S(1)}, u32[]{:S(2)}, u32[]{:S(2)}) %collective-permute-start.10) | collective-permute-done | bytes 131104 | tf_op jit(solution)/shard_map/ppermute | solution.py:376
  65.7 2.3 %shard_map.125 = (f32[2048,1]{1,0:T(8,128)S(1)}, f32[1,2048]{1,0:T(1,128)S(1)}) custom-call(bf16[2048,2048]{1,0:T(8,128)(2,1)S(1)} %get-tuple-element.98.dec_ref), custom_call_target="tpu_custom_call" | custom-call | tf_op jit(solution)/shard_map/pallas_call | solution.py:25
  68.0 4.2 %collective-permute-done.13.refs_1_ = bf16[32,2048]{1,0:T(8,128)(2,1)S(1)} collective-permute-done((bf16[32,2048]{1,0:T(8,128)(2,1)S(1)}, bf16[32,2048]{1,0:T(8,128)(2,1)S(1)}, u32[]{:S(2)}, u32[]{:S(2)}) %collective-permute-start.13) | collective-permute-done | bytes 131104 | tf_op jit(solution)/shard_map/ppermute | solution.py:376
  72.3 3.6 %shard_map.128 = (bf16[2048,256]{1,0:T(8,128)(2,1)S(1)}, bf16[256,2048]{1,0:T(8,128)(2,1)S(1)}, bf16[512,256]{1,0:T(8,128)(2,1)S(1)}) custom-call(f32[1,128]{1,0:T(1,128)S(1)} %shard_map.117.energy_ref, s32[1]{0:T(128)} %bitcast.3.own_ref, bf16[2048,2048]{1,0:T(8,128)(2,1)S(1)} %get-tuple-element.80.enc_ref, f32[1,2048]{1,0:T(1,128)S(1)} %bitcast.6, ...), custom_call_target="tpu_custom_call" | custom-call | flops 2147483648 | tf_op jit(solution)/shard_map/pallas_call | solution.py:25
  76.0 3.6 %shard_map.129 = (bf16[2048,256]{1,0:T(8,128)(2,1)S(1)}, bf16[256,2048]{1,0:T(8,128)(2,1)S(1)}, bf16[512,256]{1,0:T(8,128)(2,1)S(1)}) custom-call(f32[1,128]{1,0:T(1,128)S(1)} %shard_map.117.energy_ref, s32[1]{0:T(128)} %bitcast.3.own_ref, bf16[2048,2048]{1,0:T(8,128)(2,1)S(1)} %get-tuple-element.80.enc_ref, f32[1,2048]{1,0:T(1,128)S(1)} %bitcast.7, ...), custom_call_target="tpu_custom_call" | custom-call | flops 2147483648 | tf_op jit(solution)/shard_map/pallas_call | solution.py:25
  80.8 1.6 %collective-permute-start.17 = (bf16[128,2048]{1,0:T(8,128)(2,1)S(1)}, bf16[128,2048]{1,0:T(8,128)(2,1)S(1)}, u32[]{:S(2)}, u32[]{:S(2)}) collective-permute-start(bf16[128,2048]{1,0:T(8,128)(2,1)S(1)} %shard_map.130.refs_0_), channel_id=1, source_target_pairs={{0,8},{1,17},{2,10},{3,19},{4,12},{5,21},{6,14},{7,23},{8,0},{9,25... | collective-permute-start | bytes 1572872 | tf_op jit(solution)/shard_map/ppermute | solution.py:376
  82.7 2.5 %shard_map.132 = (bf16[256,2048]{1,0:T(8,128)(2,1)S(1)}, bf16[256,512]{1,0:T(8,128)(2,1)S(1)}) custom-call(s32[1]{0:T(128)} %bitcast.3.own_ref, bf16[2048,2048]{1,0:T(8,128)(2,1)S(1)} %get-tuple-element.98.dec_ref, f32[1,2048]{1,0:T(1,128)S(1)} %get-tuple-element.99.norms_ref, bf16[256,2048]{1,0:T(8,128)(2,1)S(1)} %get-tuple-element.111.slope_ref, ...), custom_call_target="tpu_custom_call" | custom-call | flops 2147483648 | tf_op jit(solution)/shard_map/pallas_call | solution.py:25
  85.2 4.8 %collective-permute-done.17.refs_1_.refs_0_ = bf16[128,2048]{1,0:T(8,128)(2,1)S(1)} collective-permute-done((bf16[128,2048]{1,0:T(8,128)(2,1)S(1)}, bf16[128,2048]{1,0:T(8,128)(2,1)S(1)}, u32[]{:S(2)}, u32[]{:S(2)}) %collective-permute-start.17) | collective-permute-done | bytes 524320 | tf_op jit(solution)/shard_map/ppermute | solution.py:376
  91.0 1.5 %collective-permute-done.20.refs_1_ = bf16[128,2048]{1,0:T(8,128)(2,1)S(1)} collective-permute-done((bf16[128,2048]{1,0:T(8,128)(2,1)S(1)}, bf16[128,2048]{1,0:T(8,128)(2,1)S(1)}, u32[]{:S(2)}, u32[]{:S(2)}) %collective-permute-start.20) | collective-permute-done | bytes 524320 | tf_op jit(solution)/shard_map/ppermute | solution.py:376
  92.5 2.5 %shard_map.134 = (bf16[256,2048]{1,0:T(8,128)(2,1)S(1)}, bf16[256,512]{1,0:T(8,128)(2,1)S(1)}) custom-call(s32[1]{0:T(128)} %bitcast.3.own_ref, bf16[2048,2048]{1,0:T(8,128)(2,1)S(1)} %get-tuple-element.98.dec_ref, f32[1,2048]{1,0:T(1,128)S(1)} %get-tuple-element.99.norms_ref, bf16[256,2048]{1,0:T(8,128)(2,1)S(1)} %get-tuple-element.116.slope_ref, ...), custom_call_target="tpu_custom_call" | custom-call | flops 2147483648 | tf_op jit(solution)/shard_map/pallas_call | solution.py:25
  95.0 10.0 %collective-permute-done.19.refs_0_ = bf16[256,2048]{1,0:T(8,128)(2,1)S(1)} collective-permute-done((bf16[256,2048]{1,0:T(8,128)(2,1)S(1)}, bf16[256,2048]{1,0:T(8,128)(2,1)S(1)}, u32[]{:S(2)}, u32[]{:S(2)}) %collective-permute-start.19) | collective-permute-done | bytes 1048608 | tf_op jit(solution)/shard_map/ppermute | solution.py:376
  105.3 1.5 %collective-permute-start.24 = (f32[8,2176]{1,0:T(8,128)S(1)}, f32[8,2176]{1,0:T(8,128)S(1)}, u32[]{:S(2)}, u32[]{:S(2)}) collective-permute-start(f32[8,2176]{1,0:T(8,128)S(1)} %get-tuple-element.128), channel_id=1, source_target_pairs={{0,24},{1,25},{2,26},{3,27},{4,28},{5,29},{6,30},{7,31},{8,16},{9,... | collective-permute-start | bytes 208904 | tf_op jit(solution)/shard_map/ppermute | solution.py:376
  106.8 1.5 %collective-permute-start.23 = (f32[8,2176]{1,0:T(8,128)S(1)}, f32[8,2176]{1,0:T(8,128)S(1)}, u32[]{:S(2)}, u32[]{:S(2)}) collective-permute-start(f32[8,2176]{1,0:T(8,128)S(1)} %get-tuple-element.126), channel_id=1, source_target_pairs={{0,16},{1,17},{2,18},{3,19},{4,20},{5,21},{6,22},{7,23},{8,24},{9,... | collective-permute-start | bytes 208904 | tf_op jit(solution)/shard_map/ppermute | solution.py:376
  108.9 2.7 %shard_map.137 = (bf16[256,2048]{1,0:T(8,128)(2,1)S(1)}, bf16[256,512]{1,0:T(8,128)(2,1)S(1)}) custom-call(s32[1]{0:T(128)} %bitcast.3.own_ref, bf16[2048,2048]{1,0:T(8,128)(2,1)S(1)} %get-tuple-element.98.dec_ref, f32[1,2048]{1,0:T(1,128)S(1)} %get-tuple-element.99.norms_ref, bf16[256,2048]{1,0:T(8,128)(2,1)S(1)} %get-tuple-element.135.slope_ref, ...), custom_call_target="tpu_custom_call" | custom-call | flops 2147483648 | tf_op jit(solution)/shard_map/pallas_call | solution.py:25
  111.6 2.5 %shard_map.135 = (bf16[256,2048]{1,0:T(8,128)(2,1)S(1)}, bf16[256,512]{1,0:T(8,128)(2,1)S(1)}) custom-call(s32[1]{0:T(128)} %bitcast.3.own_ref, bf16[2048,2048]{1,0:T(8,128)(2,1)S(1)} %get-tuple-element.98.dec_ref, f32[1,2048]{1,0:T(1,128)S(1)} %get-tuple-element.99.norms_ref, bf16[256,2048]{1,0:T(8,128)(2,1)S(1)} %get-tuple-element.110.slope_ref, ...), custom_call_target="tpu_custom_call" | custom-call | flops 2147483648 | tf_op jit(solution)/shard_map/pallas_call | solution.py:25
  115.1 6.4 %shard_map.138 = (f32[512,2048]{1,0:T(8,128)}, f32[2048,512]{1,0:T(8,128)}) custom-call(f32[1,128]{1,0:T(1,128)S(1)} %shard_map.117.energy_ref, s32[1]{0:T(128)} %bitcast.3.own_ref, f32[2048,1]{1,0:T(8,128)S(1)} %get-tuple-element.130.norms_ref, bf16[2048,2048]{1,0:T(8,128)(2,1)S(1)} %get-tuple-element.98.dec_ref, ...), custom_call_target="tpu_custom_call" | custom-call | flops 4294967296 | tf_op jit(solution)/shard_map/pallas_call | solution.py:25
  (53 shorter events, 11.4 us)
Async XLA Ops:
  0.6 29.5 %copy-start = (f32[2048]{0:T(1024)S(1)}, f32[2048]{0:T(1024)}, u32[]{:S(2)}) copy-start(f32[2048]{0:T(1024)} %param.15) | copy-start | bytes 24580
  0.6 0.7 copy-start.2
  6.1 11.2 %collective-permute-start.5 = (bf16[32,2048]{1,0:T(8,128)(2,1)S(1)}, bf16[32,2048]{1,0:T(8,128)(2,1)S(1)}, u32[]{:S(2)}, u32[]{:S(2)}) collective-permute-start(bf16[32,2048]{1,0:T(8,128)(2,1)S(1)} %get-tuple-element.81.refs_0_.heads_ref), channel_id=1, source_target_pairs={{0,4},{1,3},{2,6},{3,1},{4,0},{5,7},{6,2},{7,5},{8,12},{9,11},{10,... | collective-permute-start | bytes 393224 | tf_op jit(solution)/shard_map/ppermute | solution.py:376
  10.2 3.5 %collective-permute-start = (f32[1,128]{1,0:T(1,128)S(1)}, f32[1,128]{1,0:T(1,128)S(1)}, u32[]{:S(2)}, u32[]{:S(2)}) collective-permute-start(f32[1,128]{1,0:T(1,128)S(1)} %get-tuple-element.79.a_ref), channel_id=1, source_target_pairs={{0,8},{1,17},{2,10},{3,19},{4,12},{5,21},{6,14},{7,23},{8,0},{9,25... | collective-permute-start | bytes 1544 | tf_op jit(solution)/shard_map/ppermute | solution.py:376
  13.8 3.5 %collective-permute-start.1 = (f32[1,128]{1,0:T(1,128)S(1)}, f32[1,128]{1,0:T(1,128)S(1)}, u32[]{:S(2)}, u32[]{:S(2)}) collective-permute-start(f32[1,128]{1,0:T(1,128)S(1)} %shard_map.113.a_ref), channel_id=1, source_target_pairs={{0,16},{1,9},{2,18},{3,11},{4,20},{5,13},{6,22},{7,15},{8,24},{9,1... | collective-permute-start | bytes 1544 | tf_op jit(solution)/shard_map/ppermute | solution.py:376
  17.3 10.8 %collective-permute-start.6 = (bf16[64,2048]{1,0:T(8,128)(2,1)S(1)}, bf16[64,2048]{1,0:T(8,128)(2,1)S(1)}, u32[]{:S(2)}, u32[]{:S(2)}) collective-permute-start(bf16[64,2048]{1,0:T(8,128)(2,1)S(1)} %shard_map.118.refs_0_), channel_id=1, source_target_pairs={{0,2},{1,5},{2,0},{3,7},{4,6},{5,1},{6,4},{7,3},{8,10},{9,13},{10,... | collective-permute-start | bytes 786440 | tf_op jit(solution)/shard_map/ppermute | solution.py:376
  19.0 1.1 collective-permute-start.2
  20.1 4.4 %collective-permute-start.3 = (f32[1,128]{1,0:T(1,128)S(1)}, f32[1,128]{1,0:T(1,128)S(1)}, u32[]{:S(2)}, u32[]{:S(2)}) collective-permute-start(f32[1,128]{1,0:T(1,128)S(1)} %shard_map.115.a_ref), channel_id=1, source_target_pairs={{0,4},{1,3},{2,6},{3,1},{4,0},{5,7},{6,2},{7,5},{8,12},{9,11},{10,... | collective-permute-start | bytes 1544 | tf_op jit(solution)/shard_map/ppermute | solution.py:376
  24.5 3.5 %collective-permute-start.4 = (f32[1,128]{1,0:T(1,128)S(1)}, f32[1,128]{1,0:T(1,128)S(1)}, u32[]{:S(2)}, u32[]{:S(2)}) collective-permute-start(f32[1,128]{1,0:T(1,128)S(1)} %shard_map.116.a_ref), channel_id=1, source_target_pairs={{0,2},{1,5},{2,0},{3,7},{4,6},{5,1},{6,4},{7,3},{8,10},{9,13},{10,... | collective-permute-start | bytes 1544 | tf_op jit(solution)/shard_map/ppermute | solution.py:376
  28.1 2.0 %collective-permute-start.7 = (bf16[128,2048]{1,0:T(8,128)(2,1)S(1)}, bf16[128,2048]{1,0:T(8,128)(2,1)S(1)}, u32[]{:S(2)}, u32[]{:S(2)}) collective-permute-start(bf16[128,2048]{1,0:T(8,128)(2,1)S(1)} %shard_map.119.refs_0_), channel_id=1, source_target_pairs={{0,1},{1,0},{2,3},{3,2},{4,5},{5,4},{6,7},{7,6},{8,9},{9,8},{10,11... | collective-permute-start | bytes 1572872 | tf_op jit(solution)/shard_map/ppermute | solution.py:376
  38.3 26.5 %copy-start.1 = (f32[2048]{0:T(1024)S(1)}, f32[2048]{0:T(1024)}, u32[]{:S(2)}) copy-start(f32[2048]{0:T(1024)} %param.17) | copy-start | bytes 24580
  38.3 2.7 %collective-permute-start.8 = (f32[128,2048]{1,0:T(8,128)S(1)}, f32[128,2048]{1,0:T(8,128)S(1)}, u32[]{:S(2)}, u32[]{:S(2)}) collective-permute-start(f32[128,2048]{1,0:T(8,128)S(1)} %get-tuple-element.85), channel_id=1, source_target_pairs={{0,1},{1,0},{2,3},{3,2},{4,5},{5,4},{6,7},{7,6},{8,9},{9,8},{10,11... | collective-permute-start | bytes 3145736 | tf_op jit(solution)/shard_map/ppermute | solution.py:376
  38.5 9.2 %collective-permute-start.11 = (bf16[128,2048]{1,0:T(8,128)(2,1)S(1)}, bf16[128,2048]{1,0:T(8,128)(2,1)S(1)}, u32[]{:S(2)}, u32[]{:S(2)}) collective-permute-start(bf16[128,2048]{1,0:T(8,128)(2,1)S(1)} %shard_map.119.refs_0_), channel_id=1, source_target_pairs={{0,8},{1,17},{2,10},{3,19},{4,12},{5,21},{6,14},{7,23},{8,0},{9,25... | collective-permute-start | bytes 1572872 | tf_op jit(solution)/shard_map/ppermute | solution.py:376
  47.7 17.2 %collective-permute-start.15 = (bf16[256,2048]{1,0:T(8,128)(2,1)S(1)}, bf16[256,2048]{1,0:T(8,128)(2,1)S(1)}, u32[]{:S(2)}, u32[]{:S(2)}) collective-permute-start(bf16[256,2048]{1,0:T(8,128)(2,1)S(1)} %shard_map.127), channel_id=1, source_target_pairs={{0,16},{1,9},{2,18},{3,11},{4,20},{5,13},{6,22},{7,15},{8,24},{9,1... | collective-permute-start | bytes 3145736 | tf_op jit(solution)/shard_map/ppermute | solution.py:376
  49.3 10.2 %collective-permute-start.12 = (bf16[128,2048]{1,0:T(8,128)(2,1)S(1)}, bf16[128,2048]{1,0:T(8,128)(2,1)S(1)}, u32[]{:S(2)}, u32[]{:S(2)}) collective-permute-start(bf16[128,2048]{1,0:T(8,128)(2,1)S(1)} %collective-permute-done.11.refs_0_.refs_1_), channel_id=1, source_target_pairs={{0,1},{1,0},{2,3},{3,2},{4,5},{5,4},{6,7},{7,6},{8,9},{9,8},{10,11... | collective-permute-start | bytes 1572872 | tf_op jit(solution)/shard_map/ppermute | solution.py:376
  49.3 8.1 %collective-permute-start.9 = (bf16[64,2048]{1,0:T(8,128)(2,1)S(1)}, bf16[64,2048]{1,0:T(8,128)(2,1)S(1)}, u32[]{:S(2)}, u32[]{:S(2)}) collective-permute-start(bf16[64,2048]{1,0:T(8,128)(2,1)S(1)} %get-tuple-element.87), channel_id=1, source_target_pairs={{0,2},{1,5},{2,0},{3,7},{4,6},{5,1},{6,4},{7,3},{8,10},{9,13},{10,... | collective-permute-start | bytes 786440 | tf_op jit(solution)/shard_map/ppermute | solution.py:376
  57.5 7.3 %collective-permute-start.10 = (bf16[32,2048]{1,0:T(8,128)(2,1)S(1)}, bf16[32,2048]{1,0:T(8,128)(2,1)S(1)}, u32[]{:S(2)}, u32[]{:S(2)}) collective-permute-start(bf16[32,2048]{1,0:T(8,128)(2,1)S(1)} %get-tuple-element.89), channel_id=1, source_target_pairs={{0,4},{1,3},{2,6},{3,1},{4,0},{5,7},{6,2},{7,5},{8,12},{9,11},{10,... | collective-permute-start | bytes 393224 | tf_op jit(solution)/shard_map/ppermute | solution.py:376
  64.9 11.0 %collective-permute-start.16 = (bf16[256,2048]{1,0:T(8,128)(2,1)S(1)}, bf16[256,2048]{1,0:T(8,128)(2,1)S(1)}, u32[]{:S(2)}, u32[]{:S(2)}) collective-permute-start(bf16[256,2048]{1,0:T(8,128)(2,1)S(1)} %collective-permute-done.15.refs_0_), channel_id=1, source_target_pairs={{0,1},{1,0},{2,3},{3,2},{4,5},{5,4},{6,7},{7,6},{8,9},{9,8},{10,11... | collective-permute-start | bytes 3145736 | tf_op jit(solution)/shard_map/ppermute | solution.py:376
  65.0 7.2 %collective-permute-start.13 = (bf16[32,2048]{1,0:T(8,128)(2,1)S(1)}, bf16[32,2048]{1,0:T(8,128)(2,1)S(1)}, u32[]{:S(2)}, u32[]{:S(2)}) collective-permute-start(bf16[32,2048]{1,0:T(8,128)(2,1)S(1)} %get-tuple-element.96.refs_0_), channel_id=1, source_target_pairs={{0,4},{1,3},{2,6},{3,1},{4,0},{5,7},{6,2},{7,5},{8,12},{9,11},{10,... | collective-permute-start | bytes 393224 | tf_op jit(solution)/shard_map/ppermute | solution.py:376
  72.3 8.4 %collective-permute-start.14 = (bf16[64,2048]{1,0:T(8,128)(2,1)S(1)}, bf16[64,2048]{1,0:T(8,128)(2,1)S(1)}, u32[]{:S(2)}, u32[]{:S(2)}) collective-permute-start(bf16[64,2048]{1,0:T(8,128)(2,1)S(1)} %shard_map.126.refs_0_), channel_id=1, source_target_pairs={{0,2},{1,5},{2,0},{3,7},{4,6},{5,1},{6,4},{7,3},{8,10},{9,13},{10,... | collective-permute-start | bytes 786440 | tf_op jit(solution)/shard_map/ppermute | solution.py:376
  80.7 2.0 %collective-permute-start.18 = (bf16[128,2048]{1,0:T(8,128)(2,1)S(1)}, bf16[128,2048]{1,0:T(8,128)(2,1)S(1)}, u32[]{:S(2)}, u32[]{:S(2)}) collective-permute-start(bf16[128,2048]{1,0:T(8,128)(2,1)S(1)} %shard_map.130.refs_0_), channel_id=1, source_target_pairs={{0,1},{1,0},{2,3},{3,2},{4,5},{5,4},{6,7},{7,6},{8,9},{9,8},{10,11... | collective-permute-start | bytes 1572872 | tf_op jit(solution)/shard_map/ppermute | solution.py:376
  80.8 9.2 %collective-permute-start.17 = (bf16[128,2048]{1,0:T(8,128)(2,1)S(1)}, bf16[128,2048]{1,0:T(8,128)(2,1)S(1)}, u32[]{:S(2)}, u32[]{:S(2)}) collective-permute-start(bf16[128,2048]{1,0:T(8,128)(2,1)S(1)} %shard_map.130.refs_0_), channel_id=1, source_target_pairs={{0,8},{1,17},{2,10},{3,19},{4,12},{5,21},{6,14},{7,23},{8,0},{9,25... | collective-permute-start | bytes 1572872 | tf_op jit(solution)/shard_map/ppermute | solution.py:376
  85.2 19.8 %copy-start.3 = (s32[32]{0:T(128)S(1)}, s32[32]{0:T(128)}, u32[]{:S(2)}) copy-start(s32[32]{0:T(128)} %param.13) | copy-start | bytes 388
  90.1 14.9 %collective-permute-start.19 = (bf16[256,2048]{1,0:T(8,128)(2,1)S(1)}, bf16[256,2048]{1,0:T(8,128)(2,1)S(1)}, u32[]{:S(2)}, u32[]{:S(2)}) collective-permute-start(bf16[256,2048]{1,0:T(8,128)(2,1)S(1)} %shard_map.133), channel_id=1, source_target_pairs={{0,16},{1,9},{2,18},{3,11},{4,20},{5,13},{6,22},{7,15},{8,24},{9,1... | collective-permute-start | bytes 3145736 | tf_op jit(solution)/shard_map/ppermute | solution.py:376
  90.6 1.9 %collective-permute-start.20 = (bf16[128,2048]{1,0:T(8,128)(2,1)S(1)}, bf16[128,2048]{1,0:T(8,128)(2,1)S(1)}, u32[]{:S(2)}, u32[]{:S(2)}) collective-permute-start(bf16[128,2048]{1,0:T(8,128)(2,1)S(1)} %collective-permute-done.17.refs_1_.refs_0_), channel_id=1, source_target_pairs={{0,1},{1,0},{2,3},{3,2},{4,5},{5,4},{6,7},{7,6},{8,9},{9,8},{10,11... | collective-permute-start | bytes 1572872 | tf_op jit(solution)/shard_map/ppermute | solution.py:376
  105.0 6.6 %collective-permute-start.21 = (bf16[256,2048]{1,0:T(8,128)(2,1)S(1)}, bf16[256,2048]{1,0:T(8,128)(2,1)S(1)}, u32[]{:S(2)}, u32[]{:S(2)}) collective-permute-start(bf16[256,2048]{1,0:T(8,128)(2,1)S(1)} %collective-permute-done.19.refs_0_), channel_id=1, source_target_pairs={{0,1},{1,0},{2,3},{3,2},{4,5},{5,4},{6,7},{7,6},{8,9},{9,8},{10,11... | collective-permute-start | bytes 3145736 | tf_op jit(solution)/shard_map/ppermute | solution.py:376
  105.3 8.8 %collective-permute-start.24 = (f32[8,2176]{1,0:T(8,128)S(1)}, f32[8,2176]{1,0:T(8,128)S(1)}, u32[]{:S(2)}, u32[]{:S(2)}) collective-permute-start(f32[8,2176]{1,0:T(8,128)S(1)} %get-tuple-element.128), channel_id=1, source_target_pairs={{0,24},{1,25},{2,26},{3,27},{4,28},{5,29},{6,30},{7,31},{8,16},{9,... | collective-permute-start | bytes 208904 | tf_op jit(solution)/shard_map/ppermute | solution.py:376
  106.8 7.3 %collective-permute-start.23 = (f32[8,2176]{1,0:T(8,128)S(1)}, f32[8,2176]{1,0:T(8,128)S(1)}, u32[]{:S(2)}, u32[]{:S(2)}) collective-permute-start(f32[8,2176]{1,0:T(8,128)S(1)} %get-tuple-element.126), channel_id=1, source_target_pairs={{0,16},{1,17},{2,18},{3,19},{4,20},{5,21},{6,22},{7,23},{8,24},{9,... | collective-permute-start | bytes 208904 | tf_op jit(solution)/shard_map/ppermute | solution.py:376
  108.3 5.8 %collective-permute-start.22 = (f32[8,2176]{1,0:T(8,128)S(1)}, f32[8,2176]{1,0:T(8,128)S(1)}, u32[]{:S(2)}, u32[]{:S(2)}) collective-permute-start(f32[8,2176]{1,0:T(8,128)S(1)} %get-tuple-element.124), channel_id=1, source_target_pairs={{0,8},{1,9},{2,10},{3,11},{4,12},{5,13},{6,14},{7,15},{8,0},{9,1},... | collective-permute-start | bytes 208904 | tf_op jit(solution)/shard_map/ppermute | solution.py:376

commit v3 on v2

--- a/solution.py
+++ b/solution.py
@@ -21,7 +21,7 @@
 IN_SMEM = pl.BlockSpec(memory_space=pltpu.SMEM)
 
 
-def kernel_call(body, args, specs, outs, scratch=(), out_specs=None, flops=0, limit=24):
+def kernel_call(body, args, specs, outs, scratch=(), out_specs=None, flops=0, limit=12):
     return pl.pallas_call(
         body,
         in_specs=specs,
@@ -115,6 +115,29 @@
     )
 
 
+def load_body(parts, source, target, sems):
+    size = source.shape[0] // parts
+    copies = []
+    for part in range(parts):
+        here = pl.ds(part * size, size)
+        copies.append(pltpu.make_async_copy(source.at[here], target.at[here], sems.at[part]))
+    for copy in copies:
+        copy.start()
+    for copy in copies:
+        copy.wait()
+
+
+def load(x, parts=8):
+    source = pltpu.with_memory_space_constraint(x, pltpu.HBM)
+    return kernel_call(
+        functools.partial(load_body, parts),
+        [source],
+        [IN_HBM],
+        [pltpu.VMEM(x.shape, x.dtype)],
+        [pltpu.SemaphoreType.DMA((parts,))],
+    )[0]
+
+
 def norms_body(block, dec_ref, column_ref, row_ref):
     for first in range(0, dec_ref.shape[0], block):
         here = slice(first, first + block)
@@ -154,14 +177,20 @@
     return kernel_call(add_body, [a, b], [IN_VMEM] * 2, [float_array(*a.shape)], limit=4)[0]
 
 
-def join_body(*refs):
-    join(refs[:-1], refs[-1])
-
-
-def joined(*pieces):
+def join_body(halves, *refs):
+    *pieces, out = refs
+    if not halves:
+        join(pieces, out)
+        return
+    cuts = [(first, piece.shape[0] // 2) for first in (0, 1) for piece in pieces]
+    join(pieces * 2, out, [(first * size, size) for first, size in cuts])
+
+
+def joined(*pieces, halves=False):
     count = sum(piece.shape[0] for piece in pieces)
     out = [half_array(count, pieces[0].shape[1])]
-    return kernel_call(join_body, pieces, [IN_VMEM] * len(pieces), out, limit=4)[0]
+    body = functools.partial(join_body, halves)
+    return kernel_call(body, pieces, [IN_VMEM] * len(pieces), out, limit=4)[0]
 
 
 def add_split_body(a_ref, b_ref, keep_ref, send_ref):
@@ -176,43 +205,55 @@
     return kernel_call(add_split_body, [a, b], [IN_VMEM] * 2, outs, limit=4)
 
 
+def add_both_body(a_ref, b_ref, sum_ref, send_ref):
+    total = a_ref[...] + b_ref[...].astype(jnp.float32)
+    sum_ref[...] = total
+    send_ref[...] = total.astype(jnp.bfloat16)
+
+
+def add_both(a, b):
+    outs = [float_array(*a.shape), half_array(*a.shape)]
+    return kernel_call(add_both_body, [a, b], [IN_VMEM] * 2, outs, limit=4)
+
+
 def residual_body(entries, a_ref, b_ref, bias_ref, heads_ref, energy_ref, rebuilt_ref, residual_ref):
-    rebuilt = a_ref[...] + b_ref[...].astype(jnp.float32) + bias_ref[...]
-    inputs = (heads_ref[...].astype(jnp.float32) * norm_scale(energy_ref, entries)).astype(jnp.bfloat16)
-    rebuilt_ref[...] = rebuilt.astype(jnp.bfloat16)
-    residual_ref[...] = (rebuilt - inputs.astype(jnp.float32)).astype(jnp.bfloat16)
-
-
-def own_residual(entries, *args):
-    shape = args[0].shape
+    half = rebuilt_ref.shape[0]
+    scale = norm_scale(energy_ref, entries)
+    for here, there in ((slice(0, half), slice(half, 2 * half)), (slice(half, 2 * half), slice(0, half))):
+        rebuilt = a_ref[here] + b_ref[there].astype(jnp.float32) + bias_ref[...]
+        inputs = (heads_ref[here].astype(jnp.float32) * scale).astype(jnp.bfloat16)
+        residual_ref[here] = (rebuilt - inputs.astype(jnp.float32)).astype(jnp.bfloat16)
+        if here.start == 0:
+            rebuilt_ref[...] = rebuilt.astype(jnp.bfloat16)
+
+
+def pair_residual(entries, *args):
+    count, width = args[0].shape
     body = functools.partial(residual_body, entries)
-    return kernel_call(body, args, [IN_VMEM] * 5, [half_array(*shape), half_array(*shape)], limit=4)
+    return kernel_call(body, args, [IN_VMEM] * 5, [half_array(count // 2, width), half_array(count, width)], limit=6)
 
 
 def own_columns(x, own_ref, columns):
     return x[:, pl.ds(pl.multiple_of(own_ref[0] * columns, 128), columns)]
 
 
-def join(pieces, rows):
+def join(pieces, rows, cuts=None):
     start = 0
-    for piece in pieces:
-        rows[start : start + piece.shape[0]] = piece[...]
-        start += piece.shape[0]
-
-
-def encode_body(count, tile, entries, energy_ref, own_ref, enc_ref, bias_ref, *refs):
+    for piece, (first, size) in zip(pieces, cuts or [(0, piece.shape[0]) for piece in pieces], strict=True):
+        rows[start : start + size] = piece[first : first + size]
+        start += size
+
+
+def whole(parts):
+    return [(part, 0, part.shape[0]) for part in parts]
+
+
+def encode_body(cuts, tile, entries, energy_ref, own_ref, enc_ref, bias_ref, *refs):
+    count = len(cuts)
     pieces, (codes_ref, slope_ref, part_ref), (rows, *rest) = refs[:count], refs[count : count + 3], refs[count + 3 :]
     if rest:
-        dec_hbm, keep_ref, send_ref, dec_ref, rows, coded_ref, sems = rows, *rest
-        parts = sems.shape[0]
-        size = dec_hbm.shape[0] // parts
-        copies = []
-        for part in range(parts):
-            here = pl.ds(part * size, size)
-            copies.append(pltpu.make_async_copy(dec_hbm.at[here], dec_ref.at[here], sems.at[part]))
-        for copy in copies:
-            copy.start()
-    join(pieces, rows)
+        dec_ref, keep_ref, send_ref, rows, coded_ref = rows, *rest
+    join(pieces, rows, cuts)
     factor = sharpness * LOG2E
     scale = norm_scale(energy_ref, entries) * factor
     for first in range(0, enc_ref.shape[1], tile):
@@ -227,8 +268,6 @@
     part_ref[...] = part.astype(jnp.float32).T.astype(jnp.bfloat16)
     if rest:
         half = keep_ref.shape[0]
-        for copy in copies:
-            copy.wait()
         for first in range(0, dec_ref.shape[1], tile):
             here = slice(first, first + tile)
             total = jnp.dot(coded_ref[...], dec_ref[:, here], preferred_element_type=jnp.float32)
@@ -236,11 +275,16 @@
             send_ref[:, here] = total[half:]
 
 
+def cut_pieces(parts):
+    return [part for part, _, _ in parts], [(first, size) for _, first, size in parts]
+
+
 def encode(entries, energy, own, enc, bias, pieces, columns):
     width, latents = enc.shape
-    count = sum(piece.shape[0] for piece in pieces)
+    pieces, cuts = cut_pieces(pieces)
+    count = sum(size for _, size in cuts)
     return kernel_call(
-        functools.partial(encode_body, len(pieces), min(512, latents), entries),
+        functools.partial(encode_body, cuts, min(512, latents), entries),
         [energy, own, held(enc), bias, *pieces],
         [IN_VMEM, IN_SMEM] + [IN_VMEM] * (2 + len(pieces)),
         [half_array(latents, count), half_array(count, latents), half_array(columns, count)],
@@ -249,69 +293,118 @@
     )
 
 
-def rebuild_body(count, tile, entries, energy_ref, own_ref, enc_ref, bias_ref, dec_hbm, *refs):
-    pieces, outs, scratch = refs[:count], refs[count : count + 6], refs[count + 6 :]
+def rebuild_body(cuts, tile, entries, energy_ref, own_ref, enc_ref, bias_ref, dec_ref, *refs):
+    count = len(cuts)
+    pieces, outs, scratch = refs[:count], refs[count : count + 5], refs[count + 5 :]
     encode_body(
-        count, tile, entries, energy_ref, own_ref, enc_ref, bias_ref, *pieces, *outs[:3], dec_hbm, *outs[3:], *scratch
+        cuts, tile, entries, energy_ref, own_ref, enc_ref, bias_ref, *pieces, *outs[:3], dec_ref, *outs[3:], *scratch
     )
 
 
 def encode_and_rebuild(entries, energy, own, enc, bias, dec, pieces, columns):
     width, latents = enc.shape
-    count = sum(piece.shape[0] for piece in pieces)
+    pieces, cuts = cut_pieces(pieces)
+    count = sum(size for _, size in cuts)
     return kernel_call(
-        functools.partial(rebuild_body, len(pieces), min(512, latents), entries),
-        [energy, own, held(enc), bias, pltpu.with_memory_space_constraint(dec, pltpu.HBM), *pieces],
-        [IN_VMEM, IN_SMEM, IN_VMEM, IN_VMEM, IN_HBM] + [IN_VMEM] * len(pieces),
+        functools.partial(rebuild_body, cuts, min(512, latents), entries),
+        [energy, own, held(enc), bias, held(dec), *pieces],
+        [IN_VMEM, IN_SMEM] + [IN_VMEM] * (3 + len(pieces)),
         [
             half_array(latents, count),
             half_array(count, latents),
             half_array(columns, count),
             float_array(count // 2, width),
             float_array(count // 2, width),
-            pltpu.VMEM(dec.shape, dec.dtype),
         ],
-        [
-            pltpu.VMEM((count, width), jnp.bfloat16),
-            pltpu.VMEM((count, latents), jnp.bfloat16),
-            pltpu.SemaphoreType.DMA((8,)),
-        ],
+        [pltpu.VMEM((count, width), jnp.bfloat16), pltpu.VMEM((count, latents), jnp.bfloat16)],
         flops=4 * count * width * latents,
     )
 
 
-def slope_body(count, tile, all_rows, own_ref, dec_ref, norms_ref, slope_ref, *refs):
-    pieces, (grad_ref, part_ref, rows) = refs[:count], refs[count:]
-    join(pieces, rows)
-    for first in range(0, dec_ref.shape[0], tile):
+def pre_tile(rows, dec_ref, norms_ref, slope_ref, here, all_rows):
+    product = lax.dot_general(
+        rows[...], dec_ref[here, :], (((1,), (1,)), ((), ())), preferred_element_type=jnp.float32
+    )
+    grad = product * (2.0 / all_rows) + norms_ref[:, here] * (sparsity_weight / all_rows)
+    return (grad * slope_ref[:, here].astype(jnp.float32)).astype(jnp.bfloat16)
+
+
+def slope_body(cuts, tile, all_rows, own_ref, dec_ref, norms_ref, *refs):
+    sets = len(cuts)
+    slopes, refs = refs[:sets], refs[sets:]
+    pieces = []
+    for chosen in cuts:
+        pieces.append(refs[: len(chosen)])
+        refs = refs[len(chosen) :]
+    grads, parts, scratch = refs[:sets], refs[sets : 2 * sets], refs[2 * sets :]
+    for chosen, slope_ref, piece, grad_ref, part_ref, rows in zip(
+        cuts, slopes, pieces, grads, parts, scratch, strict=True
+    ):
+        join(piece, rows, chosen)
+        for first in range(0, dec_ref.shape[0], tile):
+            here = slice(first, first + tile)
+            grad_ref[:, here] = pre_tile(rows, dec_ref, norms_ref, slope_ref, here, all_rows)
+        part_ref[...] = own_columns(rows, own_ref, part_ref.shape[1])
+
+
+def pre_gradient(all_rows, own, dec, norms, slopes, sets, columns):
+    latents, width = dec.shape
+    cut_sets = [cut_pieces(pieces) for pieces in sets]
+    counts = [sum(size for _, size in cuts) for _, cuts in cut_sets]
+    args = [held(dec), norms, *slopes, *(part for parts, _ in cut_sets for part in parts)]
+    outs = kernel_call(
+        functools.partial(slope_body, [cuts for _, cuts in cut_sets], min(512, latents), all_rows),
+        [own, *args],
+        [IN_SMEM] + [IN_VMEM] * len(args),
+        [half_array(count, latents) for count in counts] + [half_array(count, columns) for count in counts],
+        [pltpu.VMEM((count, width), jnp.bfloat16) for count in counts],
+        flops=2 * sum(counts) * width * latents,
+    )
+    return list(zip(outs[: len(sets)], outs[len(sets) :], strict=True))
+
+
+def early_body(groups, tile, *refs):
+    rows, grads, coded, residual = (refs[i * groups : (i + 1) * groups] for i in range(4))
+    enc_ref, dec_ref, sums_ref = refs[4 * groups :]
+    for first in range(0, enc_ref.shape[1], tile):
         here = slice(first, first + tile)
-        product = lax.dot_general(
-            rows[...], dec_ref[here, :], (((1,), (1,)), ((), ())), preferred_element_type=jnp.float32
-        )
-        grad = product * (2.0 / all_rows) + norms_ref[:, here] * (sparsity_weight / all_rows)
-        grad_ref[:, here] = (grad * slope_ref[:, here].astype(jnp.float32)).astype(jnp.bfloat16)
-    part_ref[...] = own_columns(rows, own_ref, part_ref.shape[1])
-
-
-def pre_gradient(all_rows, own, dec, norms, slope, pieces, columns):
-    latents, width = dec.shape
-    count = sum(piece.shape[0] for piece in pieces)
+        enc, dec, sums = 0.0, 0.0, 0.0
+        for g in range(groups):
+            enc = enc + jnp.dot(rows[g][...], grads[g][:, here], preferred_element_type=jnp.float32)
+            dec = dec + jnp.dot(coded[g][here, :], residual[g][...], preferred_element_type=jnp.float32)
+            sums = sums + jnp.sum(coded[g][here, :].astype(jnp.float32), axis=1, keepdims=True)
+        enc_ref[:, here] = enc
+        dec_ref[here, :] = dec
+        sums_ref[here, :] = sums
+
+
+def early_sums(rows, grads, coded, residual):
+    columns = rows[0].shape[0]
+    latents = coded[0].shape[0]
+    count = sum(x.shape[0] for x in grads)
+    args = [*rows, *grads, *coded, *residual]
     return kernel_call(
-        functools.partial(slope_body, len(pieces), min(512, latents), all_rows),
-        [own, held(dec), norms, slope, *pieces],
-        [IN_SMEM] + [IN_VMEM] * (3 + len(pieces)),
-        [half_array(count, latents), half_array(count, columns)],
-        [pltpu.VMEM((count, width), jnp.bfloat16)],
-        flops=2 * count * width * latents,
-    )
-
-
-def weight_body(groups, tile, all_rows, entries, energy_ref, own_ref, norms_ref, dec_ref, *refs):
-    rows, grads, coded, residual = (refs[i * groups : (i + 1) * groups] for i in range(4))
-    enc_out, dec_out, enc_buffer, dec_buffer, sems = refs[4 * groups :]
+        functools.partial(early_body, len(rows), min(512, latents)),
+        args,
+        [IN_VMEM] * len(args),
+        [float_array(columns, latents), float_array(latents, columns), float_array(latents, 1)],
+        flops=4 * count * columns * latents,
+    )
+
+
+def last_body(
+    cuts, groups, tile, all_rows, entries, energy_ref, own_ref, column_ref, row_ref, dec_ref, enc_sum, dec_sum,
+    sums_ref, rows_ref, coded_ref, slope_ref, *refs,
+):
+    rows, grads, coded, parts = (refs[i * groups : (i + 1) * groups] for i in range(4))
+    refs = refs[4 * groups :]
+    count = len(cuts)
+    pieces, (enc_out, dec_out, enc_buffer, dec_buffer, residual, part, sems) = refs[:count], refs[count:]
     columns = dec_buffer.shape[2]
     steps = dec_ref.shape[0] // tile
     scale = norm_scale(energy_ref, entries)
+    join(pieces, residual, cuts)
+    part[...] = own_columns(residual, own_ref, columns)
 
     def copies(step):
         slot, here = step % 2, pl.ds(step * tile, tile)
@@ -325,40 +418,49 @@
             for copy in copies(step - 2):
                 copy.wait()
         here = slice(step * tile, (step + 1) * tile)
-        enc, dec, sums = 0.0, 0.0, 0.0
-        for g in range(groups):
-            enc = enc + jnp.dot(rows[g][...], grads[g][:, here], preferred_element_type=jnp.float32)
-            dec = dec + jnp.dot(coded[g][here, :], residual[g][...], preferred_element_type=jnp.float32)
-            sums = sums + jnp.sum(coded[g][here, :].astype(jnp.float32), axis=1, keepdims=True)
+        enc, dec, sums = enc_sum[:, here], dec_sum[here, :], sums_ref[here, :]
+        for coded_set, part_set in zip((*coded, coded_ref), (*parts, part), strict=True):
+            dec = dec + jnp.dot(coded_set[here, :], part_set[...], preferred_element_type=jnp.float32)
+            sums = sums + jnp.sum(coded_set[here, :].astype(jnp.float32), axis=1, keepdims=True)
+        weights = own_columns(dec_ref.at[here, :], own_ref, columns).astype(jnp.float32)
+        factor = sums / column_ref[here, :] * (sparsity_weight / all_rows)
+        dec_buffer[step % 2] = dec * (2.0 / all_rows) + factor * weights
+        copies(step)[1].start()
+        for rows_set, grad in zip(rows, grads, strict=True):
+            enc = enc + jnp.dot(rows_set[...], grad[:, here], preferred_element_type=jnp.float32)
+        grad = pre_tile(residual, dec_ref, row_ref, slope_ref, here, all_rows)
+        enc = enc + jnp.dot(rows_ref[...], grad, preferred_element_type=jnp.float32)
         enc_buffer[step % 2] = enc * scale
-        part = own_columns(dec_ref.at[here, :], own_ref, columns).astype(jnp.float32)
-        factor = sums / norms_ref[here, :] * (sparsity_weight / all_rows)
-        dec_buffer[step % 2] = dec * (2.0 / all_rows) + factor * part
-        for copy in copies(step):
-            copy.start()
+        copies(step)[0].start()
     for step in range(max(steps - 2, 0), steps):
         for copy in copies(step):
             copy.wait()
 
 
-def weight_gradients(all_rows, entries, energy, own, norms, dec, rows, grads, coded, residual):
-    columns = rows[0].shape[0]
-    latents = dec.shape[0]
-    count = sum(x.shape[0] for x in grads)
+def weight_gradients(all_rows, entries, energy, own, column, row, dec, early, middle, encoded, pieces):
+    coded, slope, rows = encoded
+    columns = rows.shape[0]
+    latents, width = dec.shape
+    pieces, cuts = cut_pieces(pieces)
+    count = sum(size for _, size in cuts)
     tile = min(512, latents)
-    args = [norms, held(dec), *rows, *grads, *coded, *residual]
+    middle = [x for kind in zip(*middle, strict=True) for x in kind]
+    args = [column, row, held(dec), *early, rows, coded, slope, *middle, *pieces]
     return kernel_call(
-        functools.partial(weight_body, len(rows), tile, all_rows, entries),
+        functools.partial(last_body, cuts, len(middle) // 4, tile, all_rows, entries),
         [energy, own, *args],
         [IN_VMEM, IN_SMEM] + [IN_VMEM] * len(args),
         [pltpu.HBM((columns, latents), jnp.float32), pltpu.HBM((latents, columns), jnp.float32)],
         [
             pltpu.VMEM((2, columns, tile), jnp.float32),
             pltpu.VMEM((2, tile, columns), jnp.float32),
+            pltpu.VMEM((count, width), jnp.bfloat16),
+            pltpu.VMEM((count, columns), jnp.bfloat16),
             pltpu.SemaphoreType.DMA((2, 2)),
         ],
         [IN_HBM, IN_HBM],
-        flops=4 * count * columns * latents,
+        flops=2 * count * width * latents + 4 * count * columns * latents,
+        limit=16,
     )
 
 
@@ -485,86 +587,110 @@
         if number == len(line) - 1:
             count = len(small_steps)
         for small in small_steps[:count]:
-            energy = add(energy, swap(energy, *small))
+            other = swap(energy, *small)
+            if small == line[0]:
+                dec = load(after(dec_weight, energy))
+                other = after(other, dec)
+            energy = add(energy, other)
         small_steps = small_steps[count:]
         rows = joined(rows, after(arrived, energy))
-
-    pieces = [rows, swap(rows, *plane[0])]
-    group = [rows, swap(rows, *core)]
-    *first_set, keep, send, dec = encode_and_rebuild(entries, energy, own, enc, bias, dec_weight, group, columns)
+        if number == 0:
+            pair = rows
+
+    def chunks(near, far, first, size, largest=256):
+        step = min(size, largest)
+        return [[(near, i, step), (far, i, step)] for i in range(first, first + size, step)]
+
+    hop = swap(rows, *plane[0])
+    group = whole([rows, swap(rows, *core)])
+    *first_set, keep, send = encode_and_rebuild(entries, energy, own, enc, bias, dec, group, columns)
     encoded = [first_set]
 
-    def cut(part, largest=512):
-        return [part[i : i + largest] for i in range(0, part.shape[0], largest)]
-
     def encode_next(parts, now):
-        parts = [after(part, now) for part in parts]
+        parts = [(after(part, now), *cut) for part, *cut in parts]
         encoded.append(encode(entries, energy, own, enc, bias, parts, columns))
         return encoded[-1][0]
 
-    total, sent = add_split(keep, swap(send, *core))
+    arrived = swap(after(send, hop), *core)
+    total = keep
+    far = [rows, hop]
     for number, mask in enumerate(line[::-1]):
+        last = number == len(line) - 1
+        total, sent = (add_both if last else add_split)(total, arrived)
         arrived = swap(sent, *mask)
         if number == 0:
-            for step in plane[1:]:
-                pieces = [after(piece, sent) for piece in pieces]
-                pieces.append(swap(joined(*pieces), *step))
-            second = [pieces[1], swap(pieces[1], *core)]
-        if number == len(line) - 1:
-            arrived = after(arrived, encode_next(second, sent))
-        else:
-            total, sent = add_split(total, arrived)
-    rebuilt_own, residual_own = own_residual(entries, total, arrived, out_bias, heads_out, energy)
-
-    rows = residual_own
-    for number, mask in enumerate(line):
-        arrived = swap(rows, *mask)
-        if number == 0:
-            norms_column, norms_row = decoder_norms(after(dec, rows))
-            arrived = after(arrived, norms_row)
-            far = [after(piece, rows) for piece in pieces[2:]]
-            far = [part for piece in far for part in (piece, swap(piece, *core))]
-        if number == len(line) - 1:
-            done = [encode_next([part], rows) for piece in far for part in cut(piece)]
-            arrived = after(arrived, *done)
-        rows = joined(rows, arrived)
+            hop = after(hop, sent)
+            arrived = after(arrived, encode_next(whole([hop, swap(hop, *core)]), sent))
+            for step in plane[1:2]:
+                far.append(swap(joined(*(after(piece, sent) for piece in far), halves=True), *step))
+        if last:
+            norms_column, norms_row = decoder_norms(after(dec, sent))
+            arrived = after(arrived, norms_row, far[-1])
+    rebuilt_own, rows = pair_residual(entries, total, arrived, out_bias, pair, energy)
+    for step in plane[2:]:
+        far.append(swap(joined(*(after(piece, rows) for piece in far), halves=True), *step))
+    others = [swap(after(piece, rows), *core) for piece in far[2:]]
+
+    for mask in line[1:-1]:
+        rows = joined(rows, swap(rows, *mask))
+    near, late = [rows], [swap(rows, *line[-1])]
+    near.append(swap(rows, *plane[0]))
+    done = []
+    for piece, other in zip(far[2:], others, strict=True):
+        half = piece.shape[0] // 2
+        for first in (0, half):
+            done += [encode_next(parts, rows) for parts in chunks(piece, other, first, half)]
+    late[0] = after(late[0], near[1], *done)
     grads = []
 
-    def pre(parts, now):
-        slope = encoded[len(grads)][1]
-        parts = [after(part, now) for part in parts]
-        grads.append(pre_gradient(all_rows, own, dec, norms_row, slope, parts, columns))
+    def pre(sets, now):
+        slopes = [code[1] for code in encoded[len(grads) : len(grads) + len(sets)]]
+        sets = [[(after(part, now), *cut) for part, *cut in parts] for parts in sets]
+        grads.extend(pre_gradient(all_rows, own, dec, norms_row, slopes, sets, columns))
         return grads[-1][0]
 
-    group = [rows, swap(rows, *core)]
-    pieces = [rows]
-    for number, mask in enumerate(plane):
-        sent = pieces[0] if number == 0 else joined(*pieces)
-        arrived = swap(sent, *mask)
-        if number == 0:
-            moved = send_rows(own, after(rebuilt_own, sent), places)
-            arrived = after(arrived, pre(group, sent))
-        elif number == 1:
-            arrived = after(arrived, pre([pieces[1], swap(pieces[1], *core)], sent))
-        pieces.append(arrived)
-    far = [part for piece in pieces[2:] for part in (piece, swap(piece, *core))]
-    for piece in far:
-        for part in cut(piece):
-            last = pre([part], pieces[-1])
-    moved = [after(part, last) for part in moved]
-    rebuilt = place_rows(moved, rows_here, att_width)
+    def ready(sets):
+        chosen = [(encoded[i], grads[i]) for i in sets]
+        return [(code[2], grad[0], code[0], grad[1]) for code, grad in chosen]
+
+    late.append(swap(late[0], *plane[0]))
+    near.append(swap(joined(*near), *plane[1]))
+    rows = joined(near[0], late[0])
+    done = pre([whole([rows, swap(rows, *core)])], rows)
+    moved = send_rows(own, after(rebuilt_own, rows), places)
+    near[2] = after(near[2], done)
+    hop = joined(near[1], after(late[1], done))
+    sets = [whole([hop, swap(hop, *core)])]
+    count = 2
+    for number, step in enumerate(plane[1:], 1):
+        if number > 1:
+            near.append(swap(joined(*near), *step))
+        late.append(swap(joined(*late), *step))
+        sets += chunks(near[-1], swap(near[-1], *core), 0, near[-1].shape[0])
+        if number < len(plane) - 1:
+            sets += chunks(late[-1], swap(late[-1], *core), 0, late[-1].shape[0])
+            count += 2 * len(chunks(near[-1], near[-1], 0, near[-1].shape[0]))
+    for first in range(0, len(sets), 2):
+        done = pre(sets[first : first + 2], hop)
+    last = after(late[-1], done, *moved)
+    sets = chunks(last, swap(last, *core), 0, last.shape[0])
+    for parts in sets[:-1]:
+        done = pre([parts], done)
+    early = early_sums(*([after(x, last) for x in kind] for kind in zip(*ready(range(count)), strict=True)))
     grad_enc, grad_dec = weight_gradients(
         all_rows,
         entries,
         energy,
         own,
         norms_column,
+        norms_row,
         dec,
-        [x[2] for x in encoded],
-        [x[0] for x in grads],
-        [x[0] for x in encoded],
-        [x[1] for x in grads],
-    )
+        early,
+        ready(range(count, len(grads))),
+        encoded[-1],
+        sets[-1],
+    )
+    rebuilt = place_rows([after(part, early[0]) for part in moved], rows_here, att_width)
     return (rebuilt, grad_enc, grad_dec)
 
 

time: 122 us -> 105 us (0.86)
  waiting for transfers between devices: 53.2 us -> 32.5 us
  starting transfers between devices: 22.3 us -> 25.3 us
    ppermute x25 -> x27, waiting for transfers between devices: 53.2 us -> 32.5 us  [swap(): lax.ppermute(x, ('dp', 'latent'), [(i, i ^ (odd if i & 1 else even)) for...]
    ppermute x25 -> x27, starting transfers between devices: 22.3 us -> 25.3 us  [swap(): lax.ppermute(x, ('dp', 'latent'), [(i, i ^ (odd if i & 1 else even)) for...]
    pallas_call x27 -> x28, Pallas kernels: 44.5 us -> 45.3 us  [kernel_call(): pl.pallas_call(body, in_specs=specs, out_specs=out_specs or [IN_VMEM] * l...]
  transfers between devices with their start and end apart: 25 -> 27, of which waited for: 16 -> 14; matrix products, arithmetic and copies ran while one was open for 0% -> 0% of each run, Pallas kernels for 20% -> 32%
where the time goes in v3:
time: 105 us
  Pallas kernels  45.3 us (43%)
  waiting for transfers between devices  32.5 us (31%)
  starting transfers between devices  25.3 us (24%)
    pallas_call x28, Pallas kernels, kernel_call(): pl.pallas_call(body, in_specs=specs, out_specs=out_specs or [IN_VMEM] * l...  45.3 us
    ppermute x27, waiting for transfers between devices, swap(): lax.ppermute(x, ('dp', 'latent'), [(i, i ^ (odd if i & 1 else even)) for...  32.5 us
    ppermute x27, starting transfers between devices, swap(): lax.ppermute(x, ('dp', 'latent'), [(i, i ^ (odd if i & 1 else even)) for...  25.3 us
  transfers between devices with their start and end apart: 27, of which 14 were waited for; matrix products, arithmetic and copies ran while one was open for 0% of the time, Pallas kernels for 32%

profile of v3, /device:TPU:0, one launch (start us, length us, event | category | flops | bytes accessed | tf_op | source)
XLA Modules:
  0.0 104.8 jit_solution(2793815880931704214)
XLA Ops:
  1.3 4.8 %shard_map.112 = (bf16[32,2048]{1,0:T(8,128)(2,1)S(1)}, f32[1,128]{1,0:T(1,128)S(1)}, bf16[2048,2048]{1,0:T(8,128)(2,1)S(1)}) custom-call(s32[32]{0:T(128)S(1)} %copy-done.2, bf16[32,2048]{1,0:T(8,128)(2,1)} %queries.1, bf16[1,512,1024]{2,1,0:T(8,128)(2,1)} %keys.1, bf16[1,512,1024]{2,1,0:T(8,128)(2,1)} %values.1, bf16[2048,2048]{1,0:T(8,128)(2,1)} %enc), custom_call_target="tpu_custom_call" | custom-call | flops 134217728 | tf_op jit(solution)/shard_map/pallas_call | solution.py:25
  6.1 4.1 %collective-permute-start.5 = (bf16[32,2048]{1,0:T(8,128)(2,1)S(1)}, bf16[32,2048]{1,0:T(8,128)(2,1)S(1)}, u32[]{:S(2)}, u32[]{:S(2)}) collective-permute-start(bf16[32,2048]{1,0:T(8,128)(2,1)S(1)} %get-tuple-element.94.refs_0_), channel_id=1, source_target_pairs={{0,4},{1,3},{2,6},{3,1},{4,0},{5,7},{6,2},{7,5},{8,12},{9,11},{10,... | collective-permute-start | bytes 393224 | tf_op jit(solution)/shard_map/ppermute | solution.py:478
  10.2 1.5 %collective-permute-start = (f32[1,128]{1,0:T(1,128)S(1)}, f32[1,128]{1,0:T(1,128)S(1)}, u32[]{:S(2)}, u32[]{:S(2)}) collective-permute-start(f32[1,128]{1,0:T(1,128)S(1)} %get-tuple-element.90.a_ref), channel_id=1, source_target_pairs={{0,8},{1,17},{2,10},{3,19},{4,12},{5,21},{6,14},{7,23},{8,0},{9,25... | collective-permute-start | bytes 1544 | tf_op jit(solution)/shard_map/ppermute | solution.py:478
  11.7 2.0 %collective-permute-done.b_ref = f32[1,128]{1,0:T(1,128)S(1)} collective-permute-done((f32[1,128]{1,0:T(1,128)S(1)}, f32[1,128]{1,0:T(1,128)S(1)}, u32[]{:S(2)}, u32[]{:S(2)}) %collective-permute-start) | collective-permute-done | bytes 544 | tf_op jit(solution)/shard_map/ppermute | solution.py:478
  13.7 1.5 %collective-permute-start.1 = (f32[1,128]{1,0:T(1,128)S(1)}, f32[1,128]{1,0:T(1,128)S(1)}, u32[]{:S(2)}, u32[]{:S(2)}) collective-permute-start(f32[1,128]{1,0:T(1,128)S(1)} %shard_map.113.a_ref), channel_id=1, source_target_pairs={{0,16},{1,9},{2,18},{3,11},{4,20},{5,13},{6,22},{7,15},{8,24},{9,1... | collective-permute-start | bytes 1544 | tf_op jit(solution)/shard_map/ppermute | solution.py:478
  15.3 2.0 %collective-permute-done.1.b_ref = f32[1,128]{1,0:T(1,128)S(1)} collective-permute-done((f32[1,128]{1,0:T(1,128)S(1)}, f32[1,128]{1,0:T(1,128)S(1)}, u32[]{:S(2)}, u32[]{:S(2)}) %collective-permute-start.1) | collective-permute-done | bytes 544 | tf_op jit(solution)/shard_map/ppermute | solution.py:478
  17.3 1.6 %collective-permute-start.6 = (bf16[64,2048]{1,0:T(8,128)(2,1)S(1)}, bf16[64,2048]{1,0:T(8,128)(2,1)S(1)}, u32[]{:S(2)}, u32[]{:S(2)}) collective-permute-start(bf16[64,2048]{1,0:T(8,128)(2,1)S(1)} %shard_map.119.refs_0_.heads_ref), channel_id=1, source_target_pairs={{0,2},{1,5},{2,0},{3,7},{4,6},{5,1},{6,4},{7,3},{8,10},{9,13},{10,... | collective-permute-start | bytes 786440 | tf_op jit(solution)/shard_map/ppermute | solution.py:478
  20.4 3.5 %shard_map.116.dec_ref = bf16[2048,2048]{1,0:T(8,128)(2,1)S(1)} custom-call(bf16[2048,2048]{1,0:T(8,128)(2,1)} %source), custom_call_target="tpu_custom_call" | custom-call | tf_op jit(solution)/shard_map/pallas_call | solution.py:25
  25.0 3.1 %collective-permute-done.4.b_ref = f32[1,128]{1,0:T(1,128)S(1)} collective-permute-done((f32[1,128]{1,0:T(1,128)S(1)}, f32[1,128]{1,0:T(1,128)S(1)}, u32[]{:S(2)}, u32[]{:S(2)}) %collective-permute-start.4) | collective-permute-done | bytes 544 | tf_op jit(solution)/shard_map/ppermute | solution.py:478
  28.2 1.6 %collective-permute-start.8 = (bf16[128,2048]{1,0:T(8,128)(2,1)S(1)}, bf16[128,2048]{1,0:T(8,128)(2,1)S(1)}, u32[]{:S(2)}, u32[]{:S(2)}) collective-permute-start(bf16[128,2048]{1,0:T(8,128)(2,1)S(1)} %shard_map.120.refs_0_), channel_id=1, source_target_pairs={{0,8},{1,17},{2,10},{3,19},{4,12},{5,21},{6,14},{7,23},{8,0},{9,25... | collective-permute-start | bytes 1572872 | tf_op jit(solution)/shard_map/ppermute | solution.py:478
  30.1 5.5 %shard_map.121 = (bf16[2048,256]{1,0:T(8,128)(2,1)S(1)}, bf16[256,2048]{1,0:T(8,128)(2,1)S(1)}, bf16[512,256]{1,0:T(8,128)(2,1)S(1)}, f32[128,2048]{1,0:T(8,128)S(1)}, f32[128,2048]{1,0:T(8,128)S(1)}) custom-call(f32[1,128]{1,0:T(1,128)S(1)} %shard_map.118.energy_ref, s32[1]{0:T(128)} %bitcast.3.own_ref, bf16[2048,2048]{1,0:T(8,128)(2,1)S(1)} %get-tuple-element.93.enc_ref, ...), custom_call_target="tpu_custom_call" | custom-call | flops 4294967296 | tf_op jit(solution)/shard_map/pallas_call | solution.py:25
  35.6 1.8 %collective-permute-done.8.refs_0_.refs_1_ = bf16[128,2048]{1,0:T(8,128)(2,1)S(1)} collective-permute-done((bf16[128,2048]{1,0:T(8,128)(2,1)S(1)}, bf16[128,2048]{1,0:T(8,128)(2,1)S(1)}, u32[]{:S(2)}, u32[]{:S(2)}) %collective-permute-start.8) | collective-permute-done | bytes 524320 | tf_op jit(solution)/shard_map/ppermute | solution.py:478
  37.4 2.7 %collective-permute-done.9.b_ref = f32[128,2048]{1,0:T(8,128)S(1)} collective-permute-done((f32[128,2048]{1,0:T(8,128)S(1)}, f32[128,2048]{1,0:T(8,128)S(1)}, u32[]{:S(2)}, u32[]{:S(2)}) %collective-permute-start.9) | collective-permute-done | bytes 1048608 | tf_op jit(solution)/shard_map/ppermute | solution.py:478
  40.3 1.6 %collective-permute-start.13 = (bf16[256,2048]{1,0:T(8,128)(2,1)S(1)}, bf16[256,2048]{1,0:T(8,128)(2,1)S(1)}, u32[]{:S(2)}, u32[]{:S(2)}) collective-permute-start(bf16[256,2048]{1,0:T(8,128)(2,1)S(1)} %shard_map.126), channel_id=1, source_target_pairs={{0,16},{1,9},{2,18},{3,11},{4,20},{5,13},{6,22},{7,15},{8,24},{9,1... | collective-permute-start | bytes 3145736 | tf_op jit(solution)/shard_map/ppermute | solution.py:478
  43.8 3.5 %shard_map.123 = (bf16[2048,256]{1,0:T(8,128)(2,1)S(1)}, bf16[256,2048]{1,0:T(8,128)(2,1)S(1)}, bf16[512,256]{1,0:T(8,128)(2,1)S(1)}) custom-call(f32[1,128]{1,0:T(1,128)S(1)} %shard_map.118.energy_ref, s32[1]{0:T(128)} %bitcast.3.own_ref, bf16[2048,2048]{1,0:T(8,128)(2,1)S(1)} %get-tuple-element.93.enc_ref, f32[1,2048]{1,0:T(1,128)S(1)} %bitcast.5, ...), custom_call_target="tpu_custom_call" | custom-call | flops 2147483648 | tf_op jit(solution)/shard_map/pallas_call | solution.py:25
  47.3 2.6 %collective-permute-done.10.b_ref = bf16[64,2048]{1,0:T(8,128)(2,1)S(1)} collective-permute-done((bf16[64,2048]{1,0:T(8,128)(2,1)S(1)}, bf16[64,2048]{1,0:T(8,128)(2,1)S(1)}, u32[]{:S(2)}, u32[]{:S(2)}) %collective-permute-start.10) | collective-permute-done | bytes 262176 | tf_op jit(solution)/shard_map/ppermute | solution.py:478
  50.0 2.3 %collective-permute-start.12 = (bf16[64,2048]{1,0:T(8,128)(2,1)S(1)}, bf16[64,2048]{1,0:T(8,128)(2,1)S(1)}, u32[]{:S(2)}, u32[]{:S(2)}) collective-permute-start(bf16[64,2048]{1,0:T(8,128)(2,1)S(1)} %get-tuple-element.108), channel_id=1, source_target_pairs={{0,4},{1,3},{2,6},{3,1},{4,0},{5,7},{6,2},{7,5},{8,12},{9,11},{10,... | collective-permute-start | bytes 786440 | tf_op jit(solution)/shard_map/ppermute | solution.py:478
  52.4 2.3 %shard_map.125 = (f32[2048,1]{1,0:T(8,128)S(1)}, f32[1,2048]{1,0:T(1,128)S(1)}) custom-call(bf16[2048,2048]{1,0:T(8,128)(2,1)S(1)} %shard_map.116.dec_ref), custom_call_target="tpu_custom_call" | custom-call | tf_op jit(solution)/shard_map/pallas_call | solution.py:25
  54.7 5.1 %collective-permute-done.12.b_ref = bf16[64,2048]{1,0:T(8,128)(2,1)S(1)} collective-permute-done((bf16[64,2048]{1,0:T(8,128)(2,1)S(1)}, bf16[64,2048]{1,0:T(8,128)(2,1)S(1)}, u32[]{:S(2)}, u32[]{:S(2)}) %collective-permute-start.12) | collective-permute-done | bytes 262176 | tf_op jit(solution)/shard_map/ppermute | solution.py:478
  61.2 1.5 %collective-permute-start.15 = (bf16[64,2048]{1,0:T(8,128)(2,1)S(1)}, bf16[64,2048]{1,0:T(8,128)(2,1)S(1)}, u32[]{:S(2)}, u32[]{:S(2)}) collective-permute-start(bf16[64,2048]{1,0:T(8,128)(2,1)S(1)} %get-tuple-element.114.refs_0_), channel_id=1, source_target_pairs={{0,8},{1,17},{2,10},{3,19},{4,12},{5,21},{6,14},{7,23},{8,0},{9,25... | collective-permute-start | bytes 786440 | tf_op jit(solution)/shard_map/ppermute | solution.py:478
  62.7 3.5 %shard_map.128 = (bf16[2048,256]{1,0:T(8,128)(2,1)S(1)}, bf16[256,2048]{1,0:T(8,128)(2,1)S(1)}, bf16[512,256]{1,0:T(8,128)(2,1)S(1)}) custom-call(f32[1,128]{1,0:T(1,128)S(1)} %shard_map.118.energy_ref, s32[1]{0:T(128)} %bitcast.3.own_ref, bf16[2048,2048]{1,0:T(8,128)(2,1)S(1)} %get-tuple-element.93.enc_ref, f32[1,2048]{1,0:T(1,128)S(1)} %bitcast.6, ...), custom_call_target="tpu_custom_call" | custom-call | flops 2147483648 | tf_op jit(solution)/shard_map/pallas_call | solution.py:25
  66.3 3.6 %shard_map.129 = (bf16[2048,256]{1,0:T(8,128)(2,1)S(1)}, bf16[256,2048]{1,0:T(8,128)(2,1)S(1)}, bf16[512,256]{1,0:T(8,128)(2,1)S(1)}) custom-call(f32[1,128]{1,0:T(1,128)S(1)} %shard_map.118.energy_ref, s32[1]{0:T(128)} %bitcast.3.own_ref, bf16[2048,2048]{1,0:T(8,128)(2,1)S(1)} %get-tuple-element.93.enc_ref, f32[1,2048]{1,0:T(1,128)S(1)} %bitcast.7, ...), custom_call_target="tpu_custom_call" | custom-call | flops 2147483648 | tf_op jit(solution)/shard_map/pallas_call | solution.py:25
  70.9 1.3 %collective-permute-start.17 = (bf16[64,2048]{1,0:T(8,128)(2,1)S(1)}, bf16[64,2048]{1,0:T(8,128)(2,1)S(1)}, u32[]{:S(2)}, u32[]{:S(2)}) collective-permute-start(bf16[64,2048]{1,0:T(8,128)(2,1)S(1)} %collective-permute-done.14.refs_1_.refs_0_), channel_id=1, source_target_pairs={{0,8},{1,17},{2,10},{3,19},{4,12},{5,21},{6,14},{7,23},{8,0},{9,25... | collective-permute-start | bytes 786440 | tf_op jit(solution)/shard_map/ppermute | solution.py:478
  72.1 2.5 %shard_map.133 = (bf16[256,2048]{1,0:T(8,128)(2,1)S(1)}, bf16[256,512]{1,0:T(8,128)(2,1)S(1)}) custom-call(s32[1]{0:T(128)} %bitcast.3.own_ref, bf16[2048,2048]{1,0:T(8,128)(2,1)S(1)} %shard_map.116.dec_ref, f32[1,2048]{1,0:T(1,128)S(1)} %get-tuple-element.110.norms_ref.row_ref, bf16[256,2048]{1,0:T(8,128)(2,1)S(1)} %get-tuple-element.125.refs_0_, ...), custom_call_target="tpu_custom_call" | custom-call | flops 2147483648 | tf_op jit(solution)/shard_map/pallas_call | solution.py:25
  74.6 5.5 %collective-permute-done.17.refs_1_ = bf16[64,2048]{1,0:T(8,128)(2,1)S(1)} collective-permute-done((bf16[64,2048]{1,0:T(8,128)(2,1)S(1)}, bf16[64,2048]{1,0:T(8,128)(2,1)S(1)}, u32[]{:S(2)}, u32[]{:S(2)}) %collective-permute-start.17) | collective-permute-done | bytes 262176 | tf_op jit(solution)/shard_map/ppermute | solution.py:478
  80.2 1.9 %collective-permute-done.21.refs_4_ = bf16[128,2048]{1,0:T(8,128)(2,1)S(1)} collective-permute-done((bf16[128,2048]{1,0:T(8,128)(2,1)S(1)}, bf16[128,2048]{1,0:T(8,128)(2,1)S(1)}, u32[]{:S(2)}, u32[]{:S(2)}) %collective-permute-start.21) | collective-permute-done | bytes 524320 | tf_op jit(solution)/shard_map/ppermute | solution.py:478
  83.3 1.2 %collective-permute-start.23 = (f32[8,2176]{1,0:T(8,128)S(1)}, f32[8,2176]{1,0:T(8,128)S(1)}, u32[]{:S(2)}, u32[]{:S(2)}) collective-permute-start(f32[8,2176]{1,0:T(8,128)S(1)} %get-tuple-element.136), channel_id=1, source_target_pairs={{0,8},{1,9},{2,10},{3,11},{4,12},{5,13},{6,14},{7,15},{8,0},{9,1},... | collective-permute-start | bytes 208904 | tf_op jit(solution)/shard_map/ppermute | solution.py:478
  84.5 1.4 %collective-permute-start.24 = (f32[8,2176]{1,0:T(8,128)S(1)}, f32[8,2176]{1,0:T(8,128)S(1)}, u32[]{:S(2)}, u32[]{:S(2)}) collective-permute-start(f32[8,2176]{1,0:T(8,128)S(1)} %get-tuple-element.137), channel_id=1, source_target_pairs={{0,16},{1,17},{2,18},{3,19},{4,20},{5,21},{6,22},{7,23},{8,24},{9,... | collective-permute-start | bytes 208904 | tf_op jit(solution)/shard_map/ppermute | solution.py:478
  86.9 4.9 %shard_map.136 = (bf16[256,2048]{1,0:T(8,128)(2,1)S(1)}, bf16[256,2048]{1,0:T(8,128)(2,1)S(1)}, bf16[256,512]{1,0:T(8,128)(2,1)S(1)}, bf16[256,512]{1,0:T(8,128)(2,1)S(1)}) custom-call(s32[1]{0:T(128)} %bitcast.3.own_ref, bf16[2048,2048]{1,0:T(8,128)(2,1)S(1)} %shard_map.116.dec_ref, f32[1,2048]{1,0:T(1,128)S(1)} %get-tuple-element.110.norms_ref.row_ref, ...), custom_call_target="tpu_custom_call" | custom-call | flops 4294967296 | tf_op jit(solution)/shard_map/pallas_call | solution.py:25
  91.8 2.6 %collective-permute-done.24.refs_2_ = f32[8,2176]{1,0:T(8,128)S(1)} collective-permute-done((f32[8,2176]{1,0:T(8,128)S(1)}, f32[8,2176]{1,0:T(8,128)S(1)}, u32[]{:S(2)}, u32[]{:S(2)}) %collective-permute-start.24) | collective-permute-done | bytes 69664 | tf_op jit(solution)/shard_map/ppermute | solution.py:478
  94.4 2.4 %shard_map.137 = (f32[512,2048]{1,0:T(8,128)S(1)}, f32[2048,512]{1,0:T(8,128)S(1)}, f32[2048,1]{1,0:T(8,128)S(1)}) custom-call(bf16[512,256]{1,0:T(8,128)(2,1)S(1)} %get-tuple-element.140.refs_0_, bf16[512,256]{1,0:T(8,128)(2,1)S(1)} %get-tuple-element.142.refs_1_, bf16[256,2048]{1,0:T(8,128)(2,1)S(1)} %get-tuple-element.143.refs_2_, ...), custom_call_target="tpu_custom_call" | custom-call | flops 2147483648 | tf_op jit(solution)/shard_map/pallas_call | solution.py:25
  97.7 6.9 %shard_map.139 = (f32[512,2048]{1,0:T(8,128)}, f32[2048,512]{1,0:T(8,128)}) custom-call(f32[1,128]{1,0:T(1,128)S(1)} %shard_map.118.energy_ref, s32[1]{0:T(128)} %bitcast.3.own_ref, f32[2048,1]{1,0:T(8,128)S(1)} %get-tuple-element.158.column_ref, f32[1,2048]{1,0:T(1,128)S(1)} %get-tuple-element.110.norms_ref.row_ref, ...), custom_call_target="tpu_custom_call" | custom-call | flops 3221225472 | tf_op jit(solution)/shard_map/pallas_call | solution.py:25
  (58 shorter events, 11.5 us)
Async XLA Ops:
  0.6 0.7 copy-start.2
  6.1 11.2 %collective-permute-start.5 = (bf16[32,2048]{1,0:T(8,128)(2,1)S(1)}, bf16[32,2048]{1,0:T(8,128)(2,1)S(1)}, u32[]{:S(2)}, u32[]{:S(2)}) collective-permute-start(bf16[32,2048]{1,0:T(8,128)(2,1)S(1)} %get-tuple-element.94.refs_0_), channel_id=1, source_target_pairs={{0,4},{1,3},{2,6},{3,1},{4,0},{5,7},{6,2},{7,5},{8,12},{9,11},{10,... | collective-permute-start | bytes 393224 | tf_op jit(solution)/shard_map/ppermute | solution.py:478
  10.2 3.5 %collective-permute-start = (f32[1,128]{1,0:T(1,128)S(1)}, f32[1,128]{1,0:T(1,128)S(1)}, u32[]{:S(2)}, u32[]{:S(2)}) collective-permute-start(f32[1,128]{1,0:T(1,128)S(1)} %get-tuple-element.90.a_ref), channel_id=1, source_target_pairs={{0,8},{1,17},{2,10},{3,19},{4,12},{5,21},{6,14},{7,23},{8,0},{9,25... | collective-permute-start | bytes 1544 | tf_op jit(solution)/shard_map/ppermute | solution.py:478
  13.7 3.5 %collective-permute-start.1 = (f32[1,128]{1,0:T(1,128)S(1)}, f32[1,128]{1,0:T(1,128)S(1)}, u32[]{:S(2)}, u32[]{:S(2)}) collective-permute-start(f32[1,128]{1,0:T(1,128)S(1)} %shard_map.113.a_ref), channel_id=1, source_target_pairs={{0,16},{1,9},{2,18},{3,11},{4,20},{5,13},{6,22},{7,15},{8,24},{9,1... | collective-permute-start | bytes 1544 | tf_op jit(solution)/shard_map/ppermute | solution.py:478
  17.3 10.8 %collective-permute-start.6 = (bf16[64,2048]{1,0:T(8,128)(2,1)S(1)}, bf16[64,2048]{1,0:T(8,128)(2,1)S(1)}, u32[]{:S(2)}, u32[]{:S(2)}) collective-permute-start(bf16[64,2048]{1,0:T(8,128)(2,1)S(1)} %shard_map.119.refs_0_.heads_ref), channel_id=1, source_target_pairs={{0,2},{1,5},{2,0},{3,7},{4,6},{5,1},{6,4},{7,3},{8,10},{9,13},{10,... | collective-permute-start | bytes 786440 | tf_op jit(solution)/shard_map/ppermute | solution.py:478
  19.0 1.1 %collective-permute-start.2 = (f32[1,128]{1,0:T(1,128)S(1)}, f32[1,128]{1,0:T(1,128)S(1)}, u32[]{:S(2)}, u32[]{:S(2)}) collective-permute-start(f32[1,128]{1,0:T(1,128)S(1)} %shard_map.114.a_ref), channel_id=1, source_target_pairs={{0,1},{1,0},{2,3},{3,2},{4,5},{5,4},{6,7},{7,6},{8,9},{9,8},{10,11... | collective-permute-start | bytes 1544 | tf_op jit(solution)/shard_map/ppermute | solution.py:478
  20.1 10.0 %copy-start = (f32[2048]{0:T(1024)S(1)}, f32[2048]{0:T(1024)}, u32[]{:S(2)}) copy-start(f32[2048]{0:T(1024)} %param.15) | copy-start | bytes 24580
  20.1 4.4 %collective-permute-start.3 = (f32[1,128]{1,0:T(1,128)S(1)}, f32[1,128]{1,0:T(1,128)S(1)}, u32[]{:S(2)}, u32[]{:S(2)}) collective-permute-start(f32[1,128]{1,0:T(1,128)S(1)} %shard_map.115.a_ref), channel_id=1, source_target_pairs={{0,4},{1,3},{2,6},{3,1},{4,0},{5,7},{6,2},{7,5},{8,12},{9,11},{10,... | collective-permute-start | bytes 1544 | tf_op jit(solution)/shard_map/ppermute | solution.py:478
  24.5 3.5 %collective-permute-start.4 = (f32[1,128]{1,0:T(1,128)S(1)}, f32[1,128]{1,0:T(1,128)S(1)}, u32[]{:S(2)}, u32[]{:S(2)}) collective-permute-start(f32[1,128]{1,0:T(1,128)S(1)} %shard_map.117.a_ref), channel_id=1, source_target_pairs={{0,2},{1,5},{2,0},{3,7},{4,6},{5,1},{6,4},{7,3},{8,10},{9,13},{10,... | collective-permute-start | bytes 1544 | tf_op jit(solution)/shard_map/ppermute | solution.py:478
  28.1 2.0 %collective-permute-start.7 = (bf16[128,2048]{1,0:T(8,128)(2,1)S(1)}, bf16[128,2048]{1,0:T(8,128)(2,1)S(1)}, u32[]{:S(2)}, u32[]{:S(2)}) collective-permute-start(bf16[128,2048]{1,0:T(8,128)(2,1)S(1)} %shard_map.120.refs_0_), channel_id=1, source_target_pairs={{0,1},{1,0},{2,3},{3,2},{4,5},{5,4},{6,7},{7,6},{8,9},{9,8},{10,11... | collective-permute-start | bytes 1572872 | tf_op jit(solution)/shard_map/ppermute | solution.py:478
  28.2 9.2 %collective-permute-start.8 = (bf16[128,2048]{1,0:T(8,128)(2,1)S(1)}, bf16[128,2048]{1,0:T(8,128)(2,1)S(1)}, u32[]{:S(2)}, u32[]{:S(2)}) collective-permute-start(bf16[128,2048]{1,0:T(8,128)(2,1)S(1)} %shard_map.120.refs_0_), channel_id=1, source_target_pairs={{0,8},{1,17},{2,10},{3,19},{4,12},{5,21},{6,14},{7,23},{8,0},{9,25... | collective-permute-start | bytes 1572872 | tf_op jit(solution)/shard_map/ppermute | solution.py:478
  37.4 2.7 %collective-permute-start.9 = (f32[128,2048]{1,0:T(8,128)S(1)}, f32[128,2048]{1,0:T(8,128)S(1)}, u32[]{:S(2)}, u32[]{:S(2)}) collective-permute-start(f32[128,2048]{1,0:T(8,128)S(1)} %get-tuple-element.99), channel_id=1, source_target_pairs={{0,1},{1,0},{2,3},{3,2},{4,5},{5,4},{6,7},{7,6},{8,9},{9,8},{10,11... | collective-permute-start | bytes 3145736 | tf_op jit(solution)/shard_map/ppermute | solution.py:478
  40.3 19.4 %copy-start.1 = (f32[2048]{0:T(1024)S(1)}, f32[2048]{0:T(1024)}, u32[]{:S(2)}) copy-start(f32[2048]{0:T(1024)} %param.17) | copy-start | bytes 24580
  40.3 19.4 %collective-permute-start.13 = (bf16[256,2048]{1,0:T(8,128)(2,1)S(1)}, bf16[256,2048]{1,0:T(8,128)(2,1)S(1)}, u32[]{:S(2)}, u32[]{:S(2)}) collective-permute-start(bf16[256,2048]{1,0:T(8,128)(2,1)S(1)} %shard_map.126), channel_id=1, source_target_pairs={{0,16},{1,9},{2,18},{3,11},{4,20},{5,13},{6,22},{7,15},{8,24},{9,1... | collective-permute-start | bytes 3145736 | tf_op jit(solution)/shard_map/ppermute | solution.py:478
  41.9 1.9 %collective-permute-start.11 = (bf16[128,2048]{1,0:T(8,128)(2,1)S(1)}, bf16[128,2048]{1,0:T(8,128)(2,1)S(1)}, u32[]{:S(2)}, u32[]{:S(2)}) collective-permute-start(bf16[128,2048]{1,0:T(8,128)(2,1)S(1)} %collective-permute-done.8.refs_0_.refs_1_), channel_id=1, source_target_pairs={{0,1},{1,0},{2,3},{3,2},{4,5},{5,4},{6,7},{7,6},{8,9},{9,8},{10,11... | collective-permute-start | bytes 1572872 | tf_op jit(solution)/shard_map/ppermute | solution.py:478
  41.9 8.1 %collective-permute-start.10 = (bf16[64,2048]{1,0:T(8,128)(2,1)S(1)}, bf16[64,2048]{1,0:T(8,128)(2,1)S(1)}, u32[]{:S(2)}, u32[]{:S(2)}) collective-permute-start(bf16[64,2048]{1,0:T(8,128)(2,1)S(1)} %get-tuple-element.101), channel_id=1, source_target_pairs={{0,2},{1,5},{2,0},{3,7},{4,6},{5,1},{6,4},{7,3},{8,10},{9,13},{10,... | collective-permute-start | bytes 786440 | tf_op jit(solution)/shard_map/ppermute | solution.py:478
  50.0 9.7 %collective-permute-start.12 = (bf16[64,2048]{1,0:T(8,128)(2,1)S(1)}, bf16[64,2048]{1,0:T(8,128)(2,1)S(1)}, u32[]{:S(2)}, u32[]{:S(2)}) collective-permute-start(bf16[64,2048]{1,0:T(8,128)(2,1)S(1)} %get-tuple-element.108), channel_id=1, source_target_pairs={{0,4},{1,3},{2,6},{3,1},{4,0},{5,7},{6,2},{7,5},{8,12},{9,11},{10,... | collective-permute-start | bytes 786440 | tf_op jit(solution)/shard_map/ppermute | solution.py:478
  59.9 2.8 %collective-permute-start.16 = (bf16[256,2048]{1,0:T(8,128)(2,1)S(1)}, bf16[256,2048]{1,0:T(8,128)(2,1)S(1)}, u32[]{:S(2)}, u32[]{:S(2)}) collective-permute-start(bf16[256,2048]{1,0:T(8,128)(2,1)S(1)} %collective-permute-done.13.refs_0_), channel_id=1, source_target_pairs={{0,1},{1,0},{2,3},{3,2},{4,5},{5,4},{6,7},{7,6},{8,9},{9,8},{10,11... | collective-permute-start | bytes 3145736 | tf_op jit(solution)/shard_map/ppermute | solution.py:478
  60.0 9.8 %collective-permute-start.14 = (bf16[64,2048]{1,0:T(8,128)(2,1)S(1)}, bf16[64,2048]{1,0:T(8,128)(2,1)S(1)}, u32[]{:S(2)}, u32[]{:S(2)}) collective-permute-start(bf16[64,2048]{1,0:T(8,128)(2,1)S(1)} %get-tuple-element.114.refs_0_), channel_id=1, source_target_pairs={{0,2},{1,5},{2,0},{3,7},{4,6},{5,1},{6,4},{7,3},{8,10},{9,13},{10,... | collective-permute-start | bytes 786440 | tf_op jit(solution)/shard_map/ppermute | solution.py:478
  61.2 8.6 %collective-permute-start.15 = (bf16[64,2048]{1,0:T(8,128)(2,1)S(1)}, bf16[64,2048]{1,0:T(8,128)(2,1)S(1)}, u32[]{:S(2)}, u32[]{:S(2)}) collective-permute-start(bf16[64,2048]{1,0:T(8,128)(2,1)S(1)} %get-tuple-element.114.refs_0_), channel_id=1, source_target_pairs={{0,8},{1,17},{2,10},{3,19},{4,12},{5,21},{6,14},{7,23},{8,0},{9,25... | collective-permute-start | bytes 786440 | tf_op jit(solution)/shard_map/ppermute | solution.py:478
  69.8 13.1 %copy-start.3 = (s32[32]{0:T(128)S(1)}, s32[32]{0:T(128)}, u32[]{:S(2)}) copy-start(s32[32]{0:T(128)} %param.13) | copy-start | bytes 388
  69.9 2.2 %collective-permute-start.19 = (bf16[128,2048]{1,0:T(8,128)(2,1)S(1)}, bf16[128,2048]{1,0:T(8,128)(2,1)S(1)}, u32[]{:S(2)}, u32[]{:S(2)}) collective-permute-start(bf16[128,2048]{1,0:T(8,128)(2,1)S(1)} %shard_map.130.refs_1_), channel_id=1, source_target_pairs={{0,1},{1,0},{2,3},{3,2},{4,5},{5,4},{6,7},{7,6},{8,9},{9,8},{10,11... | collective-permute-start | bytes 1572872 | tf_op jit(solution)/shard_map/ppermute | solution.py:478
  70.1 12.1 %collective-permute-start.21 = (bf16[128,2048]{1,0:T(8,128)(2,1)S(1)}, bf16[128,2048]{1,0:T(8,128)(2,1)S(1)}, u32[]{:S(2)}, u32[]{:S(2)}) collective-permute-start(bf16[128,2048]{1,0:T(8,128)(2,1)S(1)} %shard_map.135), channel_id=1, source_target_pairs={{0,16},{1,9},{2,18},{3,11},{4,20},{5,13},{6,22},{7,15},{8,24},{9,1... | collective-permute-start | bytes 1572872 | tf_op jit(solution)/shard_map/ppermute | solution.py:478
  70.9 9.2 %collective-permute-start.17 = (bf16[64,2048]{1,0:T(8,128)(2,1)S(1)}, bf16[64,2048]{1,0:T(8,128)(2,1)S(1)}, u32[]{:S(2)}, u32[]{:S(2)}) collective-permute-start(bf16[64,2048]{1,0:T(8,128)(2,1)S(1)} %collective-permute-done.14.refs_1_.refs_0_), channel_id=1, source_target_pairs={{0,8},{1,17},{2,10},{3,19},{4,12},{5,21},{6,14},{7,23},{8,0},{9,25... | collective-permute-start | bytes 786440 | tf_op jit(solution)/shard_map/ppermute | solution.py:478
  80.1 5.8 %collective-permute-start.20 = (bf16[128,2048]{1,0:T(8,128)(2,1)S(1)}, bf16[128,2048]{1,0:T(8,128)(2,1)S(1)}, u32[]{:S(2)}, u32[]{:S(2)}) collective-permute-start(bf16[128,2048]{1,0:T(8,128)(2,1)S(1)} %shard_map.134.refs_2_), channel_id=1, source_target_pairs={{0,1},{1,0},{2,3},{3,2},{4,5},{5,4},{6,7},{7,6},{8,9},{9,8},{10,11... | collective-permute-start | bytes 1572872 | tf_op jit(solution)/shard_map/ppermute | solution.py:478
  82.1 4.7 %collective-permute-start.22 = (bf16[128,2048]{1,0:T(8,128)(2,1)S(1)}, bf16[128,2048]{1,0:T(8,128)(2,1)S(1)}, u32[]{:S(2)}, u32[]{:S(2)}) collective-permute-start(bf16[128,2048]{1,0:T(8,128)(2,1)S(1)} %collective-permute-done.21.refs_4_), channel_id=1, source_target_pairs={{0,1},{1,0},{2,3},{3,2},{4,5},{5,4},{6,7},{7,6},{8,9},{9,8},{10,11... | collective-permute-start | bytes 1572872 | tf_op jit(solution)/shard_map/ppermute | solution.py:478
  82.2 12.2 %collective-permute-start.18 = (bf16[128,2048]{1,0:T(8,128)(2,1)S(1)}, bf16[128,2048]{1,0:T(8,128)(2,1)S(1)}, u32[]{:S(2)}, u32[]{:S(2)}) collective-permute-start(bf16[128,2048]{1,0:T(8,128)(2,1)S(1)} %shard_map.132), channel_id=1, source_target_pairs={{0,16},{1,9},{2,18},{3,11},{4,20},{5,13},{6,22},{7,15},{8,24},{9,1... | collective-permute-start | bytes 1572872 | tf_op jit(solution)/shard_map/ppermute | solution.py:478
  83.3 8.5 %collective-permute-start.23 = (f32[8,2176]{1,0:T(8,128)S(1)}, f32[8,2176]{1,0:T(8,128)S(1)}, u32[]{:S(2)}, u32[]{:S(2)}) collective-permute-start(f32[8,2176]{1,0:T(8,128)S(1)} %get-tuple-element.136), channel_id=1, source_target_pairs={{0,8},{1,9},{2,10},{3,11},{4,12},{5,13},{6,14},{7,15},{8,0},{9,1},... | collective-permute-start | bytes 208904 | tf_op jit(solution)/shard_map/ppermute | solution.py:478
  84.5 9.9 %collective-permute-start.24 = (f32[8,2176]{1,0:T(8,128)S(1)}, f32[8,2176]{1,0:T(8,128)S(1)}, u32[]{:S(2)}, u32[]{:S(2)}) collective-permute-start(f32[8,2176]{1,0:T(8,128)S(1)} %get-tuple-element.137), channel_id=1, source_target_pairs={{0,16},{1,17},{2,18},{3,19},{4,20},{5,21},{6,22},{7,23},{8,24},{9,... | collective-permute-start | bytes 208904 | tf_op jit(solution)/shard_map/ppermute | solution.py:478
  85.9 8.5 %collective-permute-start.25 = (f32[8,2176]{1,0:T(8,128)S(1)}, f32[8,2176]{1,0:T(8,128)S(1)}, u32[]{:S(2)}, u32[]{:S(2)}) collective-permute-start(f32[8,2176]{1,0:T(8,128)S(1)} %get-tuple-element.138), channel_id=1, source_target_pairs={{0,24},{1,25},{2,26},{3,27},{4,28},{5,29},{6,30},{7,31},{8,16},{9,... | collective-permute-start | bytes 208904 | tf_op jit(solution)/shard_map/ppermute | solution.py:478
  94.4 3.3 %collective-permute-start.26 = (bf16[128,2048]{1,0:T(8,128)(2,1)S(1)}, bf16[128,2048]{1,0:T(8,128)(2,1)S(1)}, u32[]{:S(2)}, u32[]{:S(2)}) collective-permute-start(bf16[128,2048]{1,0:T(8,128)(2,1)S(1)} %collective-permute-done.18.refs_4_), channel_id=1, source_target_pairs={{0,1},{1,0},{2,3},{3,2},{4,5},{5,4},{6,7},{7,6},{8,9},{9,8},{10,11... | collective-permute-start | bytes 1572872 | tf_op jit(solution)/shard_map/ppermute | solution.py:478

commit v4 on v3

--- a/solution.py
+++ b/solution.py
@@ -190,7 +190,8 @@
     count = sum(piece.shape[0] for piece in pieces)
     out = [half_array(count, pieces[0].shape[1])]
     body = functools.partial(join_body, halves)
-    return kernel_call(body, pieces, [IN_VMEM] * len(pieces), out, limit=4)[0]
+    limit = 4 + max(0, count - 256) // 64
+    return kernel_call(body, pieces, [IN_VMEM] * len(pieces), out, limit=limit)[0]
 
 
 def add_split_body(a_ref, b_ref, keep_ref, send_ref):
@@ -359,36 +360,58 @@
         [half_array(count, latents) for count in counts] + [half_array(count, columns) for count in counts],
         [pltpu.VMEM((count, width), jnp.bfloat16) for count in counts],
         flops=2 * sum(counts) * width * latents,
+        limit=12 + max(0, sum(counts) - 512) // 32,
     )
     return list(zip(outs[: len(sets)], outs[len(sets) :], strict=True))
 
 
-def early_body(groups, tile, *refs):
-    rows, grads, coded, residual = (refs[i * groups : (i + 1) * groups] for i in range(4))
-    enc_ref, dec_ref, sums_ref = refs[4 * groups :]
-    for first in range(0, enc_ref.shape[1], tile):
+def early_body(cuts, given, tile, all_rows, own_ref, dec_ref, norms_ref, *refs):
+    sets = len(cuts)
+    rows, coded, slopes, refs = refs[: sets + given], refs[sets + given : 2 * (sets + given)], refs[2 * (sets + given) :][:sets], refs[2 * (sets + given) + sets :]
+    grads, parts, refs = refs[:given], refs[given : 2 * given], refs[2 * given :]
+    pieces = []
+    for chosen in cuts:
+        pieces.append(refs[: len(chosen)])
+        refs = refs[len(chosen) :]
+    (enc_ref, dec_sum, sums_ref), scratch = refs[:3], refs[3:]
+    residuals, own_parts = scratch[:sets], scratch[sets:]
+    for chosen, piece, residual, part in zip(cuts, pieces, residuals, own_parts, strict=True):
+        join(piece, residual, chosen)
+        part[...] = own_columns(residual, own_ref, part.shape[1])
+    for first in range(0, dec_ref.shape[0], tile):
         here = slice(first, first + tile)
+        made = [
+            pre_tile(residual, dec_ref, norms_ref, slope_ref, here, all_rows)
+            for residual, slope_ref in zip(residuals, slopes, strict=True)
+        ]
         enc, dec, sums = 0.0, 0.0, 0.0
-        for g in range(groups):
-            enc = enc + jnp.dot(rows[g][...], grads[g][:, here], preferred_element_type=jnp.float32)
-            dec = dec + jnp.dot(coded[g][here, :], residual[g][...], preferred_element_type=jnp.float32)
-            sums = sums + jnp.sum(coded[g][here, :].astype(jnp.float32), axis=1, keepdims=True)
+        for rows_set, grad in zip(rows, [grad[:, here] for grad in grads] + made, strict=True):
+            enc = enc + jnp.dot(rows_set[...], grad, preferred_element_type=jnp.float32)
+        for coded_set, part in zip(coded, (*parts, *own_parts), strict=True):
+            dec = dec + jnp.dot(coded_set[here, :], part[...], preferred_element_type=jnp.float32)
+            sums = sums + jnp.sum(coded_set[here, :].astype(jnp.float32), axis=1, keepdims=True)
         enc_ref[:, here] = enc
-        dec_ref[here, :] = dec
+        dec_sum[here, :] = dec
         sums_ref[here, :] = sums
 
 
-def early_sums(rows, grads, coded, residual):
-    columns = rows[0].shape[0]
-    latents = coded[0].shape[0]
-    count = sum(x.shape[0] for x in grads)
-    args = [*rows, *grads, *coded, *residual]
+def early_sums(all_rows, own, dec, norms, encoded, grads, sets):
+    latents, width = dec.shape
+    columns = encoded[0][2].shape[0]
+    cut_sets = [cut_pieces(pieces) for pieces in sets]
+    counts = [sum(size for _, size in cuts) for _, cuts in cut_sets]
+    args = [held(dec), norms, *(x[2] for x in encoded), *(x[0] for x in encoded)]
+    args += [x[1] for x in encoded[len(grads) :]] + [x[0] for x in grads] + [x[1] for x in grads]
+    args += [part for parts, _ in cut_sets for part in parts]
     return kernel_call(
-        functools.partial(early_body, len(rows), min(512, latents)),
-        args,
-        [IN_VMEM] * len(args),
+        functools.partial(early_body, [cuts for _, cuts in cut_sets], len(grads), min(512, latents), all_rows),
+        [own, *args],
+        [IN_SMEM] + [IN_VMEM] * len(args),
         [float_array(columns, latents), float_array(latents, columns), float_array(latents, 1)],
-        flops=4 * count * columns * latents,
+        [pltpu.VMEM((count, width), jnp.bfloat16) for count in counts]
+        + [pltpu.VMEM((count, columns), jnp.bfloat16) for count in counts],
+        flops=2 * sum(counts) * width * latents,
+        limit=16 + max(0, sum(counts) - 512) // 32,
     )
 
 
@@ -635,12 +658,13 @@
         rows = joined(rows, swap(rows, *mask))
     near, late = [rows], [swap(rows, *line[-1])]
     near.append(swap(rows, *plane[0]))
-    done = []
+    moved = send_rows(own, after(rebuilt_own, rows), places)
+    waiting = []
     for piece, other in zip(far[2:], others, strict=True):
         half = piece.shape[0] // 2
-        for first in (0, half):
-            done += [encode_next(parts, rows) for parts in chunks(piece, other, first, half)]
-    late[0] = after(late[0], near[1], *done)
+        waiting += chunks(piece, other, 0, half) + chunks(piece, other, half, half)
+    done = [encode_next(parts, rows) for parts in waiting[:-1]]
+    late[0] = after(late[0], near[1], *done, *moved)
     grads = []
 
     def pre(sets, now):
@@ -657,11 +681,9 @@
     near.append(swap(joined(*near), *plane[1]))
     rows = joined(near[0], late[0])
     done = pre([whole([rows, swap(rows, *core)])], rows)
-    moved = send_rows(own, after(rebuilt_own, rows), places)
     near[2] = after(near[2], done)
-    hop = joined(near[1], after(late[1], done))
+    hop = joined(near[1], after(late[1], done, encode_next(waiting[-1], rows)))
     sets = [whole([hop, swap(hop, *core)])]
-    count = 2
     for number, step in enumerate(plane[1:], 1):
         if number > 1:
             near.append(swap(joined(*near), *step))
@@ -669,14 +691,17 @@
         sets += chunks(near[-1], swap(near[-1], *core), 0, near[-1].shape[0])
         if number < len(plane) - 1:
             sets += chunks(late[-1], swap(late[-1], *core), 0, late[-1].shape[0])
-            count += 2 * len(chunks(near[-1], near[-1], 0, near[-1].shape[0]))
-    for first in range(0, len(sets), 2):
+    for first in range(0, len(sets) - 2, 2):
         done = pre(sets[first : first + 2], hop)
-    last = after(late[-1], done, *moved)
+    count = len(grads)
+    sets = [[(after(part, hop), *cut) for part, *cut in parts] for parts in sets[count - 1 :]]
+    early = early_sums(all_rows, own, dec, norms_row, encoded[: count + len(sets)], grads, sets)
+    count += len(sets)
+    grads += [None] * len(sets)
+    last = after(late[-1], early[0])
     sets = chunks(last, swap(last, *core), 0, last.shape[0])
     for parts in sets[:-1]:
-        done = pre([parts], done)
-    early = early_sums(*([after(x, last) for x in kind] for kind in zip(*ready(range(count)), strict=True)))
+        pre([parts], last)
     grad_enc, grad_dec = weight_gradients(
         all_rows,
         entries,

time: 105 us -> 101 us (0.962)
  waiting for transfers between devices: 32.5 us -> 27.7 us
    ppermute x27, waiting for transfers between devices: 32.5 us -> 27.7 us  [swap(): lax.ppermute(x, ('dp', 'latent'), [(i, i ^ (odd if i & 1 else even)) for...]
    pallas_call x28 -> x27, Pallas kernels: 45.3 us -> 45.7 us  [kernel_call(): pl.pallas_call(body, in_specs=specs, out_specs=out_specs or [IN_VMEM] * l...]
  transfers between devices with their start and end apart: 27 -> 27, of which waited for: 14 -> 15; matrix products, arithmetic and copies ran while one was open for 0% -> 0% of each run, Pallas kernels for 32% -> 34%
where the time goes in v4:
time: 101 us
  Pallas kernels  45.7 us (45%)
  waiting for transfers between devices  27.7 us (27%)
  starting transfers between devices  25.9 us (26%)
  between operations  1.04 us (1%)
    pallas_call x27, Pallas kernels, kernel_call(): pl.pallas_call(body, in_specs=specs, out_specs=out_specs or [IN_VMEM] * l...  45.7 us
    ppermute x27, waiting for transfers between devices, swap(): lax.ppermute(x, ('dp', 'latent'), [(i, i ^ (odd if i & 1 else even)) for...  27.7 us
    ppermute x27, starting transfers between devices, swap(): lax.ppermute(x, ('dp', 'latent'), [(i, i ^ (odd if i & 1 else even)) for...  25.9 us
  transfers between devices with their start and end apart: 27, of which 15 were waited for; matrix products, arithmetic and copies ran while one was open for 0% of the time, Pallas kernels for 34%

profile of v4, /device:TPU:0, one launch (start us, length us, event | category | flops | bytes accessed | tf_op | source)
XLA Modules:
  0.0 101.0 jit_solution(15079990727982271673)
XLA Ops:
  1.3 4.8 %shard_map.112 = (bf16[32,2048]{1,0:T(8,128)(2,1)S(1)}, f32[1,128]{1,0:T(1,128)S(1)}, bf16[2048,2048]{1,0:T(8,128)(2,1)S(1)}) custom-call(s32[32]{0:T(128)S(1)} %copy-done.2, bf16[32,2048]{1,0:T(8,128)(2,1)} %queries.1, bf16[1,512,1024]{2,1,0:T(8,128)(2,1)} %keys.1, bf16[1,512,1024]{2,1,0:T(8,128)(2,1)} %values.1, bf16[2048,2048]{1,0:T(8,128)(2,1)} %enc), custom_call_target="tpu_custom_call" | custom-call | flops 134217728 | tf_op jit(solution)/shard_map/pallas_call | solution.py:25
  6.1 4.1 %collective-permute-start.5 = (bf16[32,2048]{1,0:T(8,128)(2,1)S(1)}, bf16[32,2048]{1,0:T(8,128)(2,1)S(1)}, u32[]{:S(2)}, u32[]{:S(2)}) collective-permute-start(bf16[32,2048]{1,0:T(8,128)(2,1)S(1)} %get-tuple-element.84.refs_0_), channel_id=1, source_target_pairs={{0,4},{1,3},{2,6},{3,1},{4,0},{5,7},{6,2},{7,5},{8,12},{9,11},{10,... | collective-permute-start | bytes 393224 | tf_op jit(solution)/shard_map/ppermute | solution.py:501
  10.2 1.5 %collective-permute-start = (f32[1,128]{1,0:T(1,128)S(1)}, f32[1,128]{1,0:T(1,128)S(1)}, u32[]{:S(2)}, u32[]{:S(2)}) collective-permute-start(f32[1,128]{1,0:T(1,128)S(1)} %get-tuple-element.80.a_ref), channel_id=1, source_target_pairs={{0,8},{1,17},{2,10},{3,19},{4,12},{5,21},{6,14},{7,23},{8,0},{9,25... | collective-permute-start | bytes 1544 | tf_op jit(solution)/shard_map/ppermute | solution.py:501
  11.7 2.0 %collective-permute-done.b_ref = f32[1,128]{1,0:T(1,128)S(1)} collective-permute-done((f32[1,128]{1,0:T(1,128)S(1)}, f32[1,128]{1,0:T(1,128)S(1)}, u32[]{:S(2)}, u32[]{:S(2)}) %collective-permute-start) | collective-permute-done | bytes 544 | tf_op jit(solution)/shard_map/ppermute | solution.py:501
  13.7 1.5 %collective-permute-start.1 = (f32[1,128]{1,0:T(1,128)S(1)}, f32[1,128]{1,0:T(1,128)S(1)}, u32[]{:S(2)}, u32[]{:S(2)}) collective-permute-start(f32[1,128]{1,0:T(1,128)S(1)} %shard_map.113.a_ref), channel_id=1, source_target_pairs={{0,16},{1,9},{2,18},{3,11},{4,20},{5,13},{6,22},{7,15},{8,24},{9,1... | collective-permute-start | bytes 1544 | tf_op jit(solution)/shard_map/ppermute | solution.py:501
  15.3 2.0 %collective-permute-done.1.b_ref = f32[1,128]{1,0:T(1,128)S(1)} collective-permute-done((f32[1,128]{1,0:T(1,128)S(1)}, f32[1,128]{1,0:T(1,128)S(1)}, u32[]{:S(2)}, u32[]{:S(2)}) %collective-permute-start.1) | collective-permute-done | bytes 544 | tf_op jit(solution)/shard_map/ppermute | solution.py:501
  17.3 1.6 %collective-permute-start.6 = (bf16[64,2048]{1,0:T(8,128)(2,1)S(1)}, bf16[64,2048]{1,0:T(8,128)(2,1)S(1)}, u32[]{:S(2)}, u32[]{:S(2)}) collective-permute-start(bf16[64,2048]{1,0:T(8,128)(2,1)S(1)} %shard_map.119.refs_0_.heads_ref), channel_id=1, source_target_pairs={{0,2},{1,5},{2,0},{3,7},{4,6},{5,1},{6,4},{7,3},{8,10},{9,13},{10,... | collective-permute-start | bytes 786440 | tf_op jit(solution)/shard_map/ppermute | solution.py:501
  20.4 3.5 %shard_map.116.dec_ref = bf16[2048,2048]{1,0:T(8,128)(2,1)S(1)} custom-call(bf16[2048,2048]{1,0:T(8,128)(2,1)} %source), custom_call_target="tpu_custom_call" | custom-call | tf_op jit(solution)/shard_map/pallas_call | solution.py:25
  25.0 3.1 %collective-permute-done.4.b_ref = f32[1,128]{1,0:T(1,128)S(1)} collective-permute-done((f32[1,128]{1,0:T(1,128)S(1)}, f32[1,128]{1,0:T(1,128)S(1)}, u32[]{:S(2)}, u32[]{:S(2)}) %collective-permute-start.4) | collective-permute-done | bytes 544 | tf_op jit(solution)/shard_map/ppermute | solution.py:501
  28.2 1.6 %collective-permute-start.8 = (bf16[128,2048]{1,0:T(8,128)(2,1)S(1)}, bf16[128,2048]{1,0:T(8,128)(2,1)S(1)}, u32[]{:S(2)}, u32[]{:S(2)}) collective-permute-start(bf16[128,2048]{1,0:T(8,128)(2,1)S(1)} %shard_map.120.refs_0_), channel_id=1, source_target_pairs={{0,8},{1,17},{2,10},{3,19},{4,12},{5,21},{6,14},{7,23},{8,0},{9,25... | collective-permute-start | bytes 1572872 | tf_op jit(solution)/shard_map/ppermute | solution.py:501
  30.1 5.6 %shard_map.121 = (bf16[2048,256]{1,0:T(8,128)(2,1)S(1)}, bf16[256,2048]{1,0:T(8,128)(2,1)S(1)}, bf16[512,256]{1,0:T(8,128)(2,1)S(1)}, f32[128,2048]{1,0:T(8,128)S(1)}, f32[128,2048]{1,0:T(8,128)S(1)}) custom-call(f32[1,128]{1,0:T(1,128)S(1)} %shard_map.118.energy_ref, s32[1]{0:T(128)} %bitcast.3.own_ref, bf16[2048,2048]{1,0:T(8,128)(2,1)S(1)} %get-tuple-element.83.enc_ref, ...), custom_call_target="tpu_custom_call" | custom-call | flops 4294967296 | tf_op jit(solution)/shard_map/pallas_call | solution.py:25
  35.7 1.8 %collective-permute-done.8.refs_0_.refs_1_ = bf16[128,2048]{1,0:T(8,128)(2,1)S(1)} collective-permute-done((bf16[128,2048]{1,0:T(8,128)(2,1)S(1)}, bf16[128,2048]{1,0:T(8,128)(2,1)S(1)}, u32[]{:S(2)}, u32[]{:S(2)}) %collective-permute-start.8) | collective-permute-done | bytes 524320 | tf_op jit(solution)/shard_map/ppermute | solution.py:501
  37.4 2.7 %collective-permute-done.9.b_ref = f32[128,2048]{1,0:T(8,128)S(1)} collective-permute-done((f32[128,2048]{1,0:T(8,128)S(1)}, f32[128,2048]{1,0:T(8,128)S(1)}, u32[]{:S(2)}, u32[]{:S(2)}) %collective-permute-start.9) | collective-permute-done | bytes 1048608 | tf_op jit(solution)/shard_map/ppermute | solution.py:501
  40.3 1.6 %collective-permute-start.13 = (bf16[256,2048]{1,0:T(8,128)(2,1)S(1)}, bf16[256,2048]{1,0:T(8,128)(2,1)S(1)}, u32[]{:S(2)}, u32[]{:S(2)}) collective-permute-start(bf16[256,2048]{1,0:T(8,128)(2,1)S(1)} %shard_map.126), channel_id=1, source_target_pairs={{0,16},{1,9},{2,18},{3,11},{4,20},{5,13},{6,22},{7,15},{8,24},{9,1... | collective-permute-start | bytes 3145736 | tf_op jit(solution)/shard_map/ppermute | solution.py:501
  42.6 1.2 %collective-permute-done.11.refs_1_ = bf16[128,2048]{1,0:T(8,128)(2,1)S(1)} collective-permute-done((bf16[128,2048]{1,0:T(8,128)(2,1)S(1)}, bf16[128,2048]{1,0:T(8,128)(2,1)S(1)}, u32[]{:S(2)}, u32[]{:S(2)}) %collective-permute-start.11) | collective-permute-done | bytes 524320 | tf_op jit(solution)/shard_map/ppermute | solution.py:501
  43.8 3.5 %shard_map.123 = (bf16[2048,256]{1,0:T(8,128)(2,1)S(1)}, bf16[256,2048]{1,0:T(8,128)(2,1)S(1)}, bf16[512,256]{1,0:T(8,128)(2,1)S(1)}) custom-call(f32[1,128]{1,0:T(1,128)S(1)} %shard_map.118.energy_ref, s32[1]{0:T(128)} %bitcast.3.own_ref, bf16[2048,2048]{1,0:T(8,128)(2,1)S(1)} %get-tuple-element.83.enc_ref, f32[1,2048]{1,0:T(1,128)S(1)} %bitcast.5, ...), custom_call_target="tpu_custom_call" | custom-call | flops 2147483648 | tf_op jit(solution)/shard_map/pallas_call | solution.py:25
  47.4 2.6 %collective-permute-done.10.b_ref = bf16[64,2048]{1,0:T(8,128)(2,1)S(1)} collective-permute-done((bf16[64,2048]{1,0:T(8,128)(2,1)S(1)}, bf16[64,2048]{1,0:T(8,128)(2,1)S(1)}, u32[]{:S(2)}, u32[]{:S(2)}) %collective-permute-start.10) | collective-permute-done | bytes 262176 | tf_op jit(solution)/shard_map/ppermute | solution.py:501
  50.1 2.3 %collective-permute-start.12 = (bf16[64,2048]{1,0:T(8,128)(2,1)S(1)}, bf16[64,2048]{1,0:T(8,128)(2,1)S(1)}, u32[]{:S(2)}, u32[]{:S(2)}) collective-permute-start(bf16[64,2048]{1,0:T(8,128)(2,1)S(1)} %get-tuple-element.98), channel_id=1, source_target_pairs={{0,4},{1,3},{2,6},{3,1},{4,0},{5,7},{6,2},{7,5},{8,12},{9,11},{10,... | collective-permute-start | bytes 786440 | tf_op jit(solution)/shard_map/ppermute | solution.py:501
  52.4 2.3 %shard_map.125 = (f32[2048,1]{1,0:T(8,128)S(1)}, f32[1,2048]{1,0:T(1,128)S(1)}) custom-call(bf16[2048,2048]{1,0:T(8,128)(2,1)S(1)} %shard_map.116.dec_ref), custom_call_target="tpu_custom_call" | custom-call | tf_op jit(solution)/shard_map/pallas_call | solution.py:25
  54.7 5.1 %collective-permute-done.12.b_ref = bf16[64,2048]{1,0:T(8,128)(2,1)S(1)} collective-permute-done((bf16[64,2048]{1,0:T(8,128)(2,1)S(1)}, bf16[64,2048]{1,0:T(8,128)(2,1)S(1)}, u32[]{:S(2)}, u32[]{:S(2)}) %collective-permute-start.12) | collective-permute-done | bytes 262176 | tf_op jit(solution)/shard_map/ppermute | solution.py:501
  60.0 1.5 %collective-permute-start.16 = (bf16[64,2048]{1,0:T(8,128)(2,1)S(1)}, bf16[64,2048]{1,0:T(8,128)(2,1)S(1)}, u32[]{:S(2)}, u32[]{:S(2)}) collective-permute-start(bf16[64,2048]{1,0:T(8,128)(2,1)S(1)} %get-tuple-element.107.refs_0_), channel_id=1, source_target_pairs={{0,8},{1,17},{2,10},{3,19},{4,12},{5,21},{6,14},{7,23},{8,0},{9,25... | collective-permute-start | bytes 786440 | tf_op jit(solution)/shard_map/ppermute | solution.py:501
  61.6 1.2 %collective-permute-start.15 = (bf16[64,2048]{1,0:T(8,128)(2,1)S(1)}, bf16[64,2048]{1,0:T(8,128)(2,1)S(1)}, u32[]{:S(2)}, u32[]{:S(2)}) collective-permute-start(bf16[64,2048]{1,0:T(8,128)(2,1)S(1)} %get-tuple-element.107.refs_0_), channel_id=1, source_target_pairs={{0,2},{1,5},{2,0},{3,7},{4,6},{5,1},{6,4},{7,3},{8,10},{9,13},{10,... | collective-permute-start | bytes 786440 | tf_op jit(solution)/shard_map/ppermute | solution.py:501
  63.7 1.3 %collective-permute-start.18 = (f32[8,2176]{1,0:T(8,128)S(1)}, f32[8,2176]{1,0:T(8,128)S(1)}, u32[]{:S(2)}, u32[]{:S(2)}) collective-permute-start(f32[8,2176]{1,0:T(8,128)S(1)} %get-tuple-element.117), channel_id=1, source_target_pairs={{0,16},{1,17},{2,18},{3,19},{4,20},{5,21},{6,22},{7,23},{8,24},{9,... | collective-permute-start | bytes 208904 | tf_op jit(solution)/shard_map/ppermute | solution.py:501
  65.0 1.6 %collective-permute-start.19 = (f32[8,2176]{1,0:T(8,128)S(1)}, f32[8,2176]{1,0:T(8,128)S(1)}, u32[]{:S(2)}, u32[]{:S(2)}) collective-permute-start(f32[8,2176]{1,0:T(8,128)S(1)} %get-tuple-element.118), channel_id=1, source_target_pairs={{0,24},{1,25},{2,26},{3,27},{4,28},{5,29},{6,30},{7,31},{8,16},{9,... | collective-permute-start | bytes 208904 | tf_op jit(solution)/shard_map/ppermute | solution.py:501
  66.6 3.5 %shard_map.129 = (bf16[2048,256]{1,0:T(8,128)(2,1)S(1)}, bf16[256,2048]{1,0:T(8,128)(2,1)S(1)}, bf16[512,256]{1,0:T(8,128)(2,1)S(1)}) custom-call(f32[1,128]{1,0:T(1,128)S(1)} %shard_map.118.energy_ref, s32[1]{0:T(128)} %bitcast.3.own_ref, bf16[2048,2048]{1,0:T(8,128)(2,1)S(1)} %get-tuple-element.83.enc_ref, f32[1,2048]{1,0:T(1,128)S(1)} %bitcast.6, ...), custom_call_target="tpu_custom_call" | custom-call | flops 2147483648 | tf_op jit(solution)/shard_map/pallas_call | solution.py:25
  71.5 1.1 %collective-permute-start.21 = (bf16[64,2048]{1,0:T(8,128)(2,1)S(1)}, bf16[64,2048]{1,0:T(8,128)(2,1)S(1)}, u32[]{:S(2)}, u32[]{:S(2)}) collective-permute-start(bf16[64,2048]{1,0:T(8,128)(2,1)S(1)} %collective-permute-done.15.refs_1_.refs_0_), channel_id=1, source_target_pairs={{0,8},{1,17},{2,10},{3,19},{4,12},{5,21},{6,14},{7,23},{8,0},{9,25... | collective-permute-start | bytes 786440 | tf_op jit(solution)/shard_map/ppermute | solution.py:501
  72.6 3.5 %shard_map.132 = (bf16[2048,256]{1,0:T(8,128)(2,1)S(1)}, bf16[256,2048]{1,0:T(8,128)(2,1)S(1)}, bf16[512,256]{1,0:T(8,128)(2,1)S(1)}) custom-call(f32[1,128]{1,0:T(1,128)S(1)} %shard_map.118.energy_ref, s32[1]{0:T(128)} %bitcast.3.own_ref, bf16[2048,2048]{1,0:T(8,128)(2,1)S(1)} %get-tuple-element.83.enc_ref, f32[1,2048]{1,0:T(1,128)S(1)} %bitcast.7, ...), custom_call_target="tpu_custom_call" | custom-call | flops 2147483648 | tf_op jit(solution)/shard_map/pallas_call | solution.py:25
  76.2 2.5 %shard_map.131 = (bf16[256,2048]{1,0:T(8,128)(2,1)S(1)}, bf16[256,512]{1,0:T(8,128)(2,1)S(1)}) custom-call(s32[1]{0:T(128)} %bitcast.3.own_ref, bf16[2048,2048]{1,0:T(8,128)(2,1)S(1)} %shard_map.116.dec_ref, f32[1,2048]{1,0:T(1,128)S(1)} %get-tuple-element.100.norms_ref.row_ref, bf16[256,2048]{1,0:T(8,128)(2,1)S(1)} %get-tuple-element.115.refs_0_, ...), custom_call_target="tpu_custom_call" | custom-call | flops 2147483648 | tf_op jit(solution)/shard_map/pallas_call | solution.py:25
  78.7 2.0 %collective-permute-done.21.refs_1_ = bf16[64,2048]{1,0:T(8,128)(2,1)S(1)} collective-permute-done((bf16[64,2048]{1,0:T(8,128)(2,1)S(1)}, bf16[64,2048]{1,0:T(8,128)(2,1)S(1)}, u32[]{:S(2)}, u32[]{:S(2)}) %collective-permute-start.21) | collective-permute-done | bytes 262176 | tf_op jit(solution)/shard_map/ppermute | solution.py:501
  80.8 1.6 %collective-permute-done.23.refs_12_ = bf16[128,2048]{1,0:T(8,128)(2,1)S(1)} collective-permute-done((bf16[128,2048]{1,0:T(8,128)(2,1)S(1)}, bf16[128,2048]{1,0:T(8,128)(2,1)S(1)}, u32[]{:S(2)}, u32[]{:S(2)}) %collective-permute-start.23) | collective-permute-done | bytes 524320 | tf_op jit(solution)/shard_map/ppermute | solution.py:501
  84.3 8.3 %shard_map.135 = (f32[512,2048]{1,0:T(8,128)S(1)}, f32[2048,512]{1,0:T(8,128)S(1)}, f32[2048,1]{1,0:T(8,128)S(1)}) custom-call(s32[1]{0:T(128)} %bitcast.3.own_ref, bf16[2048,2048]{1,0:T(8,128)(2,1)S(1)} %shard_map.116.dec_ref, f32[1,2048]{1,0:T(1,128)S(1)} %get-tuple-element.100.norms_ref.row_ref, bf16[512,256]{1,0:T(8,128)(2,1)S(1)} %get-tuple-element.105.refs_0_, ...), custom_call_target="tpu_custom_call" | custom-call | flops 4294967296 | tf_op jit(solution)/shard_map/pallas_call | solution.py:25
  94.6 6.2 %shard_map.138 = (f32[512,2048]{1,0:T(8,128)}, f32[2048,512]{1,0:T(8,128)}) custom-call(f32[1,128]{1,0:T(1,128)S(1)} %shard_map.118.energy_ref, s32[1]{0:T(128)} %bitcast.3.own_ref, f32[2048,1]{1,0:T(8,128)S(1)} %get-tuple-element.138.column_ref, f32[1,2048]{1,0:T(1,128)S(1)} %get-tuple-element.100.norms_ref.row_ref, ...), custom_call_target="tpu_custom_call" | custom-call | flops 3221225472 | tf_op jit(solution)/shard_map/pallas_call | solution.py:25
  (57 shorter events, 11.1 us)
Async XLA Ops:
  0.6 0.7 copy-start.2
  6.1 11.2 %collective-permute-start.5 = (bf16[32,2048]{1,0:T(8,128)(2,1)S(1)}, bf16[32,2048]{1,0:T(8,128)(2,1)S(1)}, u32[]{:S(2)}, u32[]{:S(2)}) collective-permute-start(bf16[32,2048]{1,0:T(8,128)(2,1)S(1)} %get-tuple-element.84.refs_0_), channel_id=1, source_target_pairs={{0,4},{1,3},{2,6},{3,1},{4,0},{5,7},{6,2},{7,5},{8,12},{9,11},{10,... | collective-permute-start | bytes 393224 | tf_op jit(solution)/shard_map/ppermute | solution.py:501
  10.2 3.5 %collective-permute-start = (f32[1,128]{1,0:T(1,128)S(1)}, f32[1,128]{1,0:T(1,128)S(1)}, u32[]{:S(2)}, u32[]{:S(2)}) collective-permute-start(f32[1,128]{1,0:T(1,128)S(1)} %get-tuple-element.80.a_ref), channel_id=1, source_target_pairs={{0,8},{1,17},{2,10},{3,19},{4,12},{5,21},{6,14},{7,23},{8,0},{9,25... | collective-permute-start | bytes 1544 | tf_op jit(solution)/shard_map/ppermute | solution.py:501
  13.7 3.5 %collective-permute-start.1 = (f32[1,128]{1,0:T(1,128)S(1)}, f32[1,128]{1,0:T(1,128)S(1)}, u32[]{:S(2)}, u32[]{:S(2)}) collective-permute-start(f32[1,128]{1,0:T(1,128)S(1)} %shard_map.113.a_ref), channel_id=1, source_target_pairs={{0,16},{1,9},{2,18},{3,11},{4,20},{5,13},{6,22},{7,15},{8,24},{9,1... | collective-permute-start | bytes 1544 | tf_op jit(solution)/shard_map/ppermute | solution.py:501
  17.3 10.8 %collective-permute-start.6 = (bf16[64,2048]{1,0:T(8,128)(2,1)S(1)}, bf16[64,2048]{1,0:T(8,128)(2,1)S(1)}, u32[]{:S(2)}, u32[]{:S(2)}) collective-permute-start(bf16[64,2048]{1,0:T(8,128)(2,1)S(1)} %shard_map.119.refs_0_.heads_ref), channel_id=1, source_target_pairs={{0,2},{1,5},{2,0},{3,7},{4,6},{5,1},{6,4},{7,3},{8,10},{9,13},{10,... | collective-permute-start | bytes 786440 | tf_op jit(solution)/shard_map/ppermute | solution.py:501
  19.0 1.1 %collective-permute-start.2 = (f32[1,128]{1,0:T(1,128)S(1)}, f32[1,128]{1,0:T(1,128)S(1)}, u32[]{:S(2)}, u32[]{:S(2)}) collective-permute-start(f32[1,128]{1,0:T(1,128)S(1)} %shard_map.114.a_ref), channel_id=1, source_target_pairs={{0,1},{1,0},{2,3},{3,2},{4,5},{5,4},{6,7},{7,6},{8,9},{9,8},{10,11... | collective-permute-start | bytes 1544 | tf_op jit(solution)/shard_map/ppermute | solution.py:501
  20.1 10.0 %copy-start = (f32[2048]{0:T(1024)S(1)}, f32[2048]{0:T(1024)}, u32[]{:S(2)}) copy-start(f32[2048]{0:T(1024)} %param.15) | copy-start | bytes 24580
  20.1 4.4 %collective-permute-start.3 = (f32[1,128]{1,0:T(1,128)S(1)}, f32[1,128]{1,0:T(1,128)S(1)}, u32[]{:S(2)}, u32[]{:S(2)}) collective-permute-start(f32[1,128]{1,0:T(1,128)S(1)} %shard_map.115.a_ref), channel_id=1, source_target_pairs={{0,4},{1,3},{2,6},{3,1},{4,0},{5,7},{6,2},{7,5},{8,12},{9,11},{10,... | collective-permute-start | bytes 1544 | tf_op jit(solution)/shard_map/ppermute | solution.py:501
  24.5 3.5 %collective-permute-start.4 = (f32[1,128]{1,0:T(1,128)S(1)}, f32[1,128]{1,0:T(1,128)S(1)}, u32[]{:S(2)}, u32[]{:S(2)}) collective-permute-start(f32[1,128]{1,0:T(1,128)S(1)} %shard_map.117.a_ref), channel_id=1, source_target_pairs={{0,2},{1,5},{2,0},{3,7},{4,6},{5,1},{6,4},{7,3},{8,10},{9,13},{10,... | collective-permute-start | bytes 1544 | tf_op jit(solution)/shard_map/ppermute | solution.py:501
  28.1 2.0 %collective-permute-start.7 = (bf16[128,2048]{1,0:T(8,128)(2,1)S(1)}, bf16[128,2048]{1,0:T(8,128)(2,1)S(1)}, u32[]{:S(2)}, u32[]{:S(2)}) collective-permute-start(bf16[128,2048]{1,0:T(8,128)(2,1)S(1)} %shard_map.120.refs_0_), channel_id=1, source_target_pairs={{0,1},{1,0},{2,3},{3,2},{4,5},{5,4},{6,7},{7,6},{8,9},{9,8},{10,11... | collective-permute-start | bytes 1572872 | tf_op jit(solution)/shard_map/ppermute | solution.py:501
  28.2 9.2 %collective-permute-start.8 = (bf16[128,2048]{1,0:T(8,128)(2,1)S(1)}, bf16[128,2048]{1,0:T(8,128)(2,1)S(1)}, u32[]{:S(2)}, u32[]{:S(2)}) collective-permute-start(bf16[128,2048]{1,0:T(8,128)(2,1)S(1)} %shard_map.120.refs_0_), channel_id=1, source_target_pairs={{0,8},{1,17},{2,10},{3,19},{4,12},{5,21},{6,14},{7,23},{8,0},{9,25... | collective-permute-start | bytes 1572872 | tf_op jit(solution)/shard_map/ppermute | solution.py:501
  37.4 2.7 %collective-permute-start.9 = (f32[128,2048]{1,0:T(8,128)S(1)}, f32[128,2048]{1,0:T(8,128)S(1)}, u32[]{:S(2)}, u32[]{:S(2)}) collective-permute-start(f32[128,2048]{1,0:T(8,128)S(1)} %get-tuple-element.89), channel_id=1, source_target_pairs={{0,1},{1,0},{2,3},{3,2},{4,5},{5,4},{6,7},{7,6},{8,9},{9,8},{10,11... | collective-permute-start | bytes 3145736 | tf_op jit(solution)/shard_map/ppermute | solution.py:501
  40.3 19.5 %copy-start.1 = (f32[2048]{0:T(1024)S(1)}, f32[2048]{0:T(1024)}, u32[]{:S(2)}) copy-start(f32[2048]{0:T(1024)} %param.17) | copy-start | bytes 24580
  40.3 22.4 %copy-start.3 = (s32[32]{0:T(128)S(1)}, s32[32]{0:T(128)}, u32[]{:S(2)}) copy-start(s32[32]{0:T(128)} %param.13) | copy-start | bytes 388
  40.3 19.4 %collective-permute-start.13 = (bf16[256,2048]{1,0:T(8,128)(2,1)S(1)}, bf16[256,2048]{1,0:T(8,128)(2,1)S(1)}, u32[]{:S(2)}, u32[]{:S(2)}) collective-permute-start(bf16[256,2048]{1,0:T(8,128)(2,1)S(1)} %shard_map.126), channel_id=1, source_target_pairs={{0,16},{1,9},{2,18},{3,11},{4,20},{5,13},{6,22},{7,15},{8,24},{9,1... | collective-permute-start | bytes 3145736 | tf_op jit(solution)/shard_map/ppermute | solution.py:501
  41.9 1.9 %collective-permute-start.11 = (bf16[128,2048]{1,0:T(8,128)(2,1)S(1)}, bf16[128,2048]{1,0:T(8,128)(2,1)S(1)}, u32[]{:S(2)}, u32[]{:S(2)}) collective-permute-start(bf16[128,2048]{1,0:T(8,128)(2,1)S(1)} %collective-permute-done.8.refs_0_.refs_1_), channel_id=1, source_target_pairs={{0,1},{1,0},{2,3},{3,2},{4,5},{5,4},{6,7},{7,6},{8,9},{9,8},{10,11... | collective-permute-start | bytes 1572872 | tf_op jit(solution)/shard_map/ppermute | solution.py:501
  41.9 8.1 %collective-permute-start.10 = (bf16[64,2048]{1,0:T(8,128)(2,1)S(1)}, bf16[64,2048]{1,0:T(8,128)(2,1)S(1)}, u32[]{:S(2)}, u32[]{:S(2)}) collective-permute-start(bf16[64,2048]{1,0:T(8,128)(2,1)S(1)} %get-tuple-element.91), channel_id=1, source_target_pairs={{0,2},{1,5},{2,0},{3,7},{4,6},{5,1},{6,4},{7,3},{8,10},{9,13},{10,... | collective-permute-start | bytes 786440 | tf_op jit(solution)/shard_map/ppermute | solution.py:501
  50.1 9.7 %collective-permute-start.12 = (bf16[64,2048]{1,0:T(8,128)(2,1)S(1)}, bf16[64,2048]{1,0:T(8,128)(2,1)S(1)}, u32[]{:S(2)}, u32[]{:S(2)}) collective-permute-start(bf16[64,2048]{1,0:T(8,128)(2,1)S(1)} %get-tuple-element.98), channel_id=1, source_target_pairs={{0,4},{1,3},{2,6},{3,1},{4,0},{5,7},{6,2},{7,5},{8,12},{9,11},{10,... | collective-permute-start | bytes 786440 | tf_op jit(solution)/shard_map/ppermute | solution.py:501
  59.9 5.1 %collective-permute-start.14 = (bf16[256,2048]{1,0:T(8,128)(2,1)S(1)}, bf16[256,2048]{1,0:T(8,128)(2,1)S(1)}, u32[]{:S(2)}, u32[]{:S(2)}) collective-permute-start(bf16[256,2048]{1,0:T(8,128)(2,1)S(1)} %collective-permute-done.13.refs_0_), channel_id=1, source_target_pairs={{0,1},{1,0},{2,3},{3,2},{4,5},{5,4},{6,7},{7,6},{8,9},{9,8},{10,11... | collective-permute-start | bytes 3145736 | tf_op jit(solution)/shard_map/ppermute | solution.py:501
  60.0 10.2 %collective-permute-start.16 = (bf16[64,2048]{1,0:T(8,128)(2,1)S(1)}, bf16[64,2048]{1,0:T(8,128)(2,1)S(1)}, u32[]{:S(2)}, u32[]{:S(2)}) collective-permute-start(bf16[64,2048]{1,0:T(8,128)(2,1)S(1)} %get-tuple-element.107.refs_0_), channel_id=1, source_target_pairs={{0,8},{1,17},{2,10},{3,19},{4,12},{5,21},{6,14},{7,23},{8,0},{9,25... | collective-permute-start | bytes 786440 | tf_op jit(solution)/shard_map/ppermute | solution.py:501
  61.6 8.6 %collective-permute-start.15 = (bf16[64,2048]{1,0:T(8,128)(2,1)S(1)}, bf16[64,2048]{1,0:T(8,128)(2,1)S(1)}, u32[]{:S(2)}, u32[]{:S(2)}) collective-permute-start(bf16[64,2048]{1,0:T(8,128)(2,1)S(1)} %get-tuple-element.107.refs_0_), channel_id=1, source_target_pairs={{0,2},{1,5},{2,0},{3,7},{4,6},{5,1},{6,4},{7,3},{8,10},{9,13},{10,... | collective-permute-start | bytes 786440 | tf_op jit(solution)/shard_map/ppermute | solution.py:501
  63.1 7.1 %collective-permute-start.17 = (f32[8,2176]{1,0:T(8,128)S(1)}, f32[8,2176]{1,0:T(8,128)S(1)}, u32[]{:S(2)}, u32[]{:S(2)}) collective-permute-start(f32[8,2176]{1,0:T(8,128)S(1)} %get-tuple-element.116), channel_id=1, source_target_pairs={{0,8},{1,9},{2,10},{3,11},{4,12},{5,13},{6,14},{7,15},{8,0},{9,1},... | collective-permute-start | bytes 208904 | tf_op jit(solution)/shard_map/ppermute | solution.py:501
  63.7 6.5 %collective-permute-start.18 = (f32[8,2176]{1,0:T(8,128)S(1)}, f32[8,2176]{1,0:T(8,128)S(1)}, u32[]{:S(2)}, u32[]{:S(2)}) collective-permute-start(f32[8,2176]{1,0:T(8,128)S(1)} %get-tuple-element.117), channel_id=1, source_target_pairs={{0,16},{1,17},{2,18},{3,19},{4,20},{5,21},{6,22},{7,23},{8,24},{9,... | collective-permute-start | bytes 208904 | tf_op jit(solution)/shard_map/ppermute | solution.py:501
  65.0 5.2 %collective-permute-start.19 = (f32[8,2176]{1,0:T(8,128)S(1)}, f32[8,2176]{1,0:T(8,128)S(1)}, u32[]{:S(2)}, u32[]{:S(2)}) collective-permute-start(f32[8,2176]{1,0:T(8,128)S(1)} %get-tuple-element.118), channel_id=1, source_target_pairs={{0,24},{1,25},{2,26},{3,27},{4,28},{5,29},{6,30},{7,31},{8,16},{9,... | collective-permute-start | bytes 208904 | tf_op jit(solution)/shard_map/ppermute | solution.py:501
  70.3 5.9 %collective-permute-start.20 = (bf16[128,2048]{1,0:T(8,128)(2,1)S(1)}, bf16[128,2048]{1,0:T(8,128)(2,1)S(1)}, u32[]{:S(2)}, u32[]{:S(2)}) collective-permute-start(bf16[128,2048]{1,0:T(8,128)(2,1)S(1)} %shard_map.130.refs_1_), channel_id=1, source_target_pairs={{0,1},{1,0},{2,3},{3,2},{4,5},{5,4},{6,7},{7,6},{8,9},{9,8},{10,11... | collective-permute-start | bytes 1572872 | tf_op jit(solution)/shard_map/ppermute | solution.py:501
  70.4 12.1 %collective-permute-start.23 = (bf16[128,2048]{1,0:T(8,128)(2,1)S(1)}, bf16[128,2048]{1,0:T(8,128)(2,1)S(1)}, u32[]{:S(2)}, u32[]{:S(2)}) collective-permute-start(bf16[128,2048]{1,0:T(8,128)(2,1)S(1)} %shard_map.134), channel_id=1, source_target_pairs={{0,16},{1,9},{2,18},{3,11},{4,20},{5,13},{6,22},{7,15},{8,24},{9,1... | collective-permute-start | bytes 1572872 | tf_op jit(solution)/shard_map/ppermute | solution.py:501
  71.5 9.2 %collective-permute-start.21 = (bf16[64,2048]{1,0:T(8,128)(2,1)S(1)}, bf16[64,2048]{1,0:T(8,128)(2,1)S(1)}, u32[]{:S(2)}, u32[]{:S(2)}) collective-permute-start(bf16[64,2048]{1,0:T(8,128)(2,1)S(1)} %collective-permute-done.15.refs_1_.refs_0_), channel_id=1, source_target_pairs={{0,8},{1,17},{2,10},{3,19},{4,12},{5,21},{6,14},{7,23},{8,0},{9,25... | collective-permute-start | bytes 786440 | tf_op jit(solution)/shard_map/ppermute | solution.py:501
  80.8 2.8 %collective-permute-start.22 = (bf16[128,2048]{1,0:T(8,128)(2,1)S(1)}, bf16[128,2048]{1,0:T(8,128)(2,1)S(1)}, u32[]{:S(2)}, u32[]{:S(2)}) collective-permute-start(bf16[128,2048]{1,0:T(8,128)(2,1)S(1)} %shard_map.133.refs_10_), channel_id=1, source_target_pairs={{0,1},{1,0},{2,3},{3,2},{4,5},{5,4},{6,7},{7,6},{8,9},{9,8},{10,11... | collective-permute-start | bytes 1572872 | tf_op jit(solution)/shard_map/ppermute | solution.py:501
  82.4 1.9 %collective-permute-start.24 = (bf16[128,2048]{1,0:T(8,128)(2,1)S(1)}, bf16[128,2048]{1,0:T(8,128)(2,1)S(1)}, u32[]{:S(2)}, u32[]{:S(2)}) collective-permute-start(bf16[128,2048]{1,0:T(8,128)(2,1)S(1)} %collective-permute-done.23.refs_12_), channel_id=1, source_target_pairs={{0,1},{1,0},{2,3},{3,2},{4,5},{5,4},{6,7},{7,6},{8,9},{9,8},{10,11... | collective-permute-start | bytes 1572872 | tf_op jit(solution)/shard_map/ppermute | solution.py:501
  82.5 10.2 %collective-permute-start.25 = (bf16[128,2048]{1,0:T(8,128)(2,1)S(1)}, bf16[128,2048]{1,0:T(8,128)(2,1)S(1)}, u32[]{:S(2)}, u32[]{:S(2)}) collective-permute-start(bf16[128,2048]{1,0:T(8,128)(2,1)S(1)} %shard_map.137), channel_id=1, source_target_pairs={{0,16},{1,9},{2,18},{3,11},{4,20},{5,13},{6,22},{7,15},{8,24},{9,1... | collective-permute-start | bytes 1572872 | tf_op jit(solution)/shard_map/ppermute | solution.py:501
  92.7 2.0 %collective-permute-start.26 = (bf16[128,2048]{1,0:T(8,128)(2,1)S(1)}, bf16[128,2048]{1,0:T(8,128)(2,1)S(1)}, u32[]{:S(2)}, u32[]{:S(2)}) collective-permute-start(bf16[128,2048]{1,0:T(8,128)(2,1)S(1)} %collective-permute-done.25.refs_0_), channel_id=1, source_target_pairs={{0,1},{1,0},{2,3},{3,2},{4,5},{5,4},{6,7},{7,6},{8,9},{9,8},{10,11... | collective-permute-start | bytes 1572872 | tf_op jit(solution)/shard_map/ppermute | solution.py:501

commit v5 on v4

--- a/solution.py
+++ b/solution.py
@@ -46,7 +46,7 @@
 
 
 def attend_body(
-    kv_heads, parts, positions_ref, queries, keys, values, enc, heads_ref, energy_ref, enc_ref, q, k, v, sems, enc_sems
+    kv_heads, positions_ref, queries, keys, values, heads_ref, energy_ref, q, k, v, sems
 ):
     rows, width = q.shape
     per_head = width // kv_heads // HEAD_DIM
@@ -57,12 +57,7 @@
         here = pl.ds(g * HEAD_DIM, HEAD_DIM)
         copies.append(pltpu.make_async_copy(keys.at[0, :, here], k.at[:, here], sems.at[2 * g]))
         copies.append(pltpu.make_async_copy(values.at[0, :, here], v.at[:, here], sems.at[2 * g + 1]))
-    size = enc.shape[0] // parts
-    weights = []
-    for part in range(parts):
-        here = pl.ds(part * size, size)
-        weights.append(pltpu.make_async_copy(enc.at[here], enc_ref.at[here], enc_sems.at[part]))
-    for copy in copies + weights:
+    for copy in copies:
         copy.start()
     whole.wait()
     shape = (rows, keys.shape[1])
@@ -70,70 +65,71 @@
     visible = lax.broadcasted_iota(jnp.int32, shape, 1) <= positions_ref[0] + row_index
     visible = jnp.concatenate([visible] * per_head, axis=0)
     energy = jnp.zeros((1, 128), jnp.float32)
+    heads = [slice(i * HEAD_DIM, (i + 1) * HEAD_DIM) for i in range(kv_heads * per_head)]
+    scores, probs = [], []
     for g in range(kv_heads):
-        heads = [slice((g * per_head + i) * HEAD_DIM, (g * per_head + i + 1) * HEAD_DIM) for i in range(per_head)]
-        grouped = jnp.concatenate([q[:, head] for head in heads], axis=0)
-        here = slice(g * HEAD_DIM, (g + 1) * HEAD_DIM)
+        grouped = jnp.concatenate([q[:, head] for head in heads[g * per_head : (g + 1) * per_head]], axis=0)
         copies[2 * g].wait()
-        scores = lax.dot_general(
-            grouped, k[:, here], (((1,), (1,)), ((), ())), preferred_element_type=jnp.float32
-        ) * HEAD_DIM ** (-0.5)
-        scores = jnp.where(visible, scores, -jnp.inf)
-        weight = jnp.exp(scores - jnp.max(scores, axis=1, keepdims=True))
-        probs = (weight / jnp.sum(weight, axis=1, keepdims=True)).astype(jnp.bfloat16)
+        product = lax.dot_general(
+            grouped, k[:, heads[g]], (((1,), (1,)), ((), ())), preferred_element_type=jnp.float32
+        )
+        scores.append(jnp.where(visible, product * HEAD_DIM ** (-0.5), -jnp.inf))
+    for score in scores:
+        weight = jnp.exp(score - jnp.max(score, axis=1, keepdims=True))
+        probs.append((weight / jnp.sum(weight, axis=1, keepdims=True)).astype(jnp.bfloat16))
+    for g in range(kv_heads):
         copies[2 * g + 1].wait()
-        mix = jnp.dot(probs, v[:, here], preferred_element_type=jnp.float32).astype(jnp.bfloat16)
-        for i, head in enumerate(heads):
+    for g in range(kv_heads):
+        mix = jnp.dot(probs[g], v[:, heads[g]], preferred_element_type=jnp.float32).astype(jnp.bfloat16)
+        for i, head in enumerate(heads[g * per_head : (g + 1) * per_head]):
             part = mix[i * rows : (i + 1) * rows]
             heads_ref[:, head] = part
             square = jnp.sum(jnp.square(part.astype(jnp.float32)), axis=0, keepdims=True)
             for lane in range(0, HEAD_DIM, 128):
                 energy = energy + square[:, lane : lane + 128]
     energy_ref[...] = energy
-    for copy in weights:
-        copy.wait()
-
-
-def attend(queries, cache_keys, cache_values, positions, enc, parts=8):
+
+
+def attend(queries, cache_keys, cache_values, positions):
     rows, width = queries.shape
     slots, kv_width = cache_keys.shape[1:]
     kv_heads = kv_width // HEAD_DIM
-    hbm = [pltpu.with_memory_space_constraint(x, pltpu.HBM) for x in (queries, cache_keys, cache_values, enc)]
+    hbm = [pltpu.with_memory_space_constraint(x, pltpu.HBM) for x in (queries, cache_keys, cache_values)]
     return kernel_call(
-        functools.partial(attend_body, kv_heads, parts),
+        functools.partial(attend_body, kv_heads),
         [positions, *hbm],
-        [IN_SMEM] + [IN_HBM] * 4,
-        [half_array(rows, width), float_array(1, 128), pltpu.VMEM(enc.shape, enc.dtype)],
+        [IN_SMEM] + [IN_HBM] * 3,
+        [half_array(rows, width), float_array(1, 128)],
         [
             pltpu.VMEM((rows, width), jnp.bfloat16),
             pltpu.VMEM((slots, kv_width), jnp.bfloat16),
             pltpu.VMEM((slots, kv_width), jnp.bfloat16),
             pltpu.SemaphoreType.DMA((2 * kv_heads + 1,)),
-            pltpu.SemaphoreType.DMA((parts,)),
         ],
         flops=4 * rows * slots * width,
     )
 
 
-def load_body(parts, source, target, sems):
+def load_body(parts, first, source, target, sems):
     size = source.shape[0] // parts
+    columns = pl.ds(first, target.shape[1])
     copies = []
     for part in range(parts):
         here = pl.ds(part * size, size)
-        copies.append(pltpu.make_async_copy(source.at[here], target.at[here], sems.at[part]))
+        copies.append(pltpu.make_async_copy(source.at[here, columns], target.at[here], sems.at[part]))
     for copy in copies:
         copy.start()
     for copy in copies:
         copy.wait()
 
 
-def load(x, parts=8):
+def load(x, first, columns, parts=8):
     source = pltpu.with_memory_space_constraint(x, pltpu.HBM)
     return kernel_call(
-        functools.partial(load_body, parts),
+        functools.partial(load_body, parts, first),
         [source],
         [IN_HBM],
-        [pltpu.VMEM(x.shape, x.dtype)],
+        [pltpu.VMEM((x.shape[0], columns), x.dtype)],
         [pltpu.SemaphoreType.DMA((parts,))],
     )[0]
 
@@ -249,7 +245,7 @@
     return [(part, 0, part.shape[0]) for part in parts]
 
 
-def encode_body(cuts, tile, entries, energy_ref, own_ref, enc_ref, bias_ref, *refs):
+def encode_body(cuts, tile, entries, energy_ref, own_ref, left_ref, right_ref, bias_ref, *refs):
     count = len(cuts)
     pieces, (codes_ref, slope_ref, part_ref), (rows, *rest) = refs[:count], refs[count : count + 3], refs[count + 3 :]
     if rest:
@@ -257,9 +253,11 @@
     join(pieces, rows, cuts)
     factor = sharpness * LOG2E
     scale = norm_scale(energy_ref, entries) * factor
-    for first in range(0, enc_ref.shape[1], tile):
+    half = left_ref.shape[1]
+    for first in range(0, 2 * half, tile):
         here = slice(first, first + tile)
-        product = jnp.dot(rows[...], enc_ref[:, here], preferred_element_type=jnp.float32)
+        side, there = (left_ref, here) if first < half else (right_ref, slice(first - half, first - half + tile))
+        product = jnp.dot(rows[...], side[:, there], preferred_element_type=jnp.float32)
         coded, slope = codes(product * scale + bias_ref[:, here] * factor)
         codes_ref[here, :] = coded.T.astype(jnp.bfloat16)
         slope_ref[:, here] = slope
@@ -273,7 +271,7 @@
             here = slice(first, first + tile)
             total = jnp.dot(coded_ref[...], dec_ref[:, here], preferred_element_type=jnp.float32)
             keep_ref[:, here] = total[:half]
-            send_ref[:, here] = total[half:]
+            send_ref[:, here] = total[half:].astype(jnp.bfloat16)
 
 
 def cut_pieces(parts):
@@ -281,41 +279,41 @@
 
 
 def encode(entries, energy, own, enc, bias, pieces, columns):
-    width, latents = enc.shape
+    width, latents = enc[0].shape[0], 2 * enc[0].shape[1]
     pieces, cuts = cut_pieces(pieces)
     count = sum(size for _, size in cuts)
     return kernel_call(
-        functools.partial(encode_body, cuts, min(512, latents), entries),
-        [energy, own, held(enc), bias, *pieces],
-        [IN_VMEM, IN_SMEM] + [IN_VMEM] * (2 + len(pieces)),
+        functools.partial(encode_body, cuts, min(512, latents // 2), entries),
+        [energy, own, *(held(x) for x in enc), bias, *pieces],
+        [IN_VMEM, IN_SMEM] + [IN_VMEM] * (3 + len(pieces)),
         [half_array(latents, count), half_array(count, latents), half_array(columns, count)],
         [pltpu.VMEM((count, width), jnp.bfloat16)],
         flops=2 * count * width * latents,
     )
 
 
-def rebuild_body(cuts, tile, entries, energy_ref, own_ref, enc_ref, bias_ref, dec_ref, *refs):
+def rebuild_body(cuts, tile, entries, energy_ref, own_ref, left_ref, right_ref, bias_ref, dec_ref, *refs):
     count = len(cuts)
     pieces, outs, scratch = refs[:count], refs[count : count + 5], refs[count + 5 :]
     encode_body(
-        cuts, tile, entries, energy_ref, own_ref, enc_ref, bias_ref, *pieces, *outs[:3], dec_ref, *outs[3:], *scratch
+        cuts, tile, entries, energy_ref, own_ref, left_ref, right_ref, bias_ref, *pieces, *outs[:3], dec_ref, *outs[3:], *scratch
     )
 
 
 def encode_and_rebuild(entries, energy, own, enc, bias, dec, pieces, columns):
-    width, latents = enc.shape
+    width, latents = enc[0].shape[0], 2 * enc[0].shape[1]
     pieces, cuts = cut_pieces(pieces)
     count = sum(size for _, size in cuts)
     return kernel_call(
-        functools.partial(rebuild_body, cuts, min(512, latents), entries),
-        [energy, own, held(enc), bias, held(dec), *pieces],
-        [IN_VMEM, IN_SMEM] + [IN_VMEM] * (3 + len(pieces)),
+        functools.partial(rebuild_body, cuts, min(512, latents // 2), entries),
+        [energy, own, *(held(x) for x in enc), bias, held(dec), *pieces],
+        [IN_VMEM, IN_SMEM] + [IN_VMEM] * (4 + len(pieces)),
         [
             half_array(latents, count),
             half_array(count, latents),
             half_array(columns, count),
             float_array(count // 2, width),
-            float_array(count // 2, width),
+            half_array(count // 2, width),
         ],
         [pltpu.VMEM((count, width), jnp.bfloat16), pltpu.VMEM((count, latents), jnp.bfloat16)],
         flops=4 * count * width * latents,
@@ -600,9 +598,10 @@
     bias, out_bias, places, own = lax.optimization_barrier(
         (enc_bias[None, :], dec_bias[None, :], shuffle[None, :], own)
     )
-    heads_out, energy, enc = attend(queries, cache_keys, cache_values, positions, after(enc_weight, bias, out_bias, places, own))
+    heads_out, energy = attend(after(queries, bias, out_bias, places, own), cache_keys, cache_values, positions)
 
     small_steps = plane + [core] + line
+    enc, latents_here = [], enc_weight.shape[1]
     rows = heads_out
     for number, mask in enumerate(line):
         arrived = swap(rows, *mask)
@@ -612,8 +611,12 @@
         for small in small_steps[:count]:
             other = swap(energy, *small)
             if small == line[0]:
-                dec = load(after(dec_weight, energy))
+                dec = load(after(dec_weight, energy), 0, att_width)
                 other = after(other, dec)
+            elif small in plane[:2]:
+                side = latents_here // 2
+                enc.append(load(after(enc_weight, energy), len(enc) * side, side))
+                other = after(other, enc[-1])
             energy = add(energy, other)
         small_steps = small_steps[count:]
         rows = joined(rows, after(arrived, energy))

time: 101 us -> 99 us (0.980)
  waiting for transfers between devices: 27.7 us -> 23.8 us
  Pallas kernels: 45.7 us -> 48.4 us
  starting transfers between devices: 25.9 us -> 24.8 us
    ppermute x27, waiting for transfers between devices: 27.7 us -> 23.8 us  [swap(): lax.ppermute(x, ('dp', 'latent'), [(i, i ^ (odd if i & 1 else even)) for...]
    pallas_call x27 -> x29, Pallas kernels: 45.7 us -> 48.4 us  [kernel_call(): pl.pallas_call(body, in_specs=specs, out_specs=out_specs or [IN_VMEM] * l...]
    ppermute x27, starting transfers between devices: 25.9 us -> 24.8 us  [swap(): lax.ppermute(x, ('dp', 'latent'), [(i, i ^ (odd if i & 1 else even)) for...]
  transfers between devices with their start and end apart: 27 -> 27, of which waited for: 15 -> 14; matrix products, arithmetic and copies ran while one was open for 0% -> 0% of each run, Pallas kernels for 34% -> 39%
where the time goes in v5:
time: 99 us; the launch traced here: 98.8 us
  Pallas kernels  48.4 us (49%)
  starting transfers between devices  24.8 us (25%)
  waiting for transfers between devices  23.8 us (24%)
  between operations  1.1 us (1%)
    pallas_call x29, Pallas kernels, kernel_call(): pl.pallas_call(body, in_specs=specs, out_specs=out_specs or [IN_VMEM] * l...  48.4 us
    ppermute x27, starting transfers between devices, swap(): lax.ppermute(x, ('dp', 'latent'), [(i, i ^ (odd if i & 1 else even)) for...  24.8 us
    ppermute x27, waiting for transfers between devices, swap(): lax.ppermute(x, ('dp', 'latent'), [(i, i ^ (odd if i & 1 else even)) for...  23.8 us
  transfers between devices with their start and end apart: 27, of which 14 were waited for; matrix products, arithmetic and copies ran while one was open for 0% of the time, Pallas kernels for 39%

profile of v5, /device:TPU:0, one launch (start us, length us, event | category | flops | bytes accessed | tf_op | source)
XLA Modules:
  0.0 98.8 jit_solution(9351815545277071846)
XLA Ops:
  1.3 3.0 %shard_map.112 = (bf16[32,2048]{1,0:T(8,128)(2,1)S(1)}, f32[1,128]{1,0:T(1,128)S(1)}) custom-call(s32[32]{0:T(128)S(1)} %copy-done.2, bf16[32,2048]{1,0:T(8,128)(2,1)} %queries, bf16[1,512,1024]{2,1,0:T(8,128)(2,1)} %keys.1, bf16[1,512,1024]{2,1,0:T(8,128)(2,1)} %values.1), custom_call_target="tpu_custom_call" | custom-call | flops 134217728 | tf_op jit(solution)/shard_map/pallas_call | solution.py:25
  4.3 4.1 %collective-permute-start.5 = (bf16[32,2048]{1,0:T(8,128)(2,1)S(1)}, bf16[32,2048]{1,0:T(8,128)(2,1)S(1)}, u32[]{:S(2)}, u32[]{:S(2)}) collective-permute-start(bf16[32,2048]{1,0:T(8,128)(2,1)S(1)} %get-tuple-element.90.refs_0_), channel_id=1, source_target_pairs={{0,4},{1,3},{2,6},{3,1},{4,0},{5,7},{6,2},{7,5},{8,12},{9,11},{10,... | collective-permute-start | bytes 393224 | tf_op jit(solution)/shard_map/ppermute | solution.py:499
  8.4 1.5 %collective-permute-start = (f32[1,128]{1,0:T(1,128)S(1)}, f32[1,128]{1,0:T(1,128)S(1)}, u32[]{:S(2)}, u32[]{:S(2)}) collective-permute-start(f32[1,128]{1,0:T(1,128)S(1)} %get-tuple-element.83.a_ref), channel_id=1, source_target_pairs={{0,8},{1,17},{2,10},{3,19},{4,12},{5,21},{6,14},{7,23},{8,0},{9,25... | collective-permute-start | bytes 1544 | tf_op jit(solution)/shard_map/ppermute | solution.py:499
  9.9 2.2 %shard_map.113.left_ref = bf16[2048,1024]{1,0:T(8,128)(2,1)S(1)} custom-call(bf16[2048,2048]{1,0:T(8,128)(2,1)} %source.1), custom_call_target="tpu_custom_call" | custom-call | tf_op jit(solution)/shard_map/pallas_call | solution.py:25
  12.1 1.6 %collective-permute-start.1 = (f32[1,128]{1,0:T(1,128)S(1)}, f32[1,128]{1,0:T(1,128)S(1)}, u32[]{:S(2)}, u32[]{:S(2)}) collective-permute-start(f32[1,128]{1,0:T(1,128)S(1)} %shard_map.114.a_ref), channel_id=1, source_target_pairs={{0,16},{1,9},{2,18},{3,11},{4,20},{5,13},{6,22},{7,15},{8,24},{9,1... | collective-permute-start | bytes 1544 | tf_op jit(solution)/shard_map/ppermute | solution.py:499
  13.7 2.2 %shard_map.115.right_ref = bf16[2048,1024]{1,0:T(8,128)(2,1)S(1)} custom-call(bf16[2048,2048]{1,0:T(8,128)(2,1)} %source.1), custom_call_target="tpu_custom_call" | custom-call | tf_op jit(solution)/shard_map/pallas_call | solution.py:25
  16.0 1.6 %collective-permute-start.6 = (bf16[64,2048]{1,0:T(8,128)(2,1)S(1)}, bf16[64,2048]{1,0:T(8,128)(2,1)S(1)}, u32[]{:S(2)}, u32[]{:S(2)}) collective-permute-start(bf16[64,2048]{1,0:T(8,128)(2,1)S(1)} %shard_map.121.refs_0_.heads_ref), channel_id=1, source_target_pairs={{0,2},{1,5},{2,0},{3,7},{4,6},{5,1},{6,4},{7,3},{8,10},{9,13},{10,... | collective-permute-start | bytes 786440 | tf_op jit(solution)/shard_map/ppermute | solution.py:499
  17.6 1.1 %collective-permute-done.2.b_ref = f32[1,128]{1,0:T(1,128)S(1)} collective-permute-done((f32[1,128]{1,0:T(1,128)S(1)}, f32[1,128]{1,0:T(1,128)S(1)}, u32[]{:S(2)}, u32[]{:S(2)}) %collective-permute-start.2) | collective-permute-done | bytes 544 | tf_op jit(solution)/shard_map/ppermute | solution.py:499
  19.1 3.5 %shard_map.118.dec_ref = bf16[2048,2048]{1,0:T(8,128)(2,1)S(1)} custom-call(bf16[2048,2048]{1,0:T(8,128)(2,1)} %source.2), custom_call_target="tpu_custom_call" | custom-call | tf_op jit(solution)/shard_map/pallas_call | solution.py:25
  23.7 3.1 %collective-permute-done.4.b_ref = f32[1,128]{1,0:T(1,128)S(1)} collective-permute-done((f32[1,128]{1,0:T(1,128)S(1)}, f32[1,128]{1,0:T(1,128)S(1)}, u32[]{:S(2)}, u32[]{:S(2)}) %collective-permute-start.4) | collective-permute-done | bytes 544 | tf_op jit(solution)/shard_map/ppermute | solution.py:499
  26.9 1.3 %collective-permute-start.8 = (bf16[128,2048]{1,0:T(8,128)(2,1)S(1)}, bf16[128,2048]{1,0:T(8,128)(2,1)S(1)}, u32[]{:S(2)}, u32[]{:S(2)}) collective-permute-start(bf16[128,2048]{1,0:T(8,128)(2,1)S(1)} %shard_map.122.refs_0_), channel_id=1, source_target_pairs={{0,8},{1,17},{2,10},{3,19},{4,12},{5,21},{6,14},{7,23},{8,0},{9,25... | collective-permute-start | bytes 1572872 | tf_op jit(solution)/shard_map/ppermute | solution.py:499
  28.8 5.6 %shard_map.123 = (bf16[2048,256]{1,0:T(8,128)(2,1)S(1)}, bf16[256,2048]{1,0:T(8,128)(2,1)S(1)}, bf16[512,256]{1,0:T(8,128)(2,1)S(1)}, f32[128,2048]{1,0:T(8,128)S(1)}, bf16[128,2048]{1,0:T(8,128)(2,1)S(1)}) custom-call(f32[1,128]{1,0:T(1,128)S(1)} %shard_map.120.energy_ref, s32[1]{0:T(128)} %bitcast.3.own_ref, bf16[2048,1024]{1,0:T(8,128)(2,1)S(1)} %shard_map.113.left_ref, ...), custom_call_target="tpu_custom_call" | custom-call | flops 4294967296 | tf_op jit(solution)/shard_map/pallas_call | solution.py:25
  34.4 1.7 %collective-permute-done.8.refs_0_.refs_1_ = bf16[128,2048]{1,0:T(8,128)(2,1)S(1)} collective-permute-done((bf16[128,2048]{1,0:T(8,128)(2,1)S(1)}, bf16[128,2048]{1,0:T(8,128)(2,1)S(1)}, u32[]{:S(2)}, u32[]{:S(2)}) %collective-permute-start.8) | collective-permute-done | bytes 524320 | tf_op jit(solution)/shard_map/ppermute | solution.py:499
  36.1 1.9 %collective-permute-done.9.b_ref = bf16[128,2048]{1,0:T(8,128)(2,1)S(1)} collective-permute-done((bf16[128,2048]{1,0:T(8,128)(2,1)S(1)}, bf16[128,2048]{1,0:T(8,128)(2,1)S(1)}, u32[]{:S(2)}, u32[]{:S(2)}) %collective-permute-start.9) | collective-permute-done | bytes 524320 | tf_op jit(solution)/shard_map/ppermute | solution.py:499
  38.2 1.4 %collective-permute-start.13 = (bf16[256,2048]{1,0:T(8,128)(2,1)S(1)}, bf16[256,2048]{1,0:T(8,128)(2,1)S(1)}, u32[]{:S(2)}, u32[]{:S(2)}) collective-permute-start(bf16[256,2048]{1,0:T(8,128)(2,1)S(1)} %shard_map.128), channel_id=1, source_target_pairs={{0,16},{1,9},{2,18},{3,11},{4,20},{5,13},{6,22},{7,15},{8,24},{9,1... | collective-permute-start | bytes 3145736 | tf_op jit(solution)/shard_map/ppermute | solution.py:499
  40.3 1.2 %collective-permute-done.11.refs_1_ = bf16[128,2048]{1,0:T(8,128)(2,1)S(1)} collective-permute-done((bf16[128,2048]{1,0:T(8,128)(2,1)S(1)}, bf16[128,2048]{1,0:T(8,128)(2,1)S(1)}, u32[]{:S(2)}, u32[]{:S(2)}) %collective-permute-start.11) | collective-permute-done | bytes 524320 | tf_op jit(solution)/shard_map/ppermute | solution.py:499
  41.5 3.6 %shard_map.125 = (bf16[2048,256]{1,0:T(8,128)(2,1)S(1)}, bf16[256,2048]{1,0:T(8,128)(2,1)S(1)}, bf16[512,256]{1,0:T(8,128)(2,1)S(1)}) custom-call(f32[1,128]{1,0:T(1,128)S(1)} %shard_map.120.energy_ref, s32[1]{0:T(128)} %bitcast.3.own_ref, bf16[2048,1024]{1,0:T(8,128)(2,1)S(1)} %shard_map.113.left_ref, bf16[2048,1024]{1,0:T(8,128)(2,1)S(1)} %shard_map.115.right_ref, ...), custom_call_target="tpu_custom_call" | custom-call | flops 2147483648 | tf_op jit(solution)/shard_map/pallas_call | solution.py:25
  45.1 2.6 %collective-permute-done.10.b_ref = bf16[64,2048]{1,0:T(8,128)(2,1)S(1)} collective-permute-done((bf16[64,2048]{1,0:T(8,128)(2,1)S(1)}, bf16[64,2048]{1,0:T(8,128)(2,1)S(1)}, u32[]{:S(2)}, u32[]{:S(2)}) %collective-permute-start.10) | collective-permute-done | bytes 262176 | tf_op jit(solution)/shard_map/ppermute | solution.py:499
  47.8 2.3 %collective-permute-start.12 = (bf16[64,2048]{1,0:T(8,128)(2,1)S(1)}, bf16[64,2048]{1,0:T(8,128)(2,1)S(1)}, u32[]{:S(2)}, u32[]{:S(2)}) collective-permute-start(bf16[64,2048]{1,0:T(8,128)(2,1)S(1)} %get-tuple-element.104), channel_id=1, source_target_pairs={{0,4},{1,3},{2,6},{3,1},{4,0},{5,7},{6,2},{7,5},{8,12},{9,11},{10,... | collective-permute-start | bytes 786440 | tf_op jit(solution)/shard_map/ppermute | solution.py:499
  50.1 2.3 %shard_map.127 = (f32[2048,1]{1,0:T(8,128)S(1)}, f32[1,2048]{1,0:T(1,128)S(1)}) custom-call(bf16[2048,2048]{1,0:T(8,128)(2,1)S(1)} %shard_map.118.dec_ref), custom_call_target="tpu_custom_call" | custom-call | tf_op jit(solution)/shard_map/pallas_call | solution.py:25
  52.4 5.0 %collective-permute-done.12.b_ref = bf16[64,2048]{1,0:T(8,128)(2,1)S(1)} collective-permute-done((bf16[64,2048]{1,0:T(8,128)(2,1)S(1)}, bf16[64,2048]{1,0:T(8,128)(2,1)S(1)}, u32[]{:S(2)}, u32[]{:S(2)}) %collective-permute-start.12) | collective-permute-done | bytes 262176 | tf_op jit(solution)/shard_map/ppermute | solution.py:499
  57.8 1.3 %collective-permute-start.16 = (bf16[64,2048]{1,0:T(8,128)(2,1)S(1)}, bf16[64,2048]{1,0:T(8,128)(2,1)S(1)}, u32[]{:S(2)}, u32[]{:S(2)}) collective-permute-start(bf16[64,2048]{1,0:T(8,128)(2,1)S(1)} %get-tuple-element.113.refs_0_), channel_id=1, source_target_pairs={{0,8},{1,17},{2,10},{3,19},{4,12},{5,21},{6,14},{7,23},{8,0},{9,25... | collective-permute-start | bytes 786440 | tf_op jit(solution)/shard_map/ppermute | solution.py:499
  59.0 1.2 %collective-permute-start.15 = (bf16[64,2048]{1,0:T(8,128)(2,1)S(1)}, bf16[64,2048]{1,0:T(8,128)(2,1)S(1)}, u32[]{:S(2)}, u32[]{:S(2)}) collective-permute-start(bf16[64,2048]{1,0:T(8,128)(2,1)S(1)} %get-tuple-element.113.refs_0_), channel_id=1, source_target_pairs={{0,2},{1,5},{2,0},{3,7},{4,6},{5,1},{6,4},{7,3},{8,10},{9,13},{10,... | collective-permute-start | bytes 786440 | tf_op jit(solution)/shard_map/ppermute | solution.py:499
  61.4 1.1 %collective-permute-start.18 = (f32[8,2176]{1,0:T(8,128)S(1)}, f32[8,2176]{1,0:T(8,128)S(1)}, u32[]{:S(2)}, u32[]{:S(2)}) collective-permute-start(f32[8,2176]{1,0:T(8,128)S(1)} %get-tuple-element.123), channel_id=1, source_target_pairs={{0,16},{1,17},{2,18},{3,19},{4,20},{5,21},{6,22},{7,23},{8,24},{9,... | collective-permute-start | bytes 208904 | tf_op jit(solution)/shard_map/ppermute | solution.py:499
  62.5 1.6 %collective-permute-start.19 = (f32[8,2176]{1,0:T(8,128)S(1)}, f32[8,2176]{1,0:T(8,128)S(1)}, u32[]{:S(2)}, u32[]{:S(2)}) collective-permute-start(f32[8,2176]{1,0:T(8,128)S(1)} %get-tuple-element.124), channel_id=1, source_target_pairs={{0,24},{1,25},{2,26},{3,27},{4,28},{5,29},{6,30},{7,31},{8,16},{9,... | collective-permute-start | bytes 208904 | tf_op jit(solution)/shard_map/ppermute | solution.py:499
  64.1 3.6 %shard_map.131 = (bf16[2048,256]{1,0:T(8,128)(2,1)S(1)}, bf16[256,2048]{1,0:T(8,128)(2,1)S(1)}, bf16[512,256]{1,0:T(8,128)(2,1)S(1)}) custom-call(f32[1,128]{1,0:T(1,128)S(1)} %shard_map.120.energy_ref, s32[1]{0:T(128)} %bitcast.3.own_ref, bf16[2048,1024]{1,0:T(8,128)(2,1)S(1)} %shard_map.113.left_ref, bf16[2048,1024]{1,0:T(8,128)(2,1)S(1)} %shard_map.115.right_ref, ...), custom_call_target="tpu_custom_call" | custom-call | flops 2147483648 | tf_op jit(solution)/shard_map/pallas_call | solution.py:25
  70.2 3.6 %shard_map.134 = (bf16[2048,256]{1,0:T(8,128)(2,1)S(1)}, bf16[256,2048]{1,0:T(8,128)(2,1)S(1)}, bf16[512,256]{1,0:T(8,128)(2,1)S(1)}) custom-call(f32[1,128]{1,0:T(1,128)S(1)} %shard_map.120.energy_ref, s32[1]{0:T(128)} %bitcast.3.own_ref, bf16[2048,1024]{1,0:T(8,128)(2,1)S(1)} %shard_map.113.left_ref, bf16[2048,1024]{1,0:T(8,128)(2,1)S(1)} %shard_map.115.right_ref, ...), custom_call_target="tpu_custom_call" | custom-call | flops 2147483648 | tf_op jit(solution)/shard_map/pallas_call | solution.py:25
  73.8 2.5 %shard_map.133 = (bf16[256,2048]{1,0:T(8,128)(2,1)S(1)}, bf16[256,512]{1,0:T(8,128)(2,1)S(1)}) custom-call(s32[1]{0:T(128)} %bitcast.3.own_ref, bf16[2048,2048]{1,0:T(8,128)(2,1)S(1)} %shard_map.118.dec_ref, f32[1,2048]{1,0:T(1,128)S(1)} %get-tuple-element.106.norms_ref.row_ref, bf16[256,2048]{1,0:T(8,128)(2,1)S(1)} %get-tuple-element.121.refs_0_, ...), custom_call_target="tpu_custom_call" | custom-call | flops 2147483648 | tf_op jit(solution)/shard_map/pallas_call | solution.py:25
  76.4 2.0 %collective-permute-done.21.refs_1_ = bf16[64,2048]{1,0:T(8,128)(2,1)S(1)} collective-permute-done((bf16[64,2048]{1,0:T(8,128)(2,1)S(1)}, bf16[64,2048]{1,0:T(8,128)(2,1)S(1)}, u32[]{:S(2)}, u32[]{:S(2)}) %collective-permute-start.21) | collective-permute-done | bytes 262176 | tf_op jit(solution)/shard_map/ppermute | solution.py:499
  78.5 1.8 %collective-permute-done.23.refs_12_ = bf16[128,2048]{1,0:T(8,128)(2,1)S(1)} collective-permute-done((bf16[128,2048]{1,0:T(8,128)(2,1)S(1)}, bf16[128,2048]{1,0:T(8,128)(2,1)S(1)}, u32[]{:S(2)}, u32[]{:S(2)}) %collective-permute-start.23) | collective-permute-done | bytes 524320 | tf_op jit(solution)/shard_map/ppermute | solution.py:499
  82.2 8.2 %shard_map.137 = (f32[512,2048]{1,0:T(8,128)S(1)}, f32[2048,512]{1,0:T(8,128)S(1)}, f32[2048,1]{1,0:T(8,128)S(1)}) custom-call(s32[1]{0:T(128)} %bitcast.3.own_ref, bf16[2048,2048]{1,0:T(8,128)(2,1)S(1)} %shard_map.118.dec_ref, f32[1,2048]{1,0:T(1,128)S(1)} %get-tuple-element.106.norms_ref.row_ref, bf16[512,256]{1,0:T(8,128)(2,1)S(1)} %get-tuple-element.111.refs_0_, ...), custom_call_target="tpu_custom_call" | custom-call | flops 4294967296 | tf_op jit(solution)/shard_map/pallas_call | solution.py:25
  92.4 6.2 %shard_map.140 = (f32[512,2048]{1,0:T(8,128)}, f32[2048,512]{1,0:T(8,128)}) custom-call(f32[1,128]{1,0:T(1,128)S(1)} %shard_map.120.energy_ref, s32[1]{0:T(128)} %bitcast.3.own_ref, f32[2048,1]{1,0:T(8,128)S(1)} %get-tuple-element.144.column_ref, f32[1,2048]{1,0:T(1,128)S(1)} %get-tuple-element.106.norms_ref.row_ref, ...), custom_call_target="tpu_custom_call" | custom-call | flops 3221225472 | tf_op jit(solution)/shard_map/pallas_call | solution.py:25
  (59 shorter events, 11.8 us)
Async XLA Ops:
  0.6 0.7 copy-start.2
  4.3 11.7 %collective-permute-start.5 = (bf16[32,2048]{1,0:T(8,128)(2,1)S(1)}, bf16[32,2048]{1,0:T(8,128)(2,1)S(1)}, u32[]{:S(2)}, u32[]{:S(2)}) collective-permute-start(bf16[32,2048]{1,0:T(8,128)(2,1)S(1)} %get-tuple-element.90.refs_0_), channel_id=1, source_target_pairs={{0,4},{1,3},{2,6},{3,1},{4,0},{5,7},{6,2},{7,5},{8,12},{9,11},{10,... | collective-permute-start | bytes 393224 | tf_op jit(solution)/shard_map/ppermute | solution.py:499
  8.4 3.7 %collective-permute-start = (f32[1,128]{1,0:T(1,128)S(1)}, f32[1,128]{1,0:T(1,128)S(1)}, u32[]{:S(2)}, u32[]{:S(2)}) collective-permute-start(f32[1,128]{1,0:T(1,128)S(1)} %get-tuple-element.83.a_ref), channel_id=1, source_target_pairs={{0,8},{1,17},{2,10},{3,19},{4,12},{5,21},{6,14},{7,23},{8,0},{9,25... | collective-permute-start | bytes 1544 | tf_op jit(solution)/shard_map/ppermute | solution.py:499
  12.1 3.8 %collective-permute-start.1 = (f32[1,128]{1,0:T(1,128)S(1)}, f32[1,128]{1,0:T(1,128)S(1)}, u32[]{:S(2)}, u32[]{:S(2)}) collective-permute-start(f32[1,128]{1,0:T(1,128)S(1)} %shard_map.114.a_ref), channel_id=1, source_target_pairs={{0,16},{1,9},{2,18},{3,11},{4,20},{5,13},{6,22},{7,15},{8,24},{9,1... | collective-permute-start | bytes 1544 | tf_op jit(solution)/shard_map/ppermute | solution.py:499
  16.0 10.8 %collective-permute-start.6 = (bf16[64,2048]{1,0:T(8,128)(2,1)S(1)}, bf16[64,2048]{1,0:T(8,128)(2,1)S(1)}, u32[]{:S(2)}, u32[]{:S(2)}) collective-permute-start(bf16[64,2048]{1,0:T(8,128)(2,1)S(1)} %shard_map.121.refs_0_.heads_ref), channel_id=1, source_target_pairs={{0,2},{1,5},{2,0},{3,7},{4,6},{5,1},{6,4},{7,3},{8,10},{9,13},{10,... | collective-permute-start | bytes 786440 | tf_op jit(solution)/shard_map/ppermute | solution.py:499
  17.6 1.1 %collective-permute-start.2 = (f32[1,128]{1,0:T(1,128)S(1)}, f32[1,128]{1,0:T(1,128)S(1)}, u32[]{:S(2)}, u32[]{:S(2)}) collective-permute-start(f32[1,128]{1,0:T(1,128)S(1)} %shard_map.116.a_ref), channel_id=1, source_target_pairs={{0,1},{1,0},{2,3},{3,2},{4,5},{5,4},{6,7},{7,6},{8,9},{9,8},{10,11... | collective-permute-start | bytes 1544 | tf_op jit(solution)/shard_map/ppermute | solution.py:499
  18.8 10.0 %copy-start = (f32[2048]{0:T(1024)S(1)}, f32[2048]{0:T(1024)}, u32[]{:S(2)}) copy-start(f32[2048]{0:T(1024)} %param.15) | copy-start | bytes 24580
  18.8 4.4 %collective-permute-start.3 = (f32[1,128]{1,0:T(1,128)S(1)}, f32[1,128]{1,0:T(1,128)S(1)}, u32[]{:S(2)}, u32[]{:S(2)}) collective-permute-start(f32[1,128]{1,0:T(1,128)S(1)} %shard_map.117.a_ref), channel_id=1, source_target_pairs={{0,4},{1,3},{2,6},{3,1},{4,0},{5,7},{6,2},{7,5},{8,12},{9,11},{10,... | collective-permute-start | bytes 1544 | tf_op jit(solution)/shard_map/ppermute | solution.py:499
  23.2 3.5 %collective-permute-start.4 = (f32[1,128]{1,0:T(1,128)S(1)}, f32[1,128]{1,0:T(1,128)S(1)}, u32[]{:S(2)}, u32[]{:S(2)}) collective-permute-start(f32[1,128]{1,0:T(1,128)S(1)} %shard_map.119.a_ref), channel_id=1, source_target_pairs={{0,2},{1,5},{2,0},{3,7},{4,6},{5,1},{6,4},{7,3},{8,10},{9,13},{10,... | collective-permute-start | bytes 1544 | tf_op jit(solution)/shard_map/ppermute | solution.py:499
  26.8 2.0 %collective-permute-start.7 = (bf16[128,2048]{1,0:T(8,128)(2,1)S(1)}, bf16[128,2048]{1,0:T(8,128)(2,1)S(1)}, u32[]{:S(2)}, u32[]{:S(2)}) collective-permute-start(bf16[128,2048]{1,0:T(8,128)(2,1)S(1)} %shard_map.122.refs_0_), channel_id=1, source_target_pairs={{0,1},{1,0},{2,3},{3,2},{4,5},{5,4},{6,7},{7,6},{8,9},{9,8},{10,11... | collective-permute-start | bytes 1572872 | tf_op jit(solution)/shard_map/ppermute | solution.py:499
  26.9 9.2 %collective-permute-start.8 = (bf16[128,2048]{1,0:T(8,128)(2,1)S(1)}, bf16[128,2048]{1,0:T(8,128)(2,1)S(1)}, u32[]{:S(2)}, u32[]{:S(2)}) collective-permute-start(bf16[128,2048]{1,0:T(8,128)(2,1)S(1)} %shard_map.122.refs_0_), channel_id=1, source_target_pairs={{0,8},{1,17},{2,10},{3,19},{4,12},{5,21},{6,14},{7,23},{8,0},{9,25... | collective-permute-start | bytes 1572872 | tf_op jit(solution)/shard_map/ppermute | solution.py:499
  36.1 1.9 %collective-permute-start.9 = (bf16[128,2048]{1,0:T(8,128)(2,1)S(1)}, bf16[128,2048]{1,0:T(8,128)(2,1)S(1)}, u32[]{:S(2)}, u32[]{:S(2)}) collective-permute-start(bf16[128,2048]{1,0:T(8,128)(2,1)S(1)} %get-tuple-element.95), channel_id=1, source_target_pairs={{0,1},{1,0},{2,3},{3,2},{4,5},{5,4},{6,7},{7,6},{8,9},{9,8},{10,11... | collective-permute-start | bytes 1572872 | tf_op jit(solution)/shard_map/ppermute | solution.py:499
  38.2 19.2 %collective-permute-start.13 = (bf16[256,2048]{1,0:T(8,128)(2,1)S(1)}, bf16[256,2048]{1,0:T(8,128)(2,1)S(1)}, u32[]{:S(2)}, u32[]{:S(2)}) collective-permute-start(bf16[256,2048]{1,0:T(8,128)(2,1)S(1)} %shard_map.128), channel_id=1, source_target_pairs={{0,16},{1,9},{2,18},{3,11},{4,20},{5,13},{6,22},{7,15},{8,24},{9,1... | collective-permute-start | bytes 3145736 | tf_op jit(solution)/shard_map/ppermute | solution.py:499
  39.6 1.9 %collective-permute-start.11 = (bf16[128,2048]{1,0:T(8,128)(2,1)S(1)}, bf16[128,2048]{1,0:T(8,128)(2,1)S(1)}, u32[]{:S(2)}, u32[]{:S(2)}) collective-permute-start(bf16[128,2048]{1,0:T(8,128)(2,1)S(1)} %collective-permute-done.8.refs_0_.refs_1_), channel_id=1, source_target_pairs={{0,1},{1,0},{2,3},{3,2},{4,5},{5,4},{6,7},{7,6},{8,9},{9,8},{10,11... | collective-permute-start | bytes 1572872 | tf_op jit(solution)/shard_map/ppermute | solution.py:499
  39.6 8.1 %collective-permute-start.10 = (bf16[64,2048]{1,0:T(8,128)(2,1)S(1)}, bf16[64,2048]{1,0:T(8,128)(2,1)S(1)}, u32[]{:S(2)}, u32[]{:S(2)}) collective-permute-start(bf16[64,2048]{1,0:T(8,128)(2,1)S(1)} %get-tuple-element.97), channel_id=1, source_target_pairs={{0,2},{1,5},{2,0},{3,7},{4,6},{5,1},{6,4},{7,3},{8,10},{9,13},{10,... | collective-permute-start | bytes 786440 | tf_op jit(solution)/shard_map/ppermute | solution.py:499
  47.7 9.7 %copy-start.1 = (f32[2048]{0:T(1024)S(1)}, f32[2048]{0:T(1024)}, u32[]{:S(2)}) copy-start(f32[2048]{0:T(1024)} %param.17) | copy-start | bytes 24580
  47.8 12.4 %copy-start.3 = (s32[32]{0:T(128)S(1)}, s32[32]{0:T(128)}, u32[]{:S(2)}) copy-start(s32[32]{0:T(128)} %param.13) | copy-start | bytes 388
  47.8 9.7 %collective-permute-start.12 = (bf16[64,2048]{1,0:T(8,128)(2,1)S(1)}, bf16[64,2048]{1,0:T(8,128)(2,1)S(1)}, u32[]{:S(2)}, u32[]{:S(2)}) collective-permute-start(bf16[64,2048]{1,0:T(8,128)(2,1)S(1)} %get-tuple-element.104), channel_id=1, source_target_pairs={{0,4},{1,3},{2,6},{3,1},{4,0},{5,7},{6,2},{7,5},{8,12},{9,11},{10,... | collective-permute-start | bytes 786440 | tf_op jit(solution)/shard_map/ppermute | solution.py:499
  57.6 4.8 %collective-permute-start.14 = (bf16[256,2048]{1,0:T(8,128)(2,1)S(1)}, bf16[256,2048]{1,0:T(8,128)(2,1)S(1)}, u32[]{:S(2)}, u32[]{:S(2)}) collective-permute-start(bf16[256,2048]{1,0:T(8,128)(2,1)S(1)} %collective-permute-done.13.refs_0_), channel_id=1, source_target_pairs={{0,1},{1,0},{2,3},{3,2},{4,5},{5,4},{6,7},{7,6},{8,9},{9,8},{10,11... | collective-permute-start | bytes 3145736 | tf_op jit(solution)/shard_map/ppermute | solution.py:499
  57.8 9.9 %collective-permute-start.16 = (bf16[64,2048]{1,0:T(8,128)(2,1)S(1)}, bf16[64,2048]{1,0:T(8,128)(2,1)S(1)}, u32[]{:S(2)}, u32[]{:S(2)}) collective-permute-start(bf16[64,2048]{1,0:T(8,128)(2,1)S(1)} %get-tuple-element.113.refs_0_), channel_id=1, source_target_pairs={{0,8},{1,17},{2,10},{3,19},{4,12},{5,21},{6,14},{7,23},{8,0},{9,25... | collective-permute-start | bytes 786440 | tf_op jit(solution)/shard_map/ppermute | solution.py:499
  59.0 9.0 %collective-permute-start.15 = (bf16[64,2048]{1,0:T(8,128)(2,1)S(1)}, bf16[64,2048]{1,0:T(8,128)(2,1)S(1)}, u32[]{:S(2)}, u32[]{:S(2)}) collective-permute-start(bf16[64,2048]{1,0:T(8,128)(2,1)S(1)} %get-tuple-element.113.refs_0_), channel_id=1, source_target_pairs={{0,2},{1,5},{2,0},{3,7},{4,6},{5,1},{6,4},{7,3},{8,10},{9,13},{10,... | collective-permute-start | bytes 786440 | tf_op jit(solution)/shard_map/ppermute | solution.py:499
  60.5 7.1 %collective-permute-start.17 = (f32[8,2176]{1,0:T(8,128)S(1)}, f32[8,2176]{1,0:T(8,128)S(1)}, u32[]{:S(2)}, u32[]{:S(2)}) collective-permute-start(f32[8,2176]{1,0:T(8,128)S(1)} %get-tuple-element.122), channel_id=1, source_target_pairs={{0,8},{1,9},{2,10},{3,11},{4,12},{5,13},{6,14},{7,15},{8,0},{9,1},... | collective-permute-start | bytes 208904 | tf_op jit(solution)/shard_map/ppermute | solution.py:499
  61.4 6.3 %collective-permute-start.18 = (f32[8,2176]{1,0:T(8,128)S(1)}, f32[8,2176]{1,0:T(8,128)S(1)}, u32[]{:S(2)}, u32[]{:S(2)}) collective-permute-start(f32[8,2176]{1,0:T(8,128)S(1)} %get-tuple-element.123), channel_id=1, source_target_pairs={{0,16},{1,17},{2,18},{3,19},{4,20},{5,21},{6,22},{7,23},{8,24},{9,... | collective-permute-start | bytes 208904 | tf_op jit(solution)/shard_map/ppermute | solution.py:499
  62.5 5.2 %collective-permute-start.19 = (f32[8,2176]{1,0:T(8,128)S(1)}, f32[8,2176]{1,0:T(8,128)S(1)}, u32[]{:S(2)}, u32[]{:S(2)}) collective-permute-start(f32[8,2176]{1,0:T(8,128)S(1)} %get-tuple-element.124), channel_id=1, source_target_pairs={{0,24},{1,25},{2,26},{3,27},{4,28},{5,29},{6,30},{7,31},{8,16},{9,... | collective-permute-start | bytes 208904 | tf_op jit(solution)/shard_map/ppermute | solution.py:499
  68.1 5.7 %collective-permute-start.20 = (bf16[128,2048]{1,0:T(8,128)(2,1)S(1)}, bf16[128,2048]{1,0:T(8,128)(2,1)S(1)}, u32[]{:S(2)}, u32[]{:S(2)}) collective-permute-start(bf16[128,2048]{1,0:T(8,128)(2,1)S(1)} %shard_map.132.refs_1_), channel_id=1, source_target_pairs={{0,1},{1,0},{2,3},{3,2},{4,5},{5,4},{6,7},{7,6},{8,9},{9,8},{10,11... | collective-permute-start | bytes 1572872 | tf_op jit(solution)/shard_map/ppermute | solution.py:499
  68.2 12.1 %collective-permute-start.23 = (bf16[128,2048]{1,0:T(8,128)(2,1)S(1)}, bf16[128,2048]{1,0:T(8,128)(2,1)S(1)}, u32[]{:S(2)}, u32[]{:S(2)}) collective-permute-start(bf16[128,2048]{1,0:T(8,128)(2,1)S(1)} %shard_map.136), channel_id=1, source_target_pairs={{0,16},{1,9},{2,18},{3,11},{4,20},{5,13},{6,22},{7,15},{8,24},{9,1... | collective-permute-start | bytes 1572872 | tf_op jit(solution)/shard_map/ppermute | solution.py:499
  69.2 9.2 %collective-permute-start.21 = (bf16[64,2048]{1,0:T(8,128)(2,1)S(1)}, bf16[64,2048]{1,0:T(8,128)(2,1)S(1)}, u32[]{:S(2)}, u32[]{:S(2)}) collective-permute-start(bf16[64,2048]{1,0:T(8,128)(2,1)S(1)} %collective-permute-done.15.refs_1_.refs_0_), channel_id=1, source_target_pairs={{0,8},{1,17},{2,10},{3,19},{4,12},{5,21},{6,14},{7,23},{8,0},{9,25... | collective-permute-start | bytes 786440 | tf_op jit(solution)/shard_map/ppermute | solution.py:499
  78.4 2.8 %collective-permute-start.22 = (bf16[128,2048]{1,0:T(8,128)(2,1)S(1)}, bf16[128,2048]{1,0:T(8,128)(2,1)S(1)}, u32[]{:S(2)}, u32[]{:S(2)}) collective-permute-start(bf16[128,2048]{1,0:T(8,128)(2,1)S(1)} %shard_map.135.refs_10_), channel_id=1, source_target_pairs={{0,1},{1,0},{2,3},{3,2},{4,5},{5,4},{6,7},{7,6},{8,9},{9,8},{10,11... | collective-permute-start | bytes 1572872 | tf_op jit(solution)/shard_map/ppermute | solution.py:499
  80.3 1.9 %collective-permute-start.24 = (bf16[128,2048]{1,0:T(8,128)(2,1)S(1)}, bf16[128,2048]{1,0:T(8,128)(2,1)S(1)}, u32[]{:S(2)}, u32[]{:S(2)}) collective-permute-start(bf16[128,2048]{1,0:T(8,128)(2,1)S(1)} %collective-permute-done.23.refs_12_), channel_id=1, source_target_pairs={{0,1},{1,0},{2,3},{3,2},{4,5},{5,4},{6,7},{7,6},{8,9},{9,8},{10,11... | collective-permute-start | bytes 1572872 | tf_op jit(solution)/shard_map/ppermute | solution.py:499
  80.3 10.1 %collective-permute-start.25 = (bf16[128,2048]{1,0:T(8,128)(2,1)S(1)}, bf16[128,2048]{1,0:T(8,128)(2,1)S(1)}, u32[]{:S(2)}, u32[]{:S(2)}) collective-permute-start(bf16[128,2048]{1,0:T(8,128)(2,1)S(1)} %shard_map.139), channel_id=1, source_target_pairs={{0,16},{1,9},{2,18},{3,11},{4,20},{5,13},{6,22},{7,15},{8,24},{9,1... | collective-permute-start | bytes 1572872 | tf_op jit(solution)/shard_map/ppermute | solution.py:499
  90.5 2.0 %collective-permute-start.26 = (bf16[128,2048]{1,0:T(8,128)(2,1)S(1)}, bf16[128,2048]{1,0:T(8,128)(2,1)S(1)}, u32[]{:S(2)}, u32[]{:S(2)}) collective-permute-start(bf16[128,2048]{1,0:T(8,128)(2,1)S(1)} %collective-permute-done.25.refs_0_), channel_id=1, source_target_pairs={{0,1},{1,0},{2,3},{3,2},{4,5},{5,4},{6,7},{7,6},{8,9},{9,8},{10,11... | collective-permute-start | bytes 1572872 | tf_op jit(solution)/shard_map/ppermute | solution.py:499

commit v6 on v5

--- a/solution.py
+++ b/solution.py
@@ -637,8 +637,8 @@
         encoded.append(encode(entries, energy, own, enc, bias, parts, columns))
         return encoded[-1][0]
 
-    arrived = swap(after(send, hop), *core)
-    total = keep
+    arrived = swap(send, *core)
+    total = after(keep, hop)
     far = [rows, hop]
     for number, mask in enumerate(line[::-1]):
         last = number == len(line) - 1

time: 99 us -> 96.9 us (0.979)
  waiting for transfers between devices: 23.8 us -> 21.3 us
    ppermute x27, waiting for transfers between devices: 23.8 us -> 21.3 us  [swap(): lax.ppermute(x, ('dp', 'latent'), [(i, i ^ (odd if i & 1 else even)) for...]
  transfers between devices with their start and end apart: 27 -> 27, of which waited for: 14 -> 14; matrix products, arithmetic and copies ran while one was open for 0% -> 0% of each run, Pallas kernels for 39% -> 40%
where the time goes in v6:
time: 96.9 us; the launch traced here: 96.7 us
  Pallas kernels  48.4 us (50%)
  starting transfers between devices  25.3 us (26%)
  waiting for transfers between devices  21.3 us (22%)
  between operations  1.09 us (1%)
    pallas_call x29, Pallas kernels, kernel_call(): pl.pallas_call(body, in_specs=specs, out_specs=out_specs or [IN_VMEM] * l...  48.4 us
    ppermute x27, starting transfers between devices, swap(): lax.ppermute(x, ('dp', 'latent'), [(i, i ^ (odd if i & 1 else even)) for...  25.3 us
    ppermute x27, waiting for transfers between devices, swap(): lax.ppermute(x, ('dp', 'latent'), [(i, i ^ (odd if i & 1 else even)) for...  21.3 us
  transfers between devices with their start and end apart: 27, of which 14 were waited for; matrix products, arithmetic and copies ran while one was open for 0% of the time, Pallas kernels for 40%

profile of v6, /device:TPU:0, one launch (start us, length us, event | category | flops | bytes accessed | tf_op | source)
XLA Modules:
  0.0 96.7 jit_solution(14030796839481669179)
XLA Ops:
  1.3 3.0 %shard_map.112 = (bf16[32,2048]{1,0:T(8,128)(2,1)S(1)}, f32[1,128]{1,0:T(1,128)S(1)}) custom-call(s32[32]{0:T(128)S(1)} %copy-done.2, bf16[32,2048]{1,0:T(8,128)(2,1)} %queries, bf16[1,512,1024]{2,1,0:T(8,128)(2,1)} %keys.1, bf16[1,512,1024]{2,1,0:T(8,128)(2,1)} %values.1), custom_call_target="tpu_custom_call" | custom-call | flops 134217728 | tf_op jit(solution)/shard_map/pallas_call | solution.py:25
  4.3 4.1 %collective-permute-start.5 = (bf16[32,2048]{1,0:T(8,128)(2,1)S(1)}, bf16[32,2048]{1,0:T(8,128)(2,1)S(1)}, u32[]{:S(2)}, u32[]{:S(2)}) collective-permute-start(bf16[32,2048]{1,0:T(8,128)(2,1)S(1)} %get-tuple-element.90.refs_0_), channel_id=1, source_target_pairs={{0,4},{1,3},{2,6},{3,1},{4,0},{5,7},{6,2},{7,5},{8,12},{9,11},{10,... | collective-permute-start | bytes 393224 | tf_op jit(solution)/shard_map/ppermute | solution.py:499
  8.4 1.5 %collective-permute-start = (f32[1,128]{1,0:T(1,128)S(1)}, f32[1,128]{1,0:T(1,128)S(1)}, u32[]{:S(2)}, u32[]{:S(2)}) collective-permute-start(f32[1,128]{1,0:T(1,128)S(1)} %get-tuple-element.83.a_ref), channel_id=1, source_target_pairs={{0,8},{1,17},{2,10},{3,19},{4,12},{5,21},{6,14},{7,23},{8,0},{9,25... | collective-permute-start | bytes 1544 | tf_op jit(solution)/shard_map/ppermute | solution.py:499
  9.9 2.2 %shard_map.113.left_ref = bf16[2048,1024]{1,0:T(8,128)(2,1)S(1)} custom-call(bf16[2048,2048]{1,0:T(8,128)(2,1)} %source.1), custom_call_target="tpu_custom_call" | custom-call | tf_op jit(solution)/shard_map/pallas_call | solution.py:25
  12.1 1.6 %collective-permute-start.1 = (f32[1,128]{1,0:T(1,128)S(1)}, f32[1,128]{1,0:T(1,128)S(1)}, u32[]{:S(2)}, u32[]{:S(2)}) collective-permute-start(f32[1,128]{1,0:T(1,128)S(1)} %shard_map.114.a_ref), channel_id=1, source_target_pairs={{0,16},{1,9},{2,18},{3,11},{4,20},{5,13},{6,22},{7,15},{8,24},{9,1... | collective-permute-start | bytes 1544 | tf_op jit(solution)/shard_map/ppermute | solution.py:499
  13.7 2.2 %shard_map.115.right_ref = bf16[2048,1024]{1,0:T(8,128)(2,1)S(1)} custom-call(bf16[2048,2048]{1,0:T(8,128)(2,1)} %source.1), custom_call_target="tpu_custom_call" | custom-call | tf_op jit(solution)/shard_map/pallas_call | solution.py:25
  16.0 1.6 %collective-permute-start.6 = (bf16[64,2048]{1,0:T(8,128)(2,1)S(1)}, bf16[64,2048]{1,0:T(8,128)(2,1)S(1)}, u32[]{:S(2)}, u32[]{:S(2)}) collective-permute-start(bf16[64,2048]{1,0:T(8,128)(2,1)S(1)} %shard_map.121.refs_0_.heads_ref), channel_id=1, source_target_pairs={{0,2},{1,5},{2,0},{3,7},{4,6},{5,1},{6,4},{7,3},{8,10},{9,13},{10,... | collective-permute-start | bytes 786440 | tf_op jit(solution)/shard_map/ppermute | solution.py:499
  17.6 1.1 %collective-permute-done.2.b_ref = f32[1,128]{1,0:T(1,128)S(1)} collective-permute-done((f32[1,128]{1,0:T(1,128)S(1)}, f32[1,128]{1,0:T(1,128)S(1)}, u32[]{:S(2)}, u32[]{:S(2)}) %collective-permute-start.2) | collective-permute-done | bytes 544 | tf_op jit(solution)/shard_map/ppermute | solution.py:499
  19.1 3.5 %shard_map.118.dec_ref = bf16[2048,2048]{1,0:T(8,128)(2,1)S(1)} custom-call(bf16[2048,2048]{1,0:T(8,128)(2,1)} %source.2), custom_call_target="tpu_custom_call" | custom-call | tf_op jit(solution)/shard_map/pallas_call | solution.py:25
  23.7 3.1 %collective-permute-done.4.b_ref = f32[1,128]{1,0:T(1,128)S(1)} collective-permute-done((f32[1,128]{1,0:T(1,128)S(1)}, f32[1,128]{1,0:T(1,128)S(1)}, u32[]{:S(2)}, u32[]{:S(2)}) %collective-permute-start.4) | collective-permute-done | bytes 544 | tf_op jit(solution)/shard_map/ppermute | solution.py:499
  26.9 1.3 %collective-permute-start.8 = (bf16[128,2048]{1,0:T(8,128)(2,1)S(1)}, bf16[128,2048]{1,0:T(8,128)(2,1)S(1)}, u32[]{:S(2)}, u32[]{:S(2)}) collective-permute-start(bf16[128,2048]{1,0:T(8,128)(2,1)S(1)} %shard_map.122.refs_0_), channel_id=1, source_target_pairs={{0,8},{1,17},{2,10},{3,19},{4,12},{5,21},{6,14},{7,23},{8,0},{9,25... | collective-permute-start | bytes 1572872 | tf_op jit(solution)/shard_map/ppermute | solution.py:499
  28.8 5.6 %shard_map.123 = (bf16[2048,256]{1,0:T(8,128)(2,1)S(1)}, bf16[256,2048]{1,0:T(8,128)(2,1)S(1)}, bf16[512,256]{1,0:T(8,128)(2,1)S(1)}, f32[128,2048]{1,0:T(8,128)S(1)}, bf16[128,2048]{1,0:T(8,128)(2,1)S(1)}) custom-call(f32[1,128]{1,0:T(1,128)S(1)} %shard_map.120.energy_ref, s32[1]{0:T(128)} %bitcast.3.own_ref, bf16[2048,1024]{1,0:T(8,128)(2,1)S(1)} %shard_map.113.left_ref, ...), custom_call_target="tpu_custom_call" | custom-call | flops 4294967296 | tf_op jit(solution)/shard_map/pallas_call | solution.py:25
  34.6 1.5 %collective-permute-done.8.refs_0_.refs_1_ = bf16[128,2048]{1,0:T(8,128)(2,1)S(1)} collective-permute-done((bf16[128,2048]{1,0:T(8,128)(2,1)S(1)}, bf16[128,2048]{1,0:T(8,128)(2,1)S(1)}, u32[]{:S(2)}, u32[]{:S(2)}) %collective-permute-start.8) | collective-permute-done | bytes 524320 | tf_op jit(solution)/shard_map/ppermute | solution.py:499
  36.6 1.3 %collective-permute-start.13 = (bf16[256,2048]{1,0:T(8,128)(2,1)S(1)}, bf16[256,2048]{1,0:T(8,128)(2,1)S(1)}, u32[]{:S(2)}, u32[]{:S(2)}) collective-permute-start(bf16[256,2048]{1,0:T(8,128)(2,1)S(1)} %shard_map.128), channel_id=1, source_target_pairs={{0,16},{1,9},{2,18},{3,11},{4,20},{5,13},{6,22},{7,15},{8,24},{9,1... | collective-permute-start | bytes 3145736 | tf_op jit(solution)/shard_map/ppermute | solution.py:499
  38.4 1.4 %collective-permute-done.11.refs_1_ = bf16[128,2048]{1,0:T(8,128)(2,1)S(1)} collective-permute-done((bf16[128,2048]{1,0:T(8,128)(2,1)S(1)}, bf16[128,2048]{1,0:T(8,128)(2,1)S(1)}, u32[]{:S(2)}, u32[]{:S(2)}) %collective-permute-start.11) | collective-permute-done | bytes 524320 | tf_op jit(solution)/shard_map/ppermute | solution.py:499
  39.8 3.6 %shard_map.125 = (bf16[2048,256]{1,0:T(8,128)(2,1)S(1)}, bf16[256,2048]{1,0:T(8,128)(2,1)S(1)}, bf16[512,256]{1,0:T(8,128)(2,1)S(1)}) custom-call(f32[1,128]{1,0:T(1,128)S(1)} %shard_map.120.energy_ref, s32[1]{0:T(128)} %bitcast.3.own_ref, bf16[2048,1024]{1,0:T(8,128)(2,1)S(1)} %shard_map.113.left_ref, bf16[2048,1024]{1,0:T(8,128)(2,1)S(1)} %shard_map.115.right_ref, ...), custom_call_target="tpu_custom_call" | custom-call | flops 2147483648 | tf_op jit(solution)/shard_map/pallas_call | solution.py:25
  43.4 2.2 %collective-permute-done.10.b_ref = bf16[64,2048]{1,0:T(8,128)(2,1)S(1)} collective-permute-done((bf16[64,2048]{1,0:T(8,128)(2,1)S(1)}, bf16[64,2048]{1,0:T(8,128)(2,1)S(1)}, u32[]{:S(2)}, u32[]{:S(2)}) %collective-permute-start.10) | collective-permute-done | bytes 262176 | tf_op jit(solution)/shard_map/ppermute | solution.py:499
  45.7 2.5 %collective-permute-start.12 = (bf16[64,2048]{1,0:T(8,128)(2,1)S(1)}, bf16[64,2048]{1,0:T(8,128)(2,1)S(1)}, u32[]{:S(2)}, u32[]{:S(2)}) collective-permute-start(bf16[64,2048]{1,0:T(8,128)(2,1)S(1)} %get-tuple-element.104), channel_id=1, source_target_pairs={{0,4},{1,3},{2,6},{3,1},{4,0},{5,7},{6,2},{7,5},{8,12},{9,11},{10,... | collective-permute-start | bytes 786440 | tf_op jit(solution)/shard_map/ppermute | solution.py:499
  48.2 2.3 %shard_map.127 = (f32[2048,1]{1,0:T(8,128)S(1)}, f32[1,2048]{1,0:T(1,128)S(1)}) custom-call(bf16[2048,2048]{1,0:T(8,128)(2,1)S(1)} %shard_map.118.dec_ref), custom_call_target="tpu_custom_call" | custom-call | tf_op jit(solution)/shard_map/pallas_call | solution.py:25
  50.5 5.0 %collective-permute-done.12.b_ref = bf16[64,2048]{1,0:T(8,128)(2,1)S(1)} collective-permute-done((bf16[64,2048]{1,0:T(8,128)(2,1)S(1)}, bf16[64,2048]{1,0:T(8,128)(2,1)S(1)}, u32[]{:S(2)}, u32[]{:S(2)}) %collective-permute-start.12) | collective-permute-done | bytes 262176 | tf_op jit(solution)/shard_map/ppermute | solution.py:499
  55.9 1.2 %collective-permute-start.16 = (bf16[64,2048]{1,0:T(8,128)(2,1)S(1)}, bf16[64,2048]{1,0:T(8,128)(2,1)S(1)}, u32[]{:S(2)}, u32[]{:S(2)}) collective-permute-start(bf16[64,2048]{1,0:T(8,128)(2,1)S(1)} %get-tuple-element.113.refs_0_), channel_id=1, source_target_pairs={{0,8},{1,17},{2,10},{3,19},{4,12},{5,21},{6,14},{7,23},{8,0},{9,25... | collective-permute-start | bytes 786440 | tf_op jit(solution)/shard_map/ppermute | solution.py:499
  57.0 1.4 %collective-permute-start.15 = (bf16[64,2048]{1,0:T(8,128)(2,1)S(1)}, bf16[64,2048]{1,0:T(8,128)(2,1)S(1)}, u32[]{:S(2)}, u32[]{:S(2)}) collective-permute-start(bf16[64,2048]{1,0:T(8,128)(2,1)S(1)} %get-tuple-element.113.refs_0_), channel_id=1, source_target_pairs={{0,2},{1,5},{2,0},{3,7},{4,6},{5,1},{6,4},{7,3},{8,10},{9,13},{10,... | collective-permute-start | bytes 786440 | tf_op jit(solution)/shard_map/ppermute | solution.py:499
  59.5 1.3 %collective-permute-start.18 = (f32[8,2176]{1,0:T(8,128)S(1)}, f32[8,2176]{1,0:T(8,128)S(1)}, u32[]{:S(2)}, u32[]{:S(2)}) collective-permute-start(f32[8,2176]{1,0:T(8,128)S(1)} %get-tuple-element.123), channel_id=1, source_target_pairs={{0,16},{1,17},{2,18},{3,19},{4,20},{5,21},{6,22},{7,23},{8,24},{9,... | collective-permute-start | bytes 208904 | tf_op jit(solution)/shard_map/ppermute | solution.py:499
  60.8 1.5 %collective-permute-start.19 = (f32[8,2176]{1,0:T(8,128)S(1)}, f32[8,2176]{1,0:T(8,128)S(1)}, u32[]{:S(2)}, u32[]{:S(2)}) collective-permute-start(f32[8,2176]{1,0:T(8,128)S(1)} %get-tuple-element.124), channel_id=1, source_target_pairs={{0,24},{1,25},{2,26},{3,27},{4,28},{5,29},{6,30},{7,31},{8,16},{9,... | collective-permute-start | bytes 208904 | tf_op jit(solution)/shard_map/ppermute | solution.py:499
  62.3 3.6 %shard_map.131 = (bf16[2048,256]{1,0:T(8,128)(2,1)S(1)}, bf16[256,2048]{1,0:T(8,128)(2,1)S(1)}, bf16[512,256]{1,0:T(8,128)(2,1)S(1)}) custom-call(f32[1,128]{1,0:T(1,128)S(1)} %shard_map.120.energy_ref, s32[1]{0:T(128)} %bitcast.3.own_ref, bf16[2048,1024]{1,0:T(8,128)(2,1)S(1)} %shard_map.113.left_ref, bf16[2048,1024]{1,0:T(8,128)(2,1)S(1)} %shard_map.115.right_ref, ...), custom_call_target="tpu_custom_call" | custom-call | flops 2147483648 | tf_op jit(solution)/shard_map/pallas_call | solution.py:25
  67.2 1.1 %collective-permute-start.21 = (bf16[64,2048]{1,0:T(8,128)(2,1)S(1)}, bf16[64,2048]{1,0:T(8,128)(2,1)S(1)}, u32[]{:S(2)}, u32[]{:S(2)}) collective-permute-start(bf16[64,2048]{1,0:T(8,128)(2,1)S(1)} %collective-permute-done.15.refs_1_.refs_0_), channel_id=1, source_target_pairs={{0,8},{1,17},{2,10},{3,19},{4,12},{5,21},{6,14},{7,23},{8,0},{9,25... | collective-permute-start | bytes 786440 | tf_op jit(solution)/shard_map/ppermute | solution.py:499
  68.3 3.6 %shard_map.134 = (bf16[2048,256]{1,0:T(8,128)(2,1)S(1)}, bf16[256,2048]{1,0:T(8,128)(2,1)S(1)}, bf16[512,256]{1,0:T(8,128)(2,1)S(1)}) custom-call(f32[1,128]{1,0:T(1,128)S(1)} %shard_map.120.energy_ref, s32[1]{0:T(128)} %bitcast.3.own_ref, bf16[2048,1024]{1,0:T(8,128)(2,1)S(1)} %shard_map.113.left_ref, bf16[2048,1024]{1,0:T(8,128)(2,1)S(1)} %shard_map.115.right_ref, ...), custom_call_target="tpu_custom_call" | custom-call | flops 2147483648 | tf_op jit(solution)/shard_map/pallas_call | solution.py:25
  71.9 2.5 %shard_map.133 = (bf16[256,2048]{1,0:T(8,128)(2,1)S(1)}, bf16[256,512]{1,0:T(8,128)(2,1)S(1)}) custom-call(s32[1]{0:T(128)} %bitcast.3.own_ref, bf16[2048,2048]{1,0:T(8,128)(2,1)S(1)} %shard_map.118.dec_ref, f32[1,2048]{1,0:T(1,128)S(1)} %get-tuple-element.106.norms_ref.row_ref, bf16[256,2048]{1,0:T(8,128)(2,1)S(1)} %get-tuple-element.121.refs_0_, ...), custom_call_target="tpu_custom_call" | custom-call | flops 2147483648 | tf_op jit(solution)/shard_map/pallas_call | solution.py:25
  74.4 2.0 %collective-permute-done.21.refs_1_ = bf16[64,2048]{1,0:T(8,128)(2,1)S(1)} collective-permute-done((bf16[64,2048]{1,0:T(8,128)(2,1)S(1)}, bf16[64,2048]{1,0:T(8,128)(2,1)S(1)}, u32[]{:S(2)}, u32[]{:S(2)}) %collective-permute-start.21) | collective-permute-done | bytes 262176 | tf_op jit(solution)/shard_map/ppermute | solution.py:499
  76.5 1.7 %collective-permute-done.23.refs_12_ = bf16[128,2048]{1,0:T(8,128)(2,1)S(1)} collective-permute-done((bf16[128,2048]{1,0:T(8,128)(2,1)S(1)}, bf16[128,2048]{1,0:T(8,128)(2,1)S(1)}, u32[]{:S(2)}, u32[]{:S(2)}) %collective-permute-start.23) | collective-permute-done | bytes 524320 | tf_op jit(solution)/shard_map/ppermute | solution.py:499
  80.1 8.2 %shard_map.137 = (f32[512,2048]{1,0:T(8,128)S(1)}, f32[2048,512]{1,0:T(8,128)S(1)}, f32[2048,1]{1,0:T(8,128)S(1)}) custom-call(s32[1]{0:T(128)} %bitcast.3.own_ref, bf16[2048,2048]{1,0:T(8,128)(2,1)S(1)} %shard_map.118.dec_ref, f32[1,2048]{1,0:T(1,128)S(1)} %get-tuple-element.106.norms_ref.row_ref, bf16[512,256]{1,0:T(8,128)(2,1)S(1)} %get-tuple-element.111.refs_0_, ...), custom_call_target="tpu_custom_call" | custom-call | flops 4294967296 | tf_op jit(solution)/shard_map/pallas_call | solution.py:25
  90.3 6.2 %shard_map.140 = (f32[512,2048]{1,0:T(8,128)}, f32[2048,512]{1,0:T(8,128)}) custom-call(f32[1,128]{1,0:T(1,128)S(1)} %shard_map.120.energy_ref, s32[1]{0:T(128)} %bitcast.3.own_ref, f32[2048,1]{1,0:T(8,128)S(1)} %get-tuple-element.144.column_ref, f32[1,2048]{1,0:T(1,128)S(1)} %get-tuple-element.106.norms_ref.row_ref, ...), custom_call_target="tpu_custom_call" | custom-call | flops 3221225472 | tf_op jit(solution)/shard_map/pallas_call | solution.py:25
  (59 shorter events, 10.8 us)
Async XLA Ops:
  0.6 0.7 copy-start.2
  4.3 11.7 %collective-permute-start.5 = (bf16[32,2048]{1,0:T(8,128)(2,1)S(1)}, bf16[32,2048]{1,0:T(8,128)(2,1)S(1)}, u32[]{:S(2)}, u32[]{:S(2)}) collective-permute-start(bf16[32,2048]{1,0:T(8,128)(2,1)S(1)} %get-tuple-element.90.refs_0_), channel_id=1, source_target_pairs={{0,4},{1,3},{2,6},{3,1},{4,0},{5,7},{6,2},{7,5},{8,12},{9,11},{10,... | collective-permute-start | bytes 393224 | tf_op jit(solution)/shard_map/ppermute | solution.py:499
  8.4 3.7 %collective-permute-start = (f32[1,128]{1,0:T(1,128)S(1)}, f32[1,128]{1,0:T(1,128)S(1)}, u32[]{:S(2)}, u32[]{:S(2)}) collective-permute-start(f32[1,128]{1,0:T(1,128)S(1)} %get-tuple-element.83.a_ref), channel_id=1, source_target_pairs={{0,8},{1,17},{2,10},{3,19},{4,12},{5,21},{6,14},{7,23},{8,0},{9,25... | collective-permute-start | bytes 1544 | tf_op jit(solution)/shard_map/ppermute | solution.py:499
  12.1 3.8 %collective-permute-start.1 = (f32[1,128]{1,0:T(1,128)S(1)}, f32[1,128]{1,0:T(1,128)S(1)}, u32[]{:S(2)}, u32[]{:S(2)}) collective-permute-start(f32[1,128]{1,0:T(1,128)S(1)} %shard_map.114.a_ref), channel_id=1, source_target_pairs={{0,16},{1,9},{2,18},{3,11},{4,20},{5,13},{6,22},{7,15},{8,24},{9,1... | collective-permute-start | bytes 1544 | tf_op jit(solution)/shard_map/ppermute | solution.py:499
  16.0 10.8 %collective-permute-start.6 = (bf16[64,2048]{1,0:T(8,128)(2,1)S(1)}, bf16[64,2048]{1,0:T(8,128)(2,1)S(1)}, u32[]{:S(2)}, u32[]{:S(2)}) collective-permute-start(bf16[64,2048]{1,0:T(8,128)(2,1)S(1)} %shard_map.121.refs_0_.heads_ref), channel_id=1, source_target_pairs={{0,2},{1,5},{2,0},{3,7},{4,6},{5,1},{6,4},{7,3},{8,10},{9,13},{10,... | collective-permute-start | bytes 786440 | tf_op jit(solution)/shard_map/ppermute | solution.py:499
  17.6 1.1 %collective-permute-start.2 = (f32[1,128]{1,0:T(1,128)S(1)}, f32[1,128]{1,0:T(1,128)S(1)}, u32[]{:S(2)}, u32[]{:S(2)}) collective-permute-start(f32[1,128]{1,0:T(1,128)S(1)} %shard_map.116.a_ref), channel_id=1, source_target_pairs={{0,1},{1,0},{2,3},{3,2},{4,5},{5,4},{6,7},{7,6},{8,9},{9,8},{10,11... | collective-permute-start | bytes 1544 | tf_op jit(solution)/shard_map/ppermute | solution.py:499
  18.8 10.0 %copy-start = (f32[2048]{0:T(1024)S(1)}, f32[2048]{0:T(1024)}, u32[]{:S(2)}) copy-start(f32[2048]{0:T(1024)} %param.15) | copy-start | bytes 24580
  18.8 4.4 %collective-permute-start.3 = (f32[1,128]{1,0:T(1,128)S(1)}, f32[1,128]{1,0:T(1,128)S(1)}, u32[]{:S(2)}, u32[]{:S(2)}) collective-permute-start(f32[1,128]{1,0:T(1,128)S(1)} %shard_map.117.a_ref), channel_id=1, source_target_pairs={{0,4},{1,3},{2,6},{3,1},{4,0},{5,7},{6,2},{7,5},{8,12},{9,11},{10,... | collective-permute-start | bytes 1544 | tf_op jit(solution)/shard_map/ppermute | solution.py:499
  23.2 3.5 %collective-permute-start.4 = (f32[1,128]{1,0:T(1,128)S(1)}, f32[1,128]{1,0:T(1,128)S(1)}, u32[]{:S(2)}, u32[]{:S(2)}) collective-permute-start(f32[1,128]{1,0:T(1,128)S(1)} %shard_map.119.a_ref), channel_id=1, source_target_pairs={{0,2},{1,5},{2,0},{3,7},{4,6},{5,1},{6,4},{7,3},{8,10},{9,13},{10,... | collective-permute-start | bytes 1544 | tf_op jit(solution)/shard_map/ppermute | solution.py:499
  26.8 2.0 %collective-permute-start.7 = (bf16[128,2048]{1,0:T(8,128)(2,1)S(1)}, bf16[128,2048]{1,0:T(8,128)(2,1)S(1)}, u32[]{:S(2)}, u32[]{:S(2)}) collective-permute-start(bf16[128,2048]{1,0:T(8,128)(2,1)S(1)} %shard_map.122.refs_0_), channel_id=1, source_target_pairs={{0,1},{1,0},{2,3},{3,2},{4,5},{5,4},{6,7},{7,6},{8,9},{9,8},{10,11... | collective-permute-start | bytes 1572872 | tf_op jit(solution)/shard_map/ppermute | solution.py:499
  26.9 9.2 %collective-permute-start.8 = (bf16[128,2048]{1,0:T(8,128)(2,1)S(1)}, bf16[128,2048]{1,0:T(8,128)(2,1)S(1)}, u32[]{:S(2)}, u32[]{:S(2)}) collective-permute-start(bf16[128,2048]{1,0:T(8,128)(2,1)S(1)} %shard_map.122.refs_0_), channel_id=1, source_target_pairs={{0,8},{1,17},{2,10},{3,19},{4,12},{5,21},{6,14},{7,23},{8,0},{9,25... | collective-permute-start | bytes 1572872 | tf_op jit(solution)/shard_map/ppermute | solution.py:499
  34.4 2.0 %collective-permute-start.9 = (bf16[128,2048]{1,0:T(8,128)(2,1)S(1)}, bf16[128,2048]{1,0:T(8,128)(2,1)S(1)}, u32[]{:S(2)}, u32[]{:S(2)}) collective-permute-start(bf16[128,2048]{1,0:T(8,128)(2,1)S(1)} %get-tuple-element.95), channel_id=1, source_target_pairs={{0,1},{1,0},{2,3},{3,2},{4,5},{5,4},{6,7},{7,6},{8,9},{9,8},{10,11... | collective-permute-start | bytes 1572872 | tf_op jit(solution)/shard_map/ppermute | solution.py:499
  36.6 18.9 %collective-permute-start.13 = (bf16[256,2048]{1,0:T(8,128)(2,1)S(1)}, bf16[256,2048]{1,0:T(8,128)(2,1)S(1)}, u32[]{:S(2)}, u32[]{:S(2)}) collective-permute-start(bf16[256,2048]{1,0:T(8,128)(2,1)S(1)} %shard_map.128), channel_id=1, source_target_pairs={{0,16},{1,9},{2,18},{3,11},{4,20},{5,13},{6,22},{7,15},{8,24},{9,1... | collective-permute-start | bytes 3145736 | tf_op jit(solution)/shard_map/ppermute | solution.py:499
  37.9 1.9 %collective-permute-start.11 = (bf16[128,2048]{1,0:T(8,128)(2,1)S(1)}, bf16[128,2048]{1,0:T(8,128)(2,1)S(1)}, u32[]{:S(2)}, u32[]{:S(2)}) collective-permute-start(bf16[128,2048]{1,0:T(8,128)(2,1)S(1)} %collective-permute-done.8.refs_0_.refs_1_), channel_id=1, source_target_pairs={{0,1},{1,0},{2,3},{3,2},{4,5},{5,4},{6,7},{7,6},{8,9},{9,8},{10,11... | collective-permute-start | bytes 1572872 | tf_op jit(solution)/shard_map/ppermute | solution.py:499
  37.9 7.7 %collective-permute-start.10 = (bf16[64,2048]{1,0:T(8,128)(2,1)S(1)}, bf16[64,2048]{1,0:T(8,128)(2,1)S(1)}, u32[]{:S(2)}, u32[]{:S(2)}) collective-permute-start(bf16[64,2048]{1,0:T(8,128)(2,1)S(1)} %get-tuple-element.97), channel_id=1, source_target_pairs={{0,2},{1,5},{2,0},{3,7},{4,6},{5,1},{6,4},{7,3},{8,10},{9,13},{10,... | collective-permute-start | bytes 786440 | tf_op jit(solution)/shard_map/ppermute | solution.py:499
  45.7 9.8 %copy-start.1 = (f32[2048]{0:T(1024)S(1)}, f32[2048]{0:T(1024)}, u32[]{:S(2)}) copy-start(f32[2048]{0:T(1024)} %param.17) | copy-start | bytes 24580
  45.7 12.7 %copy-start.3 = (s32[32]{0:T(128)S(1)}, s32[32]{0:T(128)}, u32[]{:S(2)}) copy-start(s32[32]{0:T(128)} %param.13) | copy-start | bytes 388
  45.7 9.8 %collective-permute-start.12 = (bf16[64,2048]{1,0:T(8,128)(2,1)S(1)}, bf16[64,2048]{1,0:T(8,128)(2,1)S(1)}, u32[]{:S(2)}, u32[]{:S(2)}) collective-permute-start(bf16[64,2048]{1,0:T(8,128)(2,1)S(1)} %get-tuple-element.104), channel_id=1, source_target_pairs={{0,4},{1,3},{2,6},{3,1},{4,0},{5,7},{6,2},{7,5},{8,12},{9,11},{10,... | collective-permute-start | bytes 786440 | tf_op jit(solution)/shard_map/ppermute | solution.py:499
  55.7 5.1 %collective-permute-start.14 = (bf16[256,2048]{1,0:T(8,128)(2,1)S(1)}, bf16[256,2048]{1,0:T(8,128)(2,1)S(1)}, u32[]{:S(2)}, u32[]{:S(2)}) collective-permute-start(bf16[256,2048]{1,0:T(8,128)(2,1)S(1)} %collective-permute-done.13.refs_0_), channel_id=1, source_target_pairs={{0,1},{1,0},{2,3},{3,2},{4,5},{5,4},{6,7},{7,6},{8,9},{9,8},{10,11... | collective-permute-start | bytes 3145736 | tf_op jit(solution)/shard_map/ppermute | solution.py:499
  55.9 10.1 %collective-permute-start.16 = (bf16[64,2048]{1,0:T(8,128)(2,1)S(1)}, bf16[64,2048]{1,0:T(8,128)(2,1)S(1)}, u32[]{:S(2)}, u32[]{:S(2)}) collective-permute-start(bf16[64,2048]{1,0:T(8,128)(2,1)S(1)} %get-tuple-element.113.refs_0_), channel_id=1, source_target_pairs={{0,8},{1,17},{2,10},{3,19},{4,12},{5,21},{6,14},{7,23},{8,0},{9,25... | collective-permute-start | bytes 786440 | tf_op jit(solution)/shard_map/ppermute | solution.py:499
  57.0 9.0 %collective-permute-start.15 = (bf16[64,2048]{1,0:T(8,128)(2,1)S(1)}, bf16[64,2048]{1,0:T(8,128)(2,1)S(1)}, u32[]{:S(2)}, u32[]{:S(2)}) collective-permute-start(bf16[64,2048]{1,0:T(8,128)(2,1)S(1)} %get-tuple-element.113.refs_0_), channel_id=1, source_target_pairs={{0,2},{1,5},{2,0},{3,7},{4,6},{5,1},{6,4},{7,3},{8,10},{9,13},{10,... | collective-permute-start | bytes 786440 | tf_op jit(solution)/shard_map/ppermute | solution.py:499
  58.7 7.1 %collective-permute-start.17 = (f32[8,2176]{1,0:T(8,128)S(1)}, f32[8,2176]{1,0:T(8,128)S(1)}, u32[]{:S(2)}, u32[]{:S(2)}) collective-permute-start(f32[8,2176]{1,0:T(8,128)S(1)} %get-tuple-element.122), channel_id=1, source_target_pairs={{0,8},{1,9},{2,10},{3,11},{4,12},{5,13},{6,14},{7,15},{8,0},{9,1},... | collective-permute-start | bytes 208904 | tf_op jit(solution)/shard_map/ppermute | solution.py:499
  59.5 6.4 %collective-permute-start.18 = (f32[8,2176]{1,0:T(8,128)S(1)}, f32[8,2176]{1,0:T(8,128)S(1)}, u32[]{:S(2)}, u32[]{:S(2)}) collective-permute-start(f32[8,2176]{1,0:T(8,128)S(1)} %get-tuple-element.123), channel_id=1, source_target_pairs={{0,16},{1,17},{2,18},{3,19},{4,20},{5,21},{6,22},{7,23},{8,24},{9,... | collective-permute-start | bytes 208904 | tf_op jit(solution)/shard_map/ppermute | solution.py:499
  60.8 5.2 %collective-permute-start.19 = (f32[8,2176]{1,0:T(8,128)S(1)}, f32[8,2176]{1,0:T(8,128)S(1)}, u32[]{:S(2)}, u32[]{:S(2)}) collective-permute-start(f32[8,2176]{1,0:T(8,128)S(1)} %get-tuple-element.124), channel_id=1, source_target_pairs={{0,24},{1,25},{2,26},{3,27},{4,28},{5,29},{6,30},{7,31},{8,16},{9,... | collective-permute-start | bytes 208904 | tf_op jit(solution)/shard_map/ppermute | solution.py:499
  66.0 5.8 %collective-permute-start.20 = (bf16[128,2048]{1,0:T(8,128)(2,1)S(1)}, bf16[128,2048]{1,0:T(8,128)(2,1)S(1)}, u32[]{:S(2)}, u32[]{:S(2)}) collective-permute-start(bf16[128,2048]{1,0:T(8,128)(2,1)S(1)} %shard_map.132.refs_1_), channel_id=1, source_target_pairs={{0,1},{1,0},{2,3},{3,2},{4,5},{5,4},{6,7},{7,6},{8,9},{9,8},{10,11... | collective-permute-start | bytes 1572872 | tf_op jit(solution)/shard_map/ppermute | solution.py:499
  66.2 12.1 %collective-permute-start.23 = (bf16[128,2048]{1,0:T(8,128)(2,1)S(1)}, bf16[128,2048]{1,0:T(8,128)(2,1)S(1)}, u32[]{:S(2)}, u32[]{:S(2)}) collective-permute-start(bf16[128,2048]{1,0:T(8,128)(2,1)S(1)} %shard_map.136), channel_id=1, source_target_pairs={{0,16},{1,9},{2,18},{3,11},{4,20},{5,13},{6,22},{7,15},{8,24},{9,1... | collective-permute-start | bytes 1572872 | tf_op jit(solution)/shard_map/ppermute | solution.py:499
  67.2 9.2 %collective-permute-start.21 = (bf16[64,2048]{1,0:T(8,128)(2,1)S(1)}, bf16[64,2048]{1,0:T(8,128)(2,1)S(1)}, u32[]{:S(2)}, u32[]{:S(2)}) collective-permute-start(bf16[64,2048]{1,0:T(8,128)(2,1)S(1)} %collective-permute-done.15.refs_1_.refs_0_), channel_id=1, source_target_pairs={{0,8},{1,17},{2,10},{3,19},{4,12},{5,21},{6,14},{7,23},{8,0},{9,25... | collective-permute-start | bytes 786440 | tf_op jit(solution)/shard_map/ppermute | solution.py:499
  76.4 2.8 %collective-permute-start.22 = (bf16[128,2048]{1,0:T(8,128)(2,1)S(1)}, bf16[128,2048]{1,0:T(8,128)(2,1)S(1)}, u32[]{:S(2)}, u32[]{:S(2)}) collective-permute-start(bf16[128,2048]{1,0:T(8,128)(2,1)S(1)} %shard_map.135.refs_10_), channel_id=1, source_target_pairs={{0,1},{1,0},{2,3},{3,2},{4,5},{5,4},{6,7},{7,6},{8,9},{9,8},{10,11... | collective-permute-start | bytes 1572872 | tf_op jit(solution)/shard_map/ppermute | solution.py:499
  78.2 1.9 %collective-permute-start.24 = (bf16[128,2048]{1,0:T(8,128)(2,1)S(1)}, bf16[128,2048]{1,0:T(8,128)(2,1)S(1)}, u32[]{:S(2)}, u32[]{:S(2)}) collective-permute-start(bf16[128,2048]{1,0:T(8,128)(2,1)S(1)} %collective-permute-done.23.refs_12_), channel_id=1, source_target_pairs={{0,1},{1,0},{2,3},{3,2},{4,5},{5,4},{6,7},{7,6},{8,9},{9,8},{10,11... | collective-permute-start | bytes 1572872 | tf_op jit(solution)/shard_map/ppermute | solution.py:499
  78.2 10.1 %collective-permute-start.25 = (bf16[128,2048]{1,0:T(8,128)(2,1)S(1)}, bf16[128,2048]{1,0:T(8,128)(2,1)S(1)}, u32[]{:S(2)}, u32[]{:S(2)}) collective-permute-start(bf16[128,2048]{1,0:T(8,128)(2,1)S(1)} %shard_map.139), channel_id=1, source_target_pairs={{0,16},{1,9},{2,18},{3,11},{4,20},{5,13},{6,22},{7,15},{8,24},{9,1... | collective-permute-start | bytes 1572872 | tf_op jit(solution)/shard_map/ppermute | solution.py:499
  88.4 2.0 %collective-permute-start.26 = (bf16[128,2048]{1,0:T(8,128)(2,1)S(1)}, bf16[128,2048]{1,0:T(8,128)(2,1)S(1)}, u32[]{:S(2)}, u32[]{:S(2)}) collective-permute-start(bf16[128,2048]{1,0:T(8,128)(2,1)S(1)} %collective-permute-done.25.refs_0_), channel_id=1, source_target_pairs={{0,1},{1,0},{2,3},{3,2},{4,5},{5,4},{6,7},{7,6},{8,9},{9,8},{10,11... | collective-permute-start | bytes 1572872 | tf_op jit(solution)/shard_map/ppermute | solution.py:499
